TPU v7x, 512 devices: a whole 4x4x16 slice. The times are simulated.
512 devices in a mesh: lon: 64 (over y, z_lo, core), lat: 8 (over z_hi, x).
Axes of the slice: x: 4, y: 4, z: 16 (z_hi: 2, z_lo: 8; z = z_hi * 8 + z_lo), core: 2. Of those that a mesh axis runs over, the one named last changes fastest.
Arguments:
- features: bfloat16 [2, 192, 768, 512], P(None, 'lat', 'lon'), may hold values from -6 to 6
- region_ids: int32 [2, 192, 768], P(None, 'lat', 'lon'), may hold values from 0 to 2
- ln_gain: float32 [512], replicated, may hold values from 0.1 to 1.9
- ln_bias: float32 [512], replicated, may hold values from -3 to 3
- w_qkv: bfloat16 [512, 1536], replicated
- b_qkv: float32 [1536], replicated, may hold values from -2 to 2
- w_out: bfloat16 [512, 512], replicated, may hold values from -0.25 to 0.25
- b_out: float32 [512], replicated, may hold values from -2 to 2
Outputs:
- mixed: bfloat16 [2, 192, 768, 512], P(None, 'lat', 'lon')
All inputs are finite; a program needn't handle non-finite values.
Results may differ from a plain program's by a relative error of at most 0.0056.
Values may be sent and summed in bfloat16 or wider, within the bound.
No kernel may reach another device: no remote copies, remote signals or barrier semaphores. Data moves between devices by JAX's collectives and lax.ppermute only.
A program may use at most 128 MiB of HBM per device.

v0:
```python
import jax
import jax.numpy as jnp
from jax import lax
from jax.sharding import PartitionSpec as P

HEADS = 8
WLAT = 6
WLON = 12
SLAT = 3
SLON = 6


def passed_along(block, axis, distance):
    devices = range(lax.axis_size(axis))
    route = [((i - distance) % len(devices), i) for i in devices]
    return lax.ppermute(block, axis, route)


def to_windows(array, rows, cols):
    levels = array.shape[0]
    last = array.shape[-1]
    shaped = array.reshape(levels, rows // WLAT, WLAT, cols // WLON, WLON, last)
    return shaped.transpose(1, 3, 0, 2, 4, 5).reshape(-1, levels * WLAT * WLON, last)


def from_windows(array, levels, rows, cols):
    last = array.shape[-1]
    shaped = array.reshape(rows // WLAT, cols // WLON, levels, WLAT, WLON, last)
    return shaped.transpose(2, 0, 3, 1, 4, 5).reshape(levels, rows, cols, last)


def attend(tile, labels, ln_gain, ln_bias, w_qkv, b_qkv, w_out, b_out):
    levels, rows, cols, width = tile.shape
    values = tile.astype(jnp.float32)
    center = values - jnp.mean(values, axis=-1, keepdims=True)
    spread = jnp.mean(center * center, axis=-1, keepdims=True)
    normed = (center * lax.rsqrt(spread + 1e-05) * ln_gain + ln_bias).astype(jnp.bfloat16)
    windows = to_windows(normed, rows, cols)
    marks = to_windows(labels[..., None], rows, cols)[..., 0]
    count, span = (windows.shape[0], windows.shape[1])
    head_size = width // HEADS
    packed = (
        jnp.dot(windows.reshape(count * span, width), w_qkv, preferred_element_type=jnp.float32)
        + b_qkv
    )
    packed = packed.astype(jnp.bfloat16).reshape(count, span, 3, HEADS, head_size)
    query = packed[:, :, 0]
    keys = packed[:, :, 1]
    vals = packed[:, :, 2]
    scores = jnp.einsum(
        "nqhd,nkhd->nhqk", query, keys, preferred_element_type=jnp.float32
    ) * head_size ** (-0.5)
    allowed = marks[:, None, :, None] == marks[:, None, None, :]
    scores = jnp.where(allowed, scores, -1e30)
    top = jnp.max(scores, axis=-1, keepdims=True)
    expd = jnp.exp(scores - top)
    weights = (expd / jnp.sum(expd, axis=-1, keepdims=True)).astype(jnp.bfloat16)
    heads_out = jnp.einsum("nhqk,nkhd->nqhd", weights, vals, preferred_element_type=jnp.float32)
    heads_out = heads_out.astype(jnp.bfloat16).reshape(count * span, width)
    projected = (jnp.dot(heads_out, w_out, preferred_element_type=jnp.float32) + b_out).astype(
        jnp.bfloat16
    )
    return from_windows(projected.reshape(count, span, width), levels, rows, cols)


def make_labels(ids_tile, flags):
    return ids_tile.astype(jnp.float32) + 4.0 * flags.astype(jnp.float32)[None, :, None]


def local(features, region_ids, ln_gain, ln_bias, w_qkv, b_qkv, w_out, b_out):
    levels, rows, cols, width = features.shape
    total_rows = rows * lax.axis_size("lat")
    start = lax.axis_index("lat") * rows
    ids_wire = region_ids.astype(jnp.bfloat16)
    below_feat, below_ids = passed_along((features[:, :SLAT], ids_wire[:, :SLAT]), "lat", -1)
    feat_rows = jnp.concatenate([features[:, SLAT:], below_feat], axis=1)
    ids_rows = jnp.concatenate([ids_wire[:, SLAT:], below_ids], axis=1)
    right_feat, right_ids = passed_along((feat_rows[:, :, :SLON], ids_rows[:, :, :SLON]), "lon", -1)
    tile = jnp.concatenate([feat_rows[:, :, SLON:], right_feat], axis=2)
    ids_tile = jnp.concatenate([ids_rows[:, :, SLON:], right_ids], axis=2)
    flags = (start + jnp.arange(rows) + SLAT) % total_rows < SLAT
    result = attend(
        tile, make_labels(ids_tile, flags), ln_gain, ln_bias, w_qkv, b_qkv, w_out, b_out
    )
    left_cols = passed_along(result[:, :, cols - SLON :], "lon", 1)
    result = jnp.concatenate([left_cols, result[:, :, : cols - SLON]], axis=2)
    upper_rows = passed_along(result[:, rows - SLAT :], "lat", 1)
    attended = jnp.concatenate([upper_rows, result[:, : rows - SLAT]], axis=1)
    return (features.astype(jnp.float32) + attended.astype(jnp.float32)).astype(jnp.bfloat16)


def solution(mesh):
    return jax.shard_map(
        local,
        mesh=mesh,
        in_specs=(P(None, "lat", "lon", None), P(None, "lat", "lon"), P(), P(), P(), P(), P(), P()),
        out_specs=P(None, "lat", "lon", None),
        check_vma=False,
    )
```

profile of v0, /device:TPU:8, one launch (start us, length us, event | category | flops | bytes accessed | tf_op | source)
XLA Modules:
  0.0 110.6 jit_solution(17124140886906804744)
XLA Ops:
  0.8 17.9 %collective-permute-start.2 = (bf16[2,3,12]{1,0,2:T(2,128)(2,1)S(1)}, bf16[2,3,12]{1,0,2:T(2,128)(2,1)S(1)}, u32[]{:S(2)}, u32[]{:S(2)}) collective-permute-start(bf16[2,3,12]{1,0,2:T(2,128)(2,1)S(1)} %bitcast.44), channel_id=1, source_target_pairs={{1,0},{2,1},{3,2},{4,3},{5,4},{6,5},{7,6},{0,7},{9,8},{10,9},{11,1... | collective-permute-start | bytes 440 | tf_op jit(solution)/shard_map/ppermute | solution.py:16
  18.7 1.0 slice.46
  19.7 2.7 %collective-permute-start = (bf16[2,3,12,512]{3,1,2,0:T(4,128)(2,1)S(1)}, bf16[2,3,12,512]{3,1,2,0:T(4,128)(2,1)S(1)}, u32[]{:S(2)}, u32[]{:S(2)}) collective-permute-start(bf16[2,3,12,512]{3,1,2,0:T(4,128)(2,1)S(1)} %slice.46), channel_id=1, source_target_pairs={{1,0},{2,1},{3,2},{4,3},{5,4},{6,5},{7,6},{0,7},{9,8},{10,9},{11,1... | collective-permute-start | bytes 221192 | tf_op jit(solution)/shard_map/ppermute | solution.py:16
  22.6 4.4 %collective-permute-start.3 = (bf16[2,24,6]{1,0,2:T(2,128)(2,1)S(1)}, bf16[2,24,6]{1,0,2:T(2,128)(2,1)S(1)}, u32[]{:S(2)}, u32[]{:S(2)}) collective-permute-start(bf16[2,24,6]{1,0,2:T(2,128)(2,1)S(1)} %get-tuple-element.13), channel_id=1, source_target_pairs={{8,0},{16,8},{24,16},{32,24},{40,32},{48,40},{56,48},{64,56},{72,6... | collective-permute-start | bytes 1736 | tf_op jit(solution)/shard_map/ppermute | solution.py:16
  27.1 1.2 %slice.45 = bf16[2,21,12,512]{3,1,2,0:T(8,128)(2,1)S(1)} slice(bf16[2,24,12,512]{3,1,2,0:T(8,128)(2,1)} %param.8), slice={[0:2], [3:24], [0:12], [0:512]} | slice | bytes 1032192 | tf_op jit(solution)/shard_map/slice | solution.py:76
  28.5 1.1 %collective-permute-done.3 = bf16[2,24,6]{1,0,2:T(2,128)(2,1)S(1)} collective-permute-done((bf16[2,24,6]{1,0,2:T(2,128)(2,1)S(1)}, bf16[2,24,6]{1,0,2:T(2,128)(2,1)S(1)}, u32[]{:S(2)}, u32[]{:S(2)}) %collective-permute-start.3) | collective-permute-done | bytes 608 | tf_op jit(solution)/shard_map/ppermute | solution.py:16
  30.0 11.4 %collective-permute-start.1 = (bf16[2,24,6,512]{3,1,2,0:T(8,128)(2,1)S(1)}, bf16[2,24,6,512]{3,1,2,0:T(8,128)(2,1)S(1)}, u32[]{:S(2)}, u32[]{:S(2)}) collective-permute-start(bf16[2,24,6,512]{3,1,2,0:T(8,128)(2,1)S(1)} %get-tuple-element.9), channel_id=1, source_target_pairs={{8,0},{16,8},{24,16},{32,24},{40,32},{48,40},{56,48},{64,56},{72,6... | collective-permute-start | bytes 884744 | tf_op jit(solution)/shard_map/ppermute | solution.py:16
  42.1 3.6 %collective-permute-done.1 = bf16[2,24,6,512]{3,1,2,0:T(8,128)(2,1)S(1)} collective-permute-done((bf16[2,24,6,512]{3,1,2,0:T(8,128)(2,1)S(1)}, bf16[2,24,6,512]{3,1,2,0:T(8,128)(2,1)S(1)}, u32[]{:S(2)}, u32[]{:S(2)}) %collective-permute-start.1) | collective-permute-done | bytes 294944 | tf_op jit(solution)/shard_map/ppermute | solution.py:16
  47.2 1.2 %fusion.15 = bf16[4,1,2,6,12,512]{5,2,4,3,0,1:T(2,128)(2,1)S(1)} fusion(bf16[2,4,6,1,6,512]{5,0,4,2,1,3:T(2,128)(2,1)S(1)} %bitcast.41, bf16[2,4,6,1,6,512]{5,0,4,2,1,3:T(2,128)(2,1)S(1)} %bitcast.40, f32[512]{0:T(512)S(1)} %copy-done.3, f32[512]{0:T(512)S(1)} %copy-done.4, f32[2,4,6,12]{0,3,2,1:T(8,128)S(1)} %copy.54, f32[2,4,6,12]{0,3,2,1:T(8,128)S(1)} %copy.52), kind=kLoop, calls=%fused_computation.24 | loop fusion | flops 2064384 | bytes 1188352 | tf_op jit(solution)/shard_map/transpose | solution.py:23
  49.5 2.1 %add_convert_fusion = bf16[576,1536]{1,0:T(8,128)(2,1)S(1)} fusion(bf16[576,512]{1,0:T(8,128)(2,1)} %reshape_reshape.6, bf16[512,1536]{1,0:T(8,128)(2,1)S(1)} %copy-done, f32[1536]{0:T(1024)S(1)} %copy-done.5), kind=kOutput, calls=%fused_computation.5 | convolution fusion | flops 907739136 | bytes 3938304 | tf_op jit(solution)/shard_map/dot_general | solution.py:43
  51.7 3.4 %reshape.144 = bf16[4,144,3,8,64]{4,3,2,1,0:T(8,128)(2,1)} reshape(bf16[576,1536]{1,0:T(8,128)(2,1)S(1)} %add_convert_fusion) | data formatting | bytes 3538944 | tf_op jit(solution)/shard_map/reshape | solution.py:46
  55.1 3.6 %fusion.22 = (bf16[4,144,1,8,64]{4,3,2,1,0:T(8,128)(2,1)}, bf16[4,144,1,8,64]{4,3,2,1,0:T(8,128)(2,1)}, bf16[4,144,1,8,64]{4,3,2,1,0:T(8,128)(2,1)S(1)}) fusion(bf16[4,144,3,8,64]{4,3,2,1,0:T(8,128)(2,1)} %reshape.144), kind=kLoop, calls=%fused_computation.46 | loop fusion | bytes 3538944 | tf_op jit(solution)/shard_map/slice | solution.py:49
  58.7 2.6 %copy.70 = bf16[4,144,1,8,64]{1,4,3,0,2:T(8,128)(2,1)} copy(bf16[4,144,1,8,64]{4,3,2,1,0:T(8,128)(2,1)} %get-tuple-element.5) | data formatting | bytes 1179648
  61.3 2.6 %copy.71 = bf16[4,144,1,8,64]{1,4,3,0,2:T(8,128)(2,1)} copy(bf16[4,144,1,8,64]{4,3,2,1,0:T(8,128)(2,1)} %get-tuple-element.6) | data formatting | bytes 1179648
  63.9 1.6 %copy.72 = bf16[4,144,1,8,64]{1,4,3,0,2:T(8,128)(2,1)} copy(bf16[4,144,1,8,64]{4,3,2,1,0:T(8,128)(2,1)S(1)} %get-tuple-element.7) | data formatting | bytes 1179648
  65.5 2.4 %fusion.11 = f32[4,8,144,144]{2,3,1,0:T(8,128)S(1)} fusion(bf16[4,144,1,8,64]{1,4,3,0,2:T(8,128)(2,1)} %copy.72, bf16[4,144,1,8,64]{1,4,3,0,2:T(8,128)(2,1)} %copy.71), kind=kOutput, calls=%fused_computation.20 | convolution fusion | flops 84934656 | bytes 3833856 | tf_op jit(solution)/shard_map/nqhd,nkhd->nhqk/dot_general | solution.py:50
  67.9 1.7 %fusion.24 = (f32[4,8,144]{2,1,0:T(8,128)S(1)}, f32[4,8,144,144]{2,3,1,0:T(8,128)S(1)}) fusion(f32[4,8,144,144]{2,3,1,0:T(8,128)S(1)} %fusion.11, pred[4,144,144]{1,2,0:T(8,128)(4,1)S(1)} %broadcast_compare_fusion), kind=kOutput, calls=%fused_computation.48 | output fusion | flops 3981455 | bytes 5409792 | tf_op jit(solution)/shard_map/sub | solution.py:56
  71.6 2.4 %fusion.8 = bf16[576,512]{1,0:T(8,128)(2,1)} fusion(bf16[576,512]{0,1:T(8,128)(2,1)S(1)} %reshape.142, bf16[512,512]{1,0:T(8,128)(2,1)} %param.14, f32[512]{0:T(512)S(1)} %copy-done.6), kind=kOutput, calls=%fused_computation.15 | convolution fusion | flops 302579712 | bytes 1705984 | tf_op jit(solution)/shard_map/dot_general | solution.py:60
  74.0 1.2 %reshape_reshape.7 = bf16[4,1,2,6,12,512]{5,4,3,2,0,1:T(8,128)(2,1)S(1)} reshape(bf16[576,512]{1,0:T(8,128)(2,1)} %fusion.8) | data formatting | bytes 1179648 | tf_op jit(solution)/shard_map/reshape;reshape | solution.py:28
  76.3 1.9 %collective-permute-start.4 = (bf16[2,24,6,512]{3,1,2,0:T(8,128)(2,1)S(1)}, bf16[2,24,6,512]{3,1,2,0:T(8,128)(2,1)S(1)}, u32[]{:S(2)}, u32[]{:S(2)}) collective-permute-start(bf16[2,24,6,512]{3,1,2,0:T(8,128)(2,1)S(1)} %copy.73), channel_id=1, source_target_pairs={{504,0},{0,8},{8,16},{16,24},{24,32},{32,40},{40,48},{48,56},{56,6... | collective-permute-start | bytes 884744 | tf_op jit(solution)/shard_map/ppermute | solution.py:16
  78.2 13.8 %collective-permute-done.4 = bf16[2,24,6,512]{3,1,2,0:T(8,128)(2,1)S(1)} collective-permute-done((bf16[2,24,6,512]{3,1,2,0:T(8,128)(2,1)S(1)}, bf16[2,24,6,512]{3,1,2,0:T(8,128)(2,1)S(1)}, u32[]{:S(2)}, u32[]{:S(2)}) %collective-permute-start.4) | collective-permute-done | bytes 294944 | tf_op jit(solution)/shard_map/ppermute | solution.py:16
  92.1 1.9 %collective-permute-start.5 = (bf16[2,3,12,512]{3,1,2,0:T(4,128)(2,1)S(1)}, bf16[2,3,12,512]{3,1,2,0:T(4,128)(2,1)S(1)}, u32[]{:S(2)}, u32[]{:S(2)}) collective-permute-start(bf16[2,3,12,512]{3,1,2,0:T(4,128)(2,1)S(1)} %slice.71), channel_id=1, source_target_pairs={{7,0},{0,1},{1,2},{2,3},{3,4},{4,5},{5,6},{6,7},{15,8},{8,9},{9,10... | collective-permute-start | bytes 221192 | tf_op jit(solution)/shard_map/ppermute | solution.py:16
  94.1 15.4 %collective-permute-done.5 = bf16[2,3,12,512]{3,1,2,0:T(4,128)(2,1)S(1)} collective-permute-done((bf16[2,3,12,512]{3,1,2,0:T(4,128)(2,1)S(1)}, bf16[2,3,12,512]{3,1,2,0:T(4,128)(2,1)S(1)}, u32[]{:S(2)}, u32[]{:S(2)}) %collective-permute-start.5) | collective-permute-done | bytes 73760 | tf_op jit(solution)/shard_map/ppermute | solution.py:16
  109.5 1.1 add_convert_fusion.1
  (49 shorter events, 8.0 us)
Async XLA Ops:
  0.0 49.5 %copy-start = (bf16[512,1536]{1,0:T(8,128)(2,1)S(1)}, bf16[512,1536]{1,0:T(8,128)(2,1)}, u32[]{:S(2)}) copy-start(bf16[512,1536]{1,0:T(8,128)(2,1)} %param.12) | copy-start | bytes 4718596
  0.8 21.7 %collective-permute-start.2 = (bf16[2,3,12]{1,0,2:T(2,128)(2,1)S(1)}, bf16[2,3,12]{1,0,2:T(2,128)(2,1)S(1)}, u32[]{:S(2)}, u32[]{:S(2)}) collective-permute-start(bf16[2,3,12]{1,0,2:T(2,128)(2,1)S(1)} %bitcast.44), channel_id=1, source_target_pairs={{1,0},{2,1},{3,2},{4,3},{5,4},{6,5},{7,6},{0,7},{9,8},{10,9},{11,1... | collective-permute-start | bytes 440 | tf_op jit(solution)/shard_map/ppermute | solution.py:16
  19.7 10.2 %collective-permute-start = (bf16[2,3,12,512]{3,1,2,0:T(4,128)(2,1)S(1)}, bf16[2,3,12,512]{3,1,2,0:T(4,128)(2,1)S(1)}, u32[]{:S(2)}, u32[]{:S(2)}) collective-permute-start(bf16[2,3,12,512]{3,1,2,0:T(4,128)(2,1)S(1)} %slice.46), channel_id=1, source_target_pairs={{1,0},{2,1},{3,2},{4,3},{5,4},{6,5},{7,6},{0,7},{9,8},{10,9},{11,1... | collective-permute-start | bytes 221192 | tf_op jit(solution)/shard_map/ppermute | solution.py:16
  22.6 7.0 %collective-permute-start.3 = (bf16[2,24,6]{1,0,2:T(2,128)(2,1)S(1)}, bf16[2,24,6]{1,0,2:T(2,128)(2,1)S(1)}, u32[]{:S(2)}, u32[]{:S(2)}) collective-permute-start(bf16[2,24,6]{1,0,2:T(2,128)(2,1)S(1)} %get-tuple-element.13), channel_id=1, source_target_pairs={{8,0},{16,8},{24,16},{32,24},{40,32},{48,40},{56,48},{64,56},{72,6... | collective-permute-start | bytes 1736 | tf_op jit(solution)/shard_map/ppermute | solution.py:16
  30.0 15.6 %collective-permute-start.1 = (bf16[2,24,6,512]{3,1,2,0:T(8,128)(2,1)S(1)}, bf16[2,24,6,512]{3,1,2,0:T(8,128)(2,1)S(1)}, u32[]{:S(2)}, u32[]{:S(2)}) collective-permute-start(bf16[2,24,6,512]{3,1,2,0:T(8,128)(2,1)S(1)} %get-tuple-element.9), channel_id=1, source_target_pairs={{8,0},{16,8},{24,16},{32,24},{40,32},{48,40},{56,48},{64,56},{72,6... | collective-permute-start | bytes 884744 | tf_op jit(solution)/shard_map/ppermute | solution.py:16
  41.6 5.6 %copy-start.3 = (f32[512]{0:T(512)S(1)}, f32[512]{0:T(512)}, u32[]{:S(2)}) copy-start(f32[512]{0:T(512)} %param.11) | copy-start | bytes 6148
  41.6 5.6 %copy-start.4 = (f32[512]{0:T(512)S(1)}, f32[512]{0:T(512)}, u32[]{:S(2)}) copy-start(f32[512]{0:T(512)} %param.10) | copy-start | bytes 6148
  48.5 1.1 copy-start.5
  67.9 1.7 %copy-start.2 = (bf16[4,144,1,8,64]{1,4,3,0,2:T(8,128)(2,1)S(1)}, bf16[4,144,1,8,64]{1,4,3,0,2:T(8,128)(2,1)}, u32[]{:S(2)}) copy-start(bf16[4,144,1,8,64]{1,4,3,0,2:T(8,128)(2,1)} %copy.70) | copy-start | bytes 1769476
  70.1 1.5 %copy-start.6 = (f32[512]{0:T(512)S(1)}, f32[512]{0:T(512)}, u32[]{:S(2)}) copy-start(f32[512]{0:T(512)} %param.15) | copy-start | bytes 6148
  75.8 33.7 %copy-start.1 = (bf16[2,24,12,512]{3,1,2,0:T(8,128)(2,1)S(1)}, bf16[2,24,12,512]{3,1,2,0:T(8,128)(2,1)}, u32[]{:S(2)}) copy-start(bf16[2,24,12,512]{3,1,2,0:T(8,128)(2,1)} %param.8) | copy-start | bytes 1769476
  76.3 15.7 %collective-permute-start.4 = (bf16[2,24,6,512]{3,1,2,0:T(8,128)(2,1)S(1)}, bf16[2,24,6,512]{3,1,2,0:T(8,128)(2,1)S(1)}, u32[]{:S(2)}, u32[]{:S(2)}) collective-permute-start(bf16[2,24,6,512]{3,1,2,0:T(8,128)(2,1)S(1)} %copy.73), channel_id=1, source_target_pairs={{504,0},{0,8},{8,16},{16,24},{24,32},{32,40},{40,48},{48,56},{56,6... | collective-permute-start | bytes 884744 | tf_op jit(solution)/shard_map/ppermute | solution.py:16
  92.1 17.3 %collective-permute-start.5 = (bf16[2,3,12,512]{3,1,2,0:T(4,128)(2,1)S(1)}, bf16[2,3,12,512]{3,1,2,0:T(4,128)(2,1)S(1)}, u32[]{:S(2)}, u32[]{:S(2)}) collective-permute-start(bf16[2,3,12,512]{3,1,2,0:T(4,128)(2,1)S(1)} %slice.71), channel_id=1, source_target_pairs={{7,0},{0,1},{1,2},{2,3},{3,4},{4,5},{5,6},{6,7},{15,8},{8,9},{9,10... | collective-permute-start | bytes 221192 | tf_op jit(solution)/shard_map/ppermute | solution.py:16
where the time goes:
time: 111 us
  starting transfers between devices  40.3 us (36%)
  waiting for transfers between devices  33.9 us (31%)
  local copies, waits for them, and re-layouts  22.9 us (21%)
  matrix products  7.38 us (7%)
  other arithmetic  5.71 us (5%)
    ppermute x6, starting transfers between devices, passed_along(): return lax.ppermute(block, axis, route)  40.3 us
    ppermute x6, waiting for transfers between devices, passed_along(): return lax.ppermute(block, axis, route)  33.9 us
    unnamed x19, local copies, waits for them, and re-layouts  6.87 us
    slice x1, local copies, waits for them, and re-layouts, attend(): vals = packed[:, :, 2]  3.62 us
    reshape x1, local copies, waits for them, and re-layouts, attend(): packed.astype(jnp.bfloat16).reshape(count, span, 3, HEADS, head_size)  3.4 us
    dot_general x1, matrix products, attend(): jnp.einsum('nqhd,nkhd->nhqk', query, keys, preferred_element_type=jnp.flo...  2.37 us
    dot_general x1, matrix products, attend(): jnp.dot(heads_out, w_out, preferred_element_type=jnp.float32) + b_out  2.36 us
  transfers between devices with their start and end apart: 6, of which 4 were waited for; matrix products, arithmetic and copies ran while one was open for 3% of the time, Pallas kernels for 0%

commit v1 on v0

v1 whole, which is shorter than its diff:
```python
import jax
import jax.numpy as jnp
from jax import lax
from jax.experimental import pallas as pl
from jax.experimental.pallas import tpu as pltpu
from jax.sharding import PartitionSpec as P

HEADS = 8
WLAT = 6
WLON = 12
SLAT = 3
SLON = 6
LEV = 2
D = 512
HS = D // HEADS
ROWS = 24
COLS = 12
HALF = WLAT * LEV * SLON
BLOCKS = ROWS // WLAT
SIDE = BLOCKS * HALF
PAY = SIDE + 16
STRIP = 16
BLK = WLAT * LEV * STRIP
EDGE = 40
KPAY = 4 * EDGE + 16
F32 = jnp.float32
BF16 = jnp.bfloat16
LIMIT = 60 * 1024 * 1024


def mm(a, b):
    return jnp.dot(a, b, preferred_element_type=F32)


def mm_nt(a, b):
    return lax.dot_general(a, b, (((1,), (1,)), ((), ())), preferred_element_type=F32)


def iota(shape, dim):
    return lax.broadcasted_iota(jnp.int32, shape, dim)


def place_of(k, odd_lon):
    strip, c16 = k >> 4, k & 15
    half = jnp.where(c16 >= SLON, 1, 0)
    side = half + odd_lon - 2 * half * odd_lon
    t = side * HALF + (strip >> 1) * 12 + (strip & 1) * 6 + (c16 - SLON * half)
    return jnp.where(c16 < COLS, t, -1)


def layer_norm(x, gain, bias):
    center = x - jnp.mean(x, axis=-1, keepdims=True)
    spread = jnp.mean(center * center, axis=-1, keepdims=True)
    return (center * lax.rsqrt(spread + 1e-05) * gain + bias).astype(BF16)


def edge_rows():
    odd = lax.axis_index("lat") % 2
    return (ROWS - SLAT) * odd, (ROWS - SLAT) * (1 - odd)


def prep_kernel(feat, ids, pay1, pay2, qlab, x_scr, b_scr, lab_scr):
    odd_lon = lax.axis_index("lon") % 2
    first = lax.axis_index("lat") == 0
    e1, e2 = edge_rows()
    x_scr[...] = jnp.zeros_like(x_scr)
    for i in range(ROWS):
        for l in range(LEV):
            x_scr[(i * LEV + l) * STRIP : (i * LEV + l) * STRIP + COLS, :] = feat[l, i]
    lab_scr[...] = jnp.zeros_like(lab_scr)
    from_first = jnp.where((iota((ROWS, COLS), 0) < SLAT) & first, 4.0, 0.0)
    for l in range(LEV):
        lab_scr[l * ROWS : (l + 1) * ROWS, :COLS] = ids[l].astype(F32) + from_first
    n = ROWS * LEV * STRIP
    strip = iota((n, ROWS * LEV), 0) >> 4
    pick = ((strip & 1) * ROWS + (strip >> 1)) == iota((n, ROWS * LEV), 1)
    spread = mm(jnp.where(pick, 1.0, 0.0).astype(BF16), lab_scr[...].astype(BF16))
    b_scr[...] = jnp.where((iota((n, 128), 0) & 15) == iota((n, 128), 1), spread, 0.0).astype(BF16)

    order = (iota((2 * HALF, BLK), 0) == place_of(iota((2 * HALF, BLK), 1), odd_lon))
    order = jnp.where(order, 1.0, 0.0).astype(BF16)

    def block(ref, b):
        if b < BLOCKS - 1:
            at = (SLAT + WLAT * b) * LEV * STRIP
            return ref[at : at + BLK, :]
        parts = [ref[pl.ds(pl.multiple_of(e * LEV * STRIP, 32), BLK // 2), :] for e in (e1, e2)]
        return jnp.concatenate(parts, axis=0)

    tokens = [mm(order, block(x_scr, b)) for b in range(BLOCKS)]
    marks = [mm(order, block(b_scr, b)) for b in range(BLOCKS)]
    for s, pay in enumerate((pay1, pay2)):
        own = slice(s * HALF, (s + 1) * HALF)
        pay[:SIDE, :] = jnp.concatenate([t[own] for t in tokens], axis=0).astype(BF16)
        mark = jnp.concatenate([m[own] for m in marks], axis=0)
        qlab[s] = jnp.broadcast_to(jnp.sum(mark, axis=-1, keepdims=True), (SIDE, 128))
        line = mm_nt(jnp.ones((STRIP, 128), BF16), mark.astype(BF16))
        pay[SIDE:, :] = jnp.concatenate(
            [line, jnp.zeros((STRIP, D - SIDE), F32)], axis=1
        ).astype(BF16)


def own_kernel(pay1, pay2, gain, bias, w_qkv, b_qkv, qkv):
    g, b = gain[...].reshape(1, D), bias[...].reshape(1, D)
    for s, pay in enumerate((pay1, pay2)):
        normed = layer_norm(pay[:SIDE, :].astype(F32), g, b)
        for c in range(3):
            cols = slice(c * D, (c + 1) * D)
            part = mm(normed, w_qkv[:, cols]) + b_qkv[cols].reshape(1, D)
            part = part.astype(BF16).astype(F32)
            if c == 0:
                part = part * HS ** (-0.5)
            for m in range(BLOCKS):
                qkv[s, m, :, cols] = part[m * HALF : (m + 1) * HALF].astype(BF16)


def label_line(ref, at):
    return ref[at : at + STRIP, :].astype(F32)[:8]


def shifted(line, start, to, wide):
    return pltpu.roll(line, (to - start) % D, 1)[:1, :wide]


def attention(q, k, v, q_label, k_label):
    n = q.shape[0]
    keys = k.shape[0]
    wide = 4 * HS
    allowed = q_label == k_label
    out = []
    col = iota((1, wide), 1)
    for g in range(2):
        cols = slice(g * wide, (g + 1) * wide)
        own = [(col >= h * HS) & (col < (h + 1) * HS) for h in range(4)]
        qg = q[:, cols]
        stacked = jnp.concatenate([jnp.where(o, qg, 0.0) for o in own], axis=0).astype(BF16)
        scores = mm_nt(stacked, k[:, cols])
        scores = jnp.where(allowed[None], scores.reshape(4, n, keys), -1e30)
        top = jnp.max(scores, axis=-1, keepdims=True)
        expd = jnp.exp(scores - top)
        weights = (expd / jnp.sum(expd, axis=-1, keepdims=True)).astype(BF16)
        full = mm(weights.reshape(4 * n, keys), v[:, cols])
        picked = jnp.where(own[0], full[:n], 0.0)
        for h in range(1, 4):
            picked = jnp.where(own[h], full[h * n : (h + 1) * n], picked)
        out.append(picked)
    return jnp.concatenate(out, axis=1)


def finish(heads, x, w_out, b_out, back):
    projected = (mm(heads.astype(BF16), w_out) + b_out).astype(BF16).astype(F32)
    return mm(back, (x + projected).astype(BF16)).astype(BF16)


def order_back():
    odd_lon = lax.axis_index("lon") % 2
    back = iota((BLK, 2 * HALF), 1) == place_of(iota((BLK, 2 * HALF), 0), odd_lon)
    return jnp.where(back, 1.0, 0.0).astype(BF16)


def edges_kernel(pay1, pay2, far1, far2, out1, out2):
    lane = iota((8, D), 1)
    for e, out in enumerate((out1, out2)):
        at = 32 * e
        rows, line = [], jnp.zeros((8, D), F32)
        for j, ref in enumerate((pay1, far1, pay2, far2)):
            rows.append(ref[SIDE - 80 : SIDE, :].astype(F32)[8 + at : 8 + at + EDGE])
            moved = pltpu.roll(label_line(ref, SIDE), (j * EDGE - (3 * HALF + at)) % D, 1)
            line = jnp.where((lane >= j * EDGE) & (lane < (j + 1) * EDGE), moved, line)
        out[: 4 * EDGE, :] = jnp.concatenate(rows, axis=0).astype(BF16)
        out[4 * EDGE :, :] = jnp.concatenate([line, line], axis=0).astype(BF16)


def inner_kernel(pay1, pay2, far1, far2, qlab, qkv, gain, bias, w_qkv, b_qkv, w_out, b_out, kv_edge, out, kv, done, sem):
    g, b = gain[...].reshape(1, D), bias[...].reshape(1, D)
    for s, far in enumerate((far1, far2)):
        normed = layer_norm(far[:SIDE, :].astype(F32), g, b)
        for c in range(2):
            cols = slice((c + 1) * D, (c + 2) * D)
            part = mm(normed, w_qkv[:, cols]) + b_qkv[cols].reshape(1, D)
            kv[s, :, c * D : (c + 1) * D] = part
            kv_edge[s, :, c * D : (c + 1) * D] = part[3 * HALF :].astype(BF16)
    back = order_back()
    for m in range(BLOCKS - 1):
        rows = slice(m * HALF, (m + 1) * HALF)
        heads, xs = [], []
        for s, (pay, far) in enumerate(((pay1, far1), (pay2, far2))):
            both = jnp.concatenate([qkv[s, m, :, D:].astype(F32), kv[s, rows, :]], axis=0).astype(BF16)
            own_line = shifted(label_line(pay, SIDE), m * HALF, 0, 2 * HALF)
            far_line = shifted(label_line(far, SIDE), m * HALF, HALF, 2 * HALF)
            k_label = jnp.where(iota((1, 2 * HALF), 1) < HALF, own_line, far_line)
            q_label = qlab[s, rows, :][:, :1]
            heads.append(attention(qkv[s, m, :, :D].astype(F32), both[:, :D], both[:, D:], q_label, k_label))
            xs.append(pay[:SIDE, :].astype(F32)[rows])
        strips = finish(
            jnp.concatenate(heads, axis=0), jnp.concatenate(xs, axis=0), w_out[...], b_out[...].reshape(1, D), back
        )
        for r in range(WLAT):
            for l in range(LEV):
                at = (r * LEV + l) * STRIP
                done[l, m * WLAT + r] = strips[at : at + COLS]
    copy = pltpu.make_async_copy(done, out.at[:, SLAT : ROWS - SLAT], sem)
    copy.start()
    copy.wait()


def outer_kernel(pay1, pay2, far1, far2, over1, over2, qlab, qkv, kv_edge, gain, bias, w_qkv, b_qkv, w_out, b_out, so_far, out, done1, done2, sem):
    del so_far
    g, b = gain[...].reshape(1, D), bias[...].reshape(1, D)
    e1, e2 = edge_rows()
    last = BLOCKS - 1
    results = []
    for e, over in enumerate((over1, over2)):
        normed = layer_norm(over[: 4 * EDGE, :].astype(F32), g, b)
        kv = [
            mm(normed, w_qkv[:, (c + 1) * D : (c + 2) * D]) + b_qkv[(c + 1) * D : (c + 2) * D].reshape(1, D)
            for c in range(2)
        ]
        for s, (pay, far) in enumerate(((pay1, far1), (pay2, far2))):
            keys = []
            for c in range(2):
                cols = slice(c * D, (c + 1) * D)
                own = qkv[s, last, :, (c + 1) * D : (c + 2) * D].astype(F32)
                keys.append(
                    jnp.concatenate(
                        [own, kv_edge[s, :, cols].astype(F32), kv[c][2 * EDGE * s : 2 * EDGE * (s + 1)]], axis=0
                    ).astype(BF16)
                )
            count = 2 * HALF + 2 * EDGE
            lane = iota((1, count), 1)
            own_line = shifted(label_line(pay, SIDE), last * HALF, 0, count)
            far_line = shifted(label_line(far, SIDE), last * HALF, HALF, count)
            over_line = shifted(label_line(over, 4 * EDGE), 2 * EDGE * s, 2 * HALF, count)
            k_label = jnp.where(lane < HALF, own_line, jnp.where(lane < 2 * HALF, far_line, over_line))
            piece = lane - 2 * HALF
            piece = jnp.where(piece >= EDGE, piece - EDGE, piece)
            spot = jnp.where(lane < HALF, lane, jnp.where(lane < 2 * HALF, lane - HALF, piece))
            if e == 0:
                mine = spot < HALF // 2
            else:
                mine = spot >= jnp.where(lane < 2 * HALF, HALF // 2, EDGE - HALF // 2)
            k_label = jnp.where(mine, k_label, -1.0)
            at = 32 * e
            q = qkv[s, last, :, :D].astype(F32)[at : at + EDGE]
            q_label = qlab[s, last * HALF : SIDE, :][at : at + EDGE, :1]
            results.append(attention(q, keys[0], keys[1], q_label, k_label))
    heads, xs = [], []
    for s, pay in enumerate((pay1, pay2)):
        a, z = results[s], results[2 + s]
        mid = jnp.where(iota((8, 1), 0) < 4, a[32:], z[:8])
        heads.append(jnp.concatenate([a[:32], mid, z[8:]], axis=0))
        xs.append(pay[:SIDE, :].astype(F32)[last * HALF :])
    strips = finish(
        jnp.concatenate(heads, axis=0),
        jnp.concatenate(xs, axis=0),
        w_out[...],
        b_out[...].reshape(1, D),
        order_back(),
    )
    for r in range(WLAT):
        for l in range(LEV):
            at = (r * LEV + l) * STRIP
            (done1 if r < SLAT else done2)[l, r % SLAT] = strips[at : at + COLS]
    copies = [
        pltpu.make_async_copy(done, out.at[:, pl.ds(e, SLAT)], sem.at[i])
        for i, (done, e) in enumerate(((done1, e1), (done2, e2)))
    ]
    for copy in copies:
        copy.start()
    for copy in copies:
        copy.wait()


VMEM = pl.BlockSpec(memory_space=pltpu.VMEM)
ANY = pl.BlockSpec(memory_space=pl.ANY)


def params(**more):
    return pltpu.CompilerParams(vmem_limit_bytes=LIMIT, **more)


def cost(flops, moved, exps=0):
    return pl.CostEstimate(flops=flops, bytes_accessed=moved, transcendentals=exps)


def swap(block, axis, first):
    n = lax.axis_size(axis)
    route = []
    for i in range(first, n, 2):
        route += [(i, (i + 1) % n), ((i + 1) % n, i)]
    return lax.ppermute(block, axis, route)


def local(features, region_ids, ln_gain, ln_bias, w_qkv, b_qkv, w_out, b_out):
    shape = jax.ShapeDtypeStruct
    pay1, pay2, qlab = pl.pallas_call(
        prep_kernel,
        out_shape=[shape((PAY, D), BF16), shape((PAY, D), BF16), shape((2, SIDE, 128), F32)],
        in_specs=[VMEM, VMEM],
        out_specs=[VMEM] * 3,
        scratch_shapes=[
            pltpu.VMEM((ROWS * LEV * STRIP, D), BF16),
            pltpu.VMEM((ROWS * LEV * STRIP, 128), BF16),
            pltpu.VMEM((ROWS * LEV, 128), F32),
        ],
        compiler_params=params(),
        cost_estimate=cost(4 * 144 * 192 * 640 * 2, 2_000_000),
        name="prep",
    )(features, region_ids)
    far1 = swap(pay1, "lon", 1)
    far2 = swap(pay2, "lon", 0)
    qkv = pl.pallas_call(
        own_kernel,
        out_shape=shape((2, BLOCKS, HALF, 3 * D), BF16),
        in_specs=[VMEM] * 6,
        out_specs=VMEM,
        compiler_params=params(),
        cost_estimate=cost(2 * SIDE * D * 3 * D * 2, 4_000_000),
        name="own",
    )(pay1, pay2, ln_gain, ln_bias, w_qkv, b_qkv)
    edge1, edge2 = pl.pallas_call(
        edges_kernel,
        out_shape=[shape((KPAY, D), BF16)] * 2,
        in_specs=[VMEM] * 4,
        out_specs=[VMEM] * 2,
        compiler_params=params(),
        cost_estimate=cost(1_000_000, 500_000),
        name="edges",
    )(pay1, pay2, far1, far2)
    over1 = swap(edge1, "lat", 1)
    over2 = swap(edge2, "lat", 0)
    kv_edge, so_far = pl.pallas_call(
        inner_kernel,
        out_shape=[shape((2, HALF, 2 * D), BF16), shape(features.shape, BF16)],
        in_specs=[VMEM] * 12,
        out_specs=[VMEM, ANY],
        scratch_shapes=[
            pltpu.VMEM((2, SIDE, 2 * D), F32),
            pltpu.VMEM((LEV, ROWS - 2 * SLAT, COLS, D), BF16),
            pltpu.SemaphoreType.DMA(()),
        ],
        compiler_params=params(),
        cost_estimate=cost(3_000_000_000, 5_000_000, 500_000),
        name="inner",
    )(pay1, pay2, far1, far2, qlab, qkv, ln_gain, ln_bias, w_qkv, b_qkv, w_out, b_out)
    return pl.pallas_call(
        outer_kernel,
        out_shape=shape(features.shape, BF16),
        in_specs=[VMEM] * 15 + [ANY],
        out_specs=ANY,
        scratch_shapes=[
            pltpu.VMEM((LEV, SLAT, COLS, D), BF16),
            pltpu.VMEM((LEV, SLAT, COLS, D), BF16),
            pltpu.SemaphoreType.DMA((2,)),
        ],
        input_output_aliases={15: 0},
        compiler_params=params(),
        cost_estimate=cost(1_500_000_000, 5_000_000, 200_000),
        name="outer",
    )(pay1, pay2, far1, far2, over1, over2, qlab, qkv, kv_edge, ln_gain, ln_bias, w_qkv, b_qkv, w_out, b_out, so_far)


def solution(mesh):
    return jax.shard_map(
        local,
        mesh=mesh,
        in_specs=(P(None, "lat", "lon", None), P(None, "lat", "lon"), P(), P(), P(), P(), P(), P()),
        out_specs=P(None, "lat", "lon", None),
        check_vma=False,
    )
```

time: 111 us -> 71 us (0.64)
  the two profiles are of different devices: /device:TPU:8 before, /device:TPU:1 now
where the time goes in v1:
time: 71 us; the launch traced here: 70.6 us
  starting transfers between devices  30.5 us (43%)
  Pallas kernels  24.8 us (35%)
  local copies, waits for them, and re-layouts  8 us (11%)
  waiting for transfers between devices  7.31 us (10%)
    ppermute x4, starting transfers between devices, swap(): return lax.ppermute(block, axis, route)  30.5 us
    pallas_call x1, Pallas kernels, local(): pl.pallas_call(inner_kernel, out_shape=[shape((2, HALF, 2 * D), BF16), sh...  8.4 us
    pallas_call x1, Pallas kernels, local(): pl.pallas_call(outer_kernel, out_shape=shape(features.shape, BF16), in_sp...  7.47 us
    ppermute x4, waiting for transfers between devices, swap(): return lax.ppermute(block, axis, route)  7.31 us
    unnamed x10, local copies, waits for them, and re-layouts  5.73 us
    pallas_call x1, Pallas kernels, local(): pl.pallas_call(own_kernel, out_shape=shape((2, BLOCKS, HALF, 3 * D), BF16...  4.19 us
    pallas_call x1, Pallas kernels, local(): pl.pallas_call(prep_kernel, out_shape=[shape((PAY, D), BF16), shape((PAY,...  2.65 us
    pallas_call x1, local copies, waits for them, and re-layouts, local(): pl.pallas_call(outer_kernel, out_shape=shape(features.shape, BF16), in_sp...  2.28 us
  transfers between devices with their start and end apart: 4, of which 1 were waited for; matrix products, arithmetic and copies ran while one was open for 0% of the time, Pallas kernels for 18%

profile of v1, /device:TPU:1, one launch (start us, length us, event | category | flops | bytes accessed | tf_op | source)
XLA Modules:
  0.0 70.6 jit_solution(8335019498747176472)
XLA Ops:
  0.0 1.4 %copy.11.ids = s32[2,24,12]{2,1,0:T(8,128)} copy(s32[2,24,12]{1,0,2:T(2,128)} %param.9) | data formatting | bytes 4608 | tf_op args[1]
  1.4 2.1 %copy.10.feat = bf16[2,24,12,512]{3,2,1,0:T(8,128)(2,1)} copy(bf16[2,24,12,512]{3,1,2,0:T(8,128)(2,1)} %param.8) | data formatting | bytes 1179648 | tf_op args[0]
  3.5 2.7 %prep.1 = (bf16[304,512]{1,0:T(8,128)(2,1)}, bf16[304,512]{1,0:T(8,128)(2,1)}, f32[2,288,128]{2,1,0:T(8,128)}) custom-call(bf16[2,24,12,512]{3,2,1,0:T(8,128)(2,1)} %copy.10.feat, s32[2,24,12]{2,1,0:T(8,128)} %copy.11.ids), custom_call_target="tpu_custom_call" | custom-call | flops 141557760 | bytes 2000000 | tf_op jit(solution)/shard_map/prep/pallas_call | solution.py:296
  6.2 4.9 %collective-permute-start = (bf16[304,512]{1,0:T(8,128)(2,1)}, bf16[304,512]{1,0:T(8,128)(2,1)S(1)}, u32[]{:S(2)}, u32[]{:S(2)}) collective-permute-start(bf16[304,512]{1,0:T(8,128)(2,1)} %get-tuple-element.12.pay1), channel_id=1, source_target_pairs={{8,16},{16,8},{24,32},{32,24},{40,48},{48,40},{56,64},{64,56},{72,... | collective-permute-start | bytes 933896 | tf_op jit(solution)/shard_map/ppermute | solution.py:291
  11.1 13.5 %collective-permute-start.1 = (bf16[304,512]{1,0:T(8,128)(2,1)}, bf16[304,512]{1,0:T(8,128)(2,1)S(1)}, u32[]{:S(2)}, u32[]{:S(2)}) collective-permute-start(bf16[304,512]{1,0:T(8,128)(2,1)} %get-tuple-element.13.pay2), channel_id=1, source_target_pairs={{0,8},{8,0},{16,24},{24,16},{32,40},{40,32},{48,56},{56,48},{64,72... | collective-permute-start | bytes 933896 | tf_op jit(solution)/shard_map/ppermute | solution.py:291
  24.6 4.2 %own.1.qkv = bf16[2,4,72,1536]{3,2,1,0:T(8,128)(2,1)} custom-call(bf16[304,512]{1,0:T(8,128)(2,1)} %get-tuple-element.12.pay1, bf16[304,512]{1,0:T(8,128)(2,1)} %get-tuple-element.13.pay2, f32[512]{0:T(512)} %gain.5, f32[512]{0:T(512)} %bias.5, bf16[512,1536]{1,0:T(8,128)(2,1)} %w_qkv.5, f32[1536]{0:T(1024)} %b_qkv.5), custom_call_target="tpu_custom_call" | custom-call | flops 905969664 | bytes 4000000 | tf_op jit(solution)/shard_map/own/pallas_call | solution.py:312
  28.8 0.0 collective-permute-done.far1
  28.8 0.0 copy-start
  28.8 0.0 collective-permute-done.1.far2
  28.8 0.7 %copy-done = bf16[304,512]{1,0:T(8,128)(2,1)} copy-done((bf16[304,512]{1,0:T(8,128)(2,1)}, bf16[304,512]{1,0:T(8,128)(2,1)S(1)}, u32[]{:S(2)}) %copy-start) | copy-done | bytes 311320
  29.6 0.0 copy-start.1
  29.6 0.7 %copy-done.1 = bf16[304,512]{1,0:T(8,128)(2,1)} copy-done((bf16[304,512]{1,0:T(8,128)(2,1)}, bf16[304,512]{1,0:T(8,128)(2,1)S(1)}, u32[]{:S(2)}) %copy-start.1) | copy-done | bytes 311320
  30.3 2.1 %edges.1 = (bf16[176,512]{1,0:T(8,128)(2,1)}, bf16[176,512]{1,0:T(8,128)(2,1)}) custom-call(bf16[304,512]{1,0:T(8,128)(2,1)} %get-tuple-element.12.pay1, bf16[304,512]{1,0:T(8,128)(2,1)} %get-tuple-element.13.pay2, bf16[304,512]{1,0:T(8,128)(2,1)} %copy-done, bf16[304,512]{1,0:T(8,128)(2,1)} %copy-done.1), custom_call_target="tpu_custom_call" | custom-call | flops 1000000 | bytes 500000 | tf_op jit(solution)/shard_map/edges/pallas_call | solution.py:321
  32.4 10.1 %collective-permute-start.2 = (bf16[176,512]{1,0:T(8,128)(2,1)}, bf16[176,512]{1,0:T(8,128)(2,1)S(1)}, u32[]{:S(2)}, u32[]{:S(2)}) collective-permute-start(bf16[176,512]{1,0:T(8,128)(2,1)} %get-tuple-element.14), channel_id=1, source_target_pairs={{1,2},{2,1},{3,4},{4,3},{5,6},{6,5},{7,0},{0,7},{9,10},{10,9},{11,... | collective-permute-start | bytes 540680 | tf_op jit(solution)/shard_map/ppermute | solution.py:291
  42.5 1.9 %collective-permute-start.3 = (bf16[176,512]{1,0:T(8,128)(2,1)}, bf16[176,512]{1,0:T(8,128)(2,1)S(1)}, u32[]{:S(2)}, u32[]{:S(2)}) collective-permute-start(bf16[176,512]{1,0:T(8,128)(2,1)} %get-tuple-element.15), channel_id=1, source_target_pairs={{0,1},{1,0},{2,3},{3,2},{4,5},{5,4},{6,7},{7,6},{8,9},{9,8},{10,11... | collective-permute-start | bytes 540680 | tf_op jit(solution)/shard_map/ppermute | solution.py:291
  44.4 8.4 %inner.1 = (bf16[2,72,1024]{2,1,0:T(8,128)(2,1)}, bf16[2,24,12,512]{3,2,1,0:T(8,128)(2,1)}) custom-call(bf16[304,512]{1,0:T(8,128)(2,1)} %get-tuple-element.12.pay1, bf16[304,512]{1,0:T(8,128)(2,1)} %get-tuple-element.13.pay2, bf16[304,512]{1,0:T(8,128)(2,1)} %copy-done, bf16[304,512]{1,0:T(8,128)(2,1)} %copy-done.1, f32[2,288,128]{2,1,0:T(8,128)} %get-tuple-element.16.qlab, ...), custom_call_target="tpu_custom_call" | custom-call | flops 3000000000 | bytes 5000000 | tf_op jit(solution)/shard_map/inner/pallas_call | solution.py:332
  52.8 7.3 %collective-permute-done.2.over1 = bf16[176,512]{1,0:T(8,128)(2,1)S(1)} collective-permute-done((bf16[176,512]{1,0:T(8,128)(2,1)}, bf16[176,512]{1,0:T(8,128)(2,1)S(1)}, u32[]{:S(2)}, u32[]{:S(2)}) %collective-permute-start.2) | collective-permute-done | bytes 180256 | tf_op jit(solution)/shard_map/ppermute | solution.py:291
  60.1 0.0 copy-start.2
  60.1 0.0 collective-permute-done.3.over2
  60.1 0.0 copy-start.3
  60.2 0.6 copy-done.2
  60.8 0.1 copy-done.3
  60.9 7.5 %outer.1 = bf16[2,24,12,512]{3,2,1,0:T(8,128)(2,1)} custom-call(bf16[304,512]{1,0:T(8,128)(2,1)} %get-tuple-element.12.pay1, bf16[304,512]{1,0:T(8,128)(2,1)} %get-tuple-element.13.pay2, bf16[304,512]{1,0:T(8,128)(2,1)} %copy-done, bf16[304,512]{1,0:T(8,128)(2,1)} %copy-done.1, bf16[176,512]{1,0:T(8,128)(2,1)} %copy-done.2, ...), custom_call_target="tpu_custom_call", output_to_operand_aliasing={{}: (15, {})} | custom-call | flops 1500000000 | bytes 5000000 | tf_op jit(solution)/shard_map/outer/pallas_call | solution.py:346
  68.4 2.3 %copy.12 = bf16[2,24,12,512]{3,1,2,0:T(8,128)(2,1)} copy(bf16[2,24,12,512]{3,2,1,0:T(8,128)(2,1)} %outer.1) | data formatting | bytes 1179648 | tf_op jit(solution)/shard_map/outer/pallas_call | solution.py:346
Async XLA Ops:
  6.2 22.7 %collective-permute-start = (bf16[304,512]{1,0:T(8,128)(2,1)}, bf16[304,512]{1,0:T(8,128)(2,1)S(1)}, u32[]{:S(2)}, u32[]{:S(2)}) collective-permute-start(bf16[304,512]{1,0:T(8,128)(2,1)} %get-tuple-element.12.pay1), channel_id=1, source_target_pairs={{8,16},{16,8},{24,32},{32,24},{40,48},{48,40},{56,64},{64,56},{72,... | collective-permute-start | bytes 933896 | tf_op jit(solution)/shard_map/ppermute | solution.py:291
  11.1 17.7 %collective-permute-start.1 = (bf16[304,512]{1,0:T(8,128)(2,1)}, bf16[304,512]{1,0:T(8,128)(2,1)S(1)}, u32[]{:S(2)}, u32[]{:S(2)}) collective-permute-start(bf16[304,512]{1,0:T(8,128)(2,1)} %get-tuple-element.13.pay2), channel_id=1, source_target_pairs={{0,8},{8,0},{16,24},{24,16},{32,40},{40,32},{48,56},{56,48},{64,72... | collective-permute-start | bytes 933896 | tf_op jit(solution)/shard_map/ppermute | solution.py:291
  28.8 0.7 %copy-start = (bf16[304,512]{1,0:T(8,128)(2,1)}, bf16[304,512]{1,0:T(8,128)(2,1)S(1)}, u32[]{:S(2)}) copy-start(bf16[304,512]{1,0:T(8,128)(2,1)S(1)} %collective-permute-done.far1) | copy-start | bytes 933892
  29.6 0.7 %copy-start.1 = (bf16[304,512]{1,0:T(8,128)(2,1)}, bf16[304,512]{1,0:T(8,128)(2,1)S(1)}, u32[]{:S(2)}) copy-start(bf16[304,512]{1,0:T(8,128)(2,1)S(1)} %collective-permute-done.1.far2) | copy-start | bytes 933892
  32.4 27.8 %collective-permute-start.2 = (bf16[176,512]{1,0:T(8,128)(2,1)}, bf16[176,512]{1,0:T(8,128)(2,1)S(1)}, u32[]{:S(2)}, u32[]{:S(2)}) collective-permute-start(bf16[176,512]{1,0:T(8,128)(2,1)} %get-tuple-element.14), channel_id=1, source_target_pairs={{1,2},{2,1},{3,4},{4,3},{5,6},{6,5},{7,0},{0,7},{9,10},{10,9},{11,... | collective-permute-start | bytes 540680 | tf_op jit(solution)/shard_map/ppermute | solution.py:291
  42.5 17.6 %collective-permute-start.3 = (bf16[176,512]{1,0:T(8,128)(2,1)}, bf16[176,512]{1,0:T(8,128)(2,1)S(1)}, u32[]{:S(2)}, u32[]{:S(2)}) collective-permute-start(bf16[176,512]{1,0:T(8,128)(2,1)} %get-tuple-element.15), channel_id=1, source_target_pairs={{0,1},{1,0},{2,3},{3,2},{4,5},{5,4},{6,7},{7,6},{8,9},{9,8},{10,11... | collective-permute-start | bytes 540680 | tf_op jit(solution)/shard_map/ppermute | solution.py:291
  60.1 0.7 copy-start.2
  60.1 0.7 %copy-start.3 = (bf16[176,512]{1,0:T(8,128)(2,1)}, bf16[176,512]{1,0:T(8,128)(2,1)S(1)}, u32[]{:S(2)}) copy-start(bf16[176,512]{1,0:T(8,128)(2,1)S(1)} %collective-permute-done.3.over2) | copy-start | bytes 540676

commit v2 on v0

v2 whole, which is shorter than its diff:
```python
import functools

import jax
import jax.numpy as jnp
from jax import lax
from jax.experimental import pallas as pl
from jax.experimental.pallas import tpu as pltpu
from jax.sharding import PartitionSpec as P

HEADS = 8
WLAT = 6
WLON = 12
SLAT = 3
SLON = 6
LEV = 2
D = 512
HS = D // HEADS
ROWS = 24
COLS = 12
HALF = WLAT * LEV * SLON
BLOCKS = ROWS // WLAT
SIDE = BLOCKS * HALF
PAY = SIDE + 16
EDGE = 40
LAT_RUN = 4
LON_RUN = 16
F32 = jnp.float32
BF16 = jnp.bfloat16
LIMIT = 24 * 1024 * 1024


def mm(a, b):
    return jnp.dot(a, b, preferred_element_type=F32)


def mm_nt(a, b):
    return lax.dot_general(a, b, (((1,), (1,)), ((), ())), preferred_element_type=F32)


def iota(shape, dim):
    return lax.broadcasted_iota(jnp.int32, shape, dim)


def place_of(n, odd_lat):
    l = jnp.where(n >= SIDE // 2, 1, 0)
    n = n - SIDE // 2 * l
    c = sum(jnp.where(n >= ROWS * q, 1, 0) for q in range(1, SLON))
    i = n - ROWS * c
    top = 3 * HALF + HALF // 2 * odd_lat + 12 * i
    bottom = 3 * HALF + HALF // 2 * (1 - odd_lat) + 12 * (i - (ROWS - SLAT))
    base = jnp.where(i < SLAT, top, jnp.where(i >= ROWS - SLAT, bottom, 12 * (i - SLAT)))
    return base + SLON * l + c, i, LEV * c + l


def layer_norm(x, gain, bias):
    center = x - jnp.mean(x, axis=-1, keepdims=True)
    spread = jnp.mean(center * center, axis=-1, keepdims=True)
    return (center * lax.rsqrt(spread + 1e-05) * gain + bias).astype(BF16)


def side_rows(s, l):
    odd = lax.axis_index("lon") % 2
    half = odd if s == 0 else 1 - odd
    return pl.multiple_of(l * SIDE + half * (SIDE // 2), SIDE // 2)


def prep_kernel(feat, ids, pay1, pay2, qlab, lab):
    odd_lon = lax.axis_index("lon") % 2
    odd_lat = lax.axis_index("lat") % 2
    first = lax.axis_index("lat") == 0
    place, lat, strip = place_of(iota((1, SIDE), 1), odd_lat)
    order = jnp.where(iota((SIDE, SIDE), 0) == place, 1.0, 0.0)
    spread = jnp.where(iota((128, SIDE), 0) == lat, 1.0, 0.0).astype(BF16)
    from_first = jnp.where((iota((LEV, ROWS), 1) < SLAT) & first, 4.0, 0.0)
    lab[...] = jnp.zeros_like(lab)
    for s, pay in enumerate((pay1, pay2)):
        tokens = jnp.concatenate([feat[pl.ds(side_rows(s, l), SIDE // 2), :] for l in range(LEV)], axis=0)
        pay[:SIDE, :] = mm(order.astype(BF16), tokens).astype(BF16)
        half = odd_lon if s == 0 else 1 - odd_lon
        for c in range(SLON):
            lab[s, LEV * c : LEV * (c + 1), :ROWS] = ids[SLON * half + c].astype(F32) + from_first
        line = mm(lab[s].astype(BF16), spread)
        line = jnp.sum(jnp.where(iota((16, SIDE), 0) == strip, line, 0.0), axis=0, keepdims=True)
        qlab[s] = jnp.broadcast_to(jnp.sum(order * line, axis=-1, keepdims=True), (SIDE, 128))
        line = mm_nt(jnp.broadcast_to(line, (16, SIDE)).astype(BF16), order.astype(BF16))
        pay[SIDE:, :] = jnp.concatenate([line, jnp.zeros((16, D - SIDE), F32)], axis=1).astype(BF16)


def own_kernel(pay1, pay2, gain, bias, w_qkv, b_qkv, qkv):
    g, b = gain[...].reshape(1, D), bias[...].reshape(1, D)
    for s, pay in enumerate((pay1, pay2)):
        normed = layer_norm(pay[:SIDE, :].astype(F32), g, b)
        for c in range(3):
            cols = slice(c * D, (c + 1) * D)
            part = mm(normed, w_qkv[:, cols]) + b_qkv[cols].reshape(1, D)
            part = part.astype(BF16).astype(F32)
            if c == 0:
                part = part * HS ** (-0.5)
            for m in range(BLOCKS):
                qkv[s, m, :, cols] = part[m * HALF : (m + 1) * HALF].astype(BF16)


def label_line(ref, at):
    return ref[...].astype(F32)[at : at + 8]


def shifted(line, start, to):
    return pltpu.roll(line, (to - start) % D, 1)


def attention(q, k, v, q_label, k_label):
    n = q.shape[0]
    keys = k.shape[0]
    wide = 4 * HS
    allowed = q_label == k_label
    out = []
    col = iota((1, wide), 1)
    for g in range(2):
        cols = slice(g * wide, (g + 1) * wide)
        own = [(col >= h * HS) & (col < (h + 1) * HS) for h in range(4)]
        qg = q[:, cols]
        stacked = jnp.concatenate([jnp.where(o, qg, 0.0) for o in own], axis=0).astype(BF16)
        scores = mm_nt(stacked, k[:, cols])
        scores = jnp.where(allowed[None], scores.reshape(4, n, keys), -1e30)
        top = jnp.max(scores, axis=-1, keepdims=True)
        expd = jnp.exp(scores - top)
        weights = (expd / jnp.sum(expd, axis=-1, keepdims=True)).astype(BF16)
        full = mm(weights.reshape(4 * n, keys), v[:, cols])
        picked = jnp.where(own[0], full[:n], 0.0)
        for h in range(1, 4):
            picked = jnp.where(own[h], full[h * n : (h + 1) * n], picked)
        out.append(picked)
    return jnp.concatenate(out, axis=1)


def finish(heads, x, w_out, b_out):
    projected = (mm(heads.astype(BF16), w_out) + b_out).astype(BF16).astype(F32)
    return (x + projected).astype(BF16)


def edge_piece(ref, e):
    at = 3 * HALF + 32 * e
    return ref[...].astype(F32)[at : at + EDGE]


def edge_labels(parts):
    lane = iota((8, D), 1)
    out = jnp.zeros((8, D), F32)
    for j, (line, start) in enumerate(parts):
        out = jnp.where((lane >= j * EDGE) & (lane < (j + 1) * EDGE), shifted(line, start, j * EDGE), out)
    return out


def edge_kernel(e, *refs):
    sides, out = refs[:-1], refs[-1]
    rows = [edge_piece(ref, e) for ref in sides]
    line = edge_labels([(label_line(ref, SIDE), 3 * HALF + 32 * e) for ref in sides])
    rows += [line] * ((out.shape[0] - len(rows) * EDGE) // 8)
    out[...] = jnp.concatenate(rows, axis=0).astype(BF16)


def far_pairs(axis, size):
    at = lax.axis_index(axis)
    return (at % size == 0) | (at % size == size - 1)


def corner_kernel(pay1, far1, over1, out):
    lat_far = far_pairs("lat", LAT_RUN)
    both_far = lat_far & far_pairs("lon", LON_RUN)
    a, b, c = edge_piece(pay1, 0), edge_piece(far1, 0), over1[...].astype(F32)[:EDGE]
    la, lb = (shifted(label_line(ref, SIDE), 3 * HALF, 0) for ref in (pay1, far1))
    lc = label_line(over1, 3 * EDGE)
    one = jnp.where(both_far, 1.0, 0.0)
    two = jnp.where(lat_far, 1.0, 0.0)

    def choose(a, b, c):
        return jnp.where(jnp.full(a.shape, one) > 0.5, a, jnp.where(jnp.full(a.shape, two) > 0.5, c, b))

    out[...] = jnp.concatenate([choose(a, b, c), choose(la, lb, lc)], axis=0).astype(BF16)


def inner_kernel(pay1, pay2, far1, far2, qlab, qkv, gain, bias, w_qkv, b_qkv, w_out, b_out, kv_edge, mixed, back, kv):
    g, b = gain[...].reshape(1, D), bias[...].reshape(1, D)
    for s, far in enumerate((far1, far2)):
        normed = layer_norm(far[:SIDE, :].astype(F32), g, b)
        for c in range(2):
            cols = slice((c + 1) * D, (c + 2) * D)
            part = mm(normed, w_qkv[:, cols]) + b_qkv[cols].reshape(1, D)
            kv[s, :, c * D : (c + 1) * D] = part
            kv_edge[s, :, c * D : (c + 1) * D] = part[3 * HALF :].astype(BF16)
    place, _, _ = place_of(iota((SIDE, 1), 0), lax.axis_index("lat") % 2)
    back[...] = jnp.where(iota((SIDE, SIDE), 1) == place, 1.0, 0.0).astype(BF16)
    for m in range(BLOCKS - 1):
        rows = slice(m * HALF, (m + 1) * HALF)
        heads, xs = [], []
        for s, (pay, far) in enumerate(((pay1, far1), (pay2, far2))):
            both = jnp.concatenate([qkv[s, m, :, D:].astype(F32), kv[s, rows, :]], axis=0).astype(BF16)
            own_line = shifted(label_line(pay, SIDE), m * HALF, 0)[:1, : 2 * HALF]
            far_line = shifted(label_line(far, SIDE), m * HALF, HALF)[:1, : 2 * HALF]
            k_label = jnp.where(iota((1, 2 * HALF), 1) < HALF, own_line, far_line)
            q_label = qlab[s, rows, :][:, :1]
            heads.append(attention(qkv[s, m, :, :D].astype(F32), both[:, :D], both[:, D:], q_label, k_label))
            xs.append(pay[:SIDE, :].astype(F32)[rows])
        done = finish(jnp.concatenate(heads, axis=0), jnp.concatenate(xs, axis=0), w_out[...], b_out[...].reshape(1, D))
        mixed[0, m] = done[:HALF]
        mixed[1, m] = done[HALF:]


def project_kv(x, g, b, w_qkv, b_qkv):
    normed = layer_norm(x, g, b)
    return [
        mm(normed, w_qkv[:, (c + 1) * D : (c + 2) * D]) + b_qkv[(c + 1) * D : (c + 2) * D].reshape(1, D) for c in range(2)
    ]


def edge_window(e, s, pay, far, over_kv, over_line, qlab, qkv, kv_edge):
    last = BLOCKS - 1
    keys = []
    for c in range(2):
        own = qkv[s, last, :, (c + 1) * D : (c + 2) * D].astype(F32)
        far_part = kv_edge[s, :, c * D : (c + 1) * D].astype(F32)
        keys.append(jnp.concatenate([own, far_part, over_kv[c]], axis=0).astype(BF16))
    count = 2 * HALF + 2 * EDGE
    lane = iota((1, count), 1)
    own_line = shifted(label_line(pay, SIDE), last * HALF, 0)[:1, :count]
    far_line = shifted(label_line(far, SIDE), last * HALF, HALF)[:1, :count]
    k_label = jnp.where(lane < HALF, own_line, jnp.where(lane < 2 * HALF, far_line, over_line[:1, :count]))
    piece = lane - 2 * HALF
    piece = jnp.where(piece >= EDGE, piece - EDGE, piece)
    spot = jnp.where(lane < HALF, lane, jnp.where(lane < 2 * HALF, lane - HALF, piece))
    if e == 0:
        mine = spot < HALF // 2
    else:
        mine = spot >= jnp.where(lane < 2 * HALF, HALF // 2, EDGE - HALF // 2)
    k_label = jnp.where(mine, k_label, -1.0)
    at = 32 * e
    q = qkv[s, last, :, :D].astype(F32)[at : at + EDGE]
    q_label = qlab[s, last * HALF : SIDE, :][at : at + EDGE, :1]
    return attention(q, keys[0], keys[1], q_label, k_label)


def outer_kernel(
    pay1, pay2, far1, far2, over1, over2, corner, qlab, qkv, kv_edge, mixed, back, gain, bias, w_qkv, b_qkv, w_out, b_out, out
):
    g, b = gain[...].reshape(1, D), bias[...].reshape(1, D)
    kv1 = project_kv(over1[...].astype(F32), g, b, w_qkv, b_qkv)
    kv2 = project_kv(over2[...].astype(F32), g, b, w_qkv, b_qkv)
    kv3 = project_kv(corner[...].astype(F32), g, b, w_qkv, b_qkv)
    line1, line2 = label_line(over1, 3 * EDGE), label_line(over2, 4 * EDGE)
    line3 = label_line(corner, EDGE)
    lane = iota((8, D), 1)
    first = jnp.where(lane < 2 * HALF + EDGE, shifted(line1, 0, 2 * HALF), shifted(line3, 0, 2 * HALF + EDGE))
    rest = (qlab, qkv, kv_edge)
    z0 = edge_window(1, 0, pay1, far1, [k[: 2 * EDGE] for k in kv2], shifted(line2, 0, 2 * HALF), *rest)
    z1 = edge_window(1, 1, pay2, far2, [k[2 * EDGE : 4 * EDGE] for k in kv2], shifted(line2, 2 * EDGE, 2 * HALF), *rest)
    a1 = edge_window(0, 1, pay2, far2, [k[EDGE : 3 * EDGE] for k in kv1], shifted(line1, EDGE, 2 * HALF), *rest)
    a0_kv = [jnp.concatenate([k1[:EDGE], k3[:EDGE]], axis=0) for k1, k3 in zip(kv1, kv3)]
    a0 = edge_window(0, 0, pay1, far1, a0_kv, first, *rest)
    heads, xs = [], []
    for pay, a, z in ((pay1, a0, z0), (pay2, a1, z1)):
        mid = jnp.where(iota((8, 1), 0) < 4, a[32:], z[:8])
        heads.append(jnp.concatenate([a[:32], mid, z[8:]], axis=0))
        xs.append(pay[:SIDE, :].astype(F32)[3 * HALF :])
    edges = finish(jnp.concatenate(heads, axis=0), jnp.concatenate(xs, axis=0), w_out[...], b_out[...].reshape(1, D))
    edges = edges.astype(F32)
    for s in range(2):
        parts = [mixed[s, m].astype(F32) for m in range(BLOCKS - 1)] + [edges[s * HALF : (s + 1) * HALF]]
        done = mm(back[...], jnp.concatenate(parts, axis=0).astype(BF16)).astype(BF16)
        for l in range(LEV):
            out[pl.ds(side_rows(s, l), SIDE // 2), :] = done[l * (SIDE // 2) : (l + 1) * (SIDE // 2)]


VMEM = pl.BlockSpec(memory_space=pltpu.VMEM)


def cost(flops, moved, exps=0):
    return pl.CostEstimate(flops=flops, bytes_accessed=moved, transcendentals=exps)


def call(kernel, name, outs, args, flops, scratch=(), keep=True):
    make = pltpu.VMEM if keep else jax.ShapeDtypeStruct
    return pl.pallas_call(
        kernel,
        out_shape=[make(shape, dtype) for shape, dtype in outs],
        in_specs=[VMEM] * len(args),
        out_specs=[VMEM] * len(outs),
        scratch_shapes=list(scratch),
        compiler_params=pltpu.CompilerParams(vmem_limit_bytes=LIMIT),
        cost_estimate=cost(flops, 4_000_000, 500_000),
        name=name,
    )(*args)


def held(x):
    return pltpu.with_memory_space_constraint(x, pltpu.VMEM)


def pairs(axis, first):
    n = lax.axis_size(axis)
    return [(i, (i + 1) % n) for i in range(first, n, 2)]


def swap(block, axis, first):
    route = [way for i, j in pairs(axis, first) for way in ((i, j), (j, i))]
    return held(lax.ppermute(block, axis, route))


def swap_corners(block):
    n_lon, n_lat = lax.axis_size("lon"), lax.axis_size("lat")
    over_lon = {i: j for p in pairs("lon", 1) for i, j in (p, p[::-1])}
    over_lat = {i: j for p in pairs("lat", 1) for i, j in (p, p[::-1])}
    route = []
    for o in range(n_lon):
        for a in range(n_lat):
            to_o, to_a = o, a
            if a % LAT_RUN in (0, LAT_RUN - 1):
                to_o = over_lon[o]
                if o % LON_RUN in (0, LON_RUN - 1):
                    to_a = over_lat[a]
            else:
                to_a = over_lat[a]
            route.append((o * n_lat + a, to_o * n_lat + to_a))
    return held(lax.ppermute(block, ("lon", "lat"), route))


def local(features, region_ids, ln_gain, ln_bias, w_qkv, b_qkv, w_out, b_out):
    feat = features.transpose(0, 2, 1, 3).reshape(2 * SIDE, D)
    ids = region_ids.transpose(2, 0, 1)
    norm = (held(ln_gain), held(ln_bias))
    into = (held(w_qkv), held(b_qkv))
    outof = (held(w_out), held(b_out))
    pay1, pay2, qlab = call(
        prep_kernel,
        "prep",
        [((PAY, D), BF16), ((PAY, D), BF16), ((2, SIDE, 128), F32)],
        (feat, ids),
        200_000_000,
        [pltpu.VMEM((2, 16, 128), F32)],
    )
    pay1, pay2, qlab = held(pay1), held(pay2), held(qlab)
    far2 = swap(pay2, "lon", 0)
    far1 = swap(pay1, "lon", 1)
    (edge1,) = call(
        functools.partial(edge_kernel, 0), "edge1", [((3 * EDGE + 8, D), BF16)], (pay1, pay2, far2), 1_000_000
    )
    over1 = swap(edge1, "lat", 1)
    (qkv,) = call(own_kernel, "own", [((2, BLOCKS, HALF, 3 * D), BF16)], (pay1, pay2, *norm, *into), 900_000_000)
    qkv = held(qkv)
    (edge2,) = call(
        functools.partial(edge_kernel, 1), "edge2", [((4 * EDGE + 16, D), BF16)], (pay1, far1, pay2, far2), 1_000_000
    )
    over2 = swap(edge2, "lat", 0)
    kv_edge, mixed, back = call(
        inner_kernel,
        "inner",
        [((2, HALF, 2 * D), BF16), ((2, BLOCKS - 1, HALF, D), BF16), ((SIDE, SIDE), BF16)],
        (pay1, pay2, far1, far2, qlab, qkv, *norm, *into, *outof),
        3_000_000_000,
        [pltpu.VMEM((2, SIDE, 2 * D), F32)],
    )
    kv_edge, mixed, back = held(kv_edge), held(mixed), held(back)
    (bend,) = call(corner_kernel, "corner", [((EDGE + 8, D), BF16)], (pay1, far1, over1), 1_000_000)
    corner = swap_corners(bend)
    (out,) = call(
        outer_kernel,
        "outer",
        [((2 * SIDE, D), BF16)],
        (pay1, pay2, far1, far2, over1, over2, corner, qlab, qkv, kv_edge, mixed, back, *norm, *into, *outof),
        1_500_000_000,
        keep=False,
    )
    return out.reshape(LEV, COLS, ROWS, D).transpose(0, 2, 1, 3)


def solution(mesh):
    return jax.shard_map(
        local,
        mesh=mesh,
        in_specs=(P(None, "lat", "lon", None), P(None, "lat", "lon"), P(), P(), P(), P(), P(), P()),
        out_specs=P(None, "lat", "lon", None),
        check_vma=False,
    )
```

time: 111 us -> 55.6 us (0.50)
  the two profiles are of different devices: /device:TPU:8 before, /device:TPU:1 now
where the time goes in v2:
time: 55.6 us; the launch traced here: 54.6 us
  starting transfers between devices  40.8 us (73%)
  Pallas kernels  11.2 us (20%)
  local copies, waits for them, and re-layouts  1.91 us (3%)
    ppermute x4, starting transfers between devices, swap(): return held(lax.ppermute(block, axis, route))  25.6 us
    ppermute x1, starting transfers between devices, swap_corners(): return held(lax.ppermute(block, ('lon', 'lat'), route))  15.2 us
    pallas_call x7, Pallas kernels, call(): pl.pallas_call(kernel, out_shape=[make(shape, dtype) for shape, dtype in...  11.2 us
    unnamed x16, local copies, waits for them, and re-layouts  1.91 us
  transfers between devices with their start and end apart: 5, of which 1 were waited for; matrix products, arithmetic and copies ran while one was open for 0% of the time, Pallas kernels for 10%

profile of v2, /device:TPU:1, one launch (start us, length us, event | category | flops | bytes accessed | tf_op | source)
XLA Modules:
  0.0 54.6 jit_solution(1230038456046346228)
XLA Ops:
  0.0 0.0 copy-start.3
  0.0 0.0 copy-start.6
  0.0 1.2 %copy-done.6 = bf16[2,24,12,512]{3,1,2,0:T(8,128)(2,1)S(1)} copy-done((bf16[2,24,12,512]{3,1,2,0:T(8,128)(2,1)S(1)}, bf16[2,24,12,512]{3,1,2,0:T(8,128)(2,1)}, u32[]{:S(2)}) %copy-start.6) | copy-done | bytes 589848
  1.2 0.7 %copy-done.7 = s32[2,24,12]{1,0,2:T(2,128)S(1)} copy-done((s32[2,24,12]{1,0,2:T(2,128)S(1)}, s32[2,24,12]{1,0,2:T(2,128)}, u32[]{:S(2)}) %copy-start.7) | copy-done | bytes 2328
  1.9 0.8 %prep.1 = (bf16[304,512]{1,0:T(8,128)(2,1)S(1)}, bf16[304,512]{1,0:T(8,128)(2,1)S(1)}, f32[2,288,128]{2,1,0:T(8,128)S(1)}) custom-call(bf16[576,512]{1,0:T(8,128)(2,1)S(1)} %bitcast.7, s32[12,2,24]{2,1,0:T(2,128)S(1)} %bitcast.8), custom_call_target="tpu_custom_call" | custom-call | flops 200000000 | bytes 4000000 | tf_op jit(solution)/shard_map/prep/pallas_call | solution.py:282
  2.7 8.8 %collective-permute-start.1 = (bf16[304,512]{1,0:T(8,128)(2,1)S(1)}, bf16[304,512]{1,0:T(8,128)(2,1)S(1)}, u32[]{:S(2)}, u32[]{:S(2)}) collective-permute-start(bf16[304,512]{1,0:T(8,128)(2,1)S(1)} %get-tuple-element.12.refs_1_.refs_2_.pay2), channel_id=1, source_target_pairs={{0,8},{8,0},{16,24},{24,16},{32,40},{40,32},{48,56},{56,48},{64,72... | collective-permute-start | bytes 933896 | tf_op jit(solution)/shard_map/ppermute | solution.py:305
  11.5 1.9 %collective-permute-start = (bf16[304,512]{1,0:T(8,128)(2,1)S(1)}, bf16[304,512]{1,0:T(8,128)(2,1)S(1)}, u32[]{:S(2)}, u32[]{:S(2)}) collective-permute-start(bf16[304,512]{1,0:T(8,128)(2,1)S(1)} %get-tuple-element.11.refs_0_.pay1), channel_id=1, source_target_pairs={{8,16},{16,8},{24,32},{32,24},{40,48},{48,40},{56,64},{64,56},{72,... | collective-permute-start | bytes 933896 | tf_op jit(solution)/shard_map/ppermute | solution.py:305
  13.4 0.0 collective-permute-done.1.refs_2_.refs_3_.far2
  13.5 0.1 edge1.1
  13.5 12.9 %collective-permute-start.2 = (bf16[128,512]{1,0:T(8,128)(2,1)S(1)}, bf16[128,512]{1,0:T(8,128)(2,1)S(1)}, u32[]{:S(2)}, u32[]{:S(2)}) collective-permute-start(bf16[128,512]{1,0:T(8,128)(2,1)S(1)} %edge1.1), channel_id=1, source_target_pairs={{1,2},{2,1},{3,4},{4,3},{5,6},{6,5},{7,0},{0,7},{9,10},{10,9},{11,... | collective-permute-start | bytes 393224 | tf_op jit(solution)/shard_map/ppermute | solution.py:305
  26.5 1.3 %own.1.qkv = bf16[2,4,72,1536]{3,2,1,0:T(8,128)(2,1)S(1)} custom-call(bf16[304,512]{1,0:T(8,128)(2,1)S(1)} %get-tuple-element.11.refs_0_.pay1, bf16[304,512]{1,0:T(8,128)(2,1)S(1)} %get-tuple-element.12.refs_1_.refs_2_.pay2, f32[512]{0:T(512)S(1)} %copy-done.3, f32[512]{0:T(512)S(1)} %copy-done.4, bf16[512,1536]{1,0:T(8,128)(2,1)S(1)} %copy-done, ...), custom_call_target="tpu_custom_call" | custom-call | flops 900000000 | bytes 4000000 | tf_op jit(solution)/shard_map/own/pallas_call | solution.py:282
  27.8 0.0 copy-start.1
  27.8 0.0 copy-start.5
  27.8 0.0 collective-permute-done.refs_1_.far1
  27.8 0.1 edge2.1
  27.9 2.0 %collective-permute-start.3 = (bf16[176,512]{1,0:T(8,128)(2,1)S(1)}, bf16[176,512]{1,0:T(8,128)(2,1)S(1)}, u32[]{:S(2)}, u32[]{:S(2)}) collective-permute-start(bf16[176,512]{1,0:T(8,128)(2,1)S(1)} %edge2.1), channel_id=1, source_target_pairs={{0,1},{1,0},{2,3},{3,2},{4,5},{5,4},{6,7},{7,6},{8,9},{9,8},{10,11... | collective-permute-start | bytes 540680 | tf_op jit(solution)/shard_map/ppermute | solution.py:305
  30.0 0.5 collective-permute-done.2.over1
  30.4 0.1 corner.1
  30.5 15.2 %collective-permute-start.4 = (bf16[48,512]{1,0:T(8,128)(2,1)S(1)}, bf16[48,512]{1,0:T(8,128)(2,1)S(1)}, u32[]{:S(2)}, u32[]{:S(2)}) collective-permute-start(bf16[48,512]{1,0:T(8,128)(2,1)S(1)} %corner.1), channel_id=1, source_target_pairs={{0,511},{1,2},{2,1},{3,508},{4,507},{5,6},{6,5},{7,504},{8,16},{9,... | collective-permute-start | bytes 147464 | tf_op jit(solution)/shard_map/ppermute | solution.py:323
  45.7 0.0 copy-done.1
  45.7 3.8 %inner.1 = (bf16[2,72,1024]{2,1,0:T(8,128)(2,1)S(1)}, bf16[2,3,72,512]{3,2,1,0:T(8,128)(2,1)S(1)}, bf16[288,288]{1,0:T(8,128)(2,1)S(1)}) custom-call(bf16[304,512]{1,0:T(8,128)(2,1)S(1)} %get-tuple-element.11.refs_0_.pay1, bf16[304,512]{1,0:T(8,128)(2,1)S(1)} %get-tuple-element.12.refs_1_.refs_2_.pay2, ...), custom_call_target="tpu_custom_call" | custom-call | flops 3000000000 | bytes 4000000 | tf_op jit(solution)/shard_map/inner/pallas_call | solution.py:282
  49.5 0.0 collective-permute-done.3.over2
  49.6 0.0 collective-permute-done.4.corner
  49.6 5.0 %outer.1 = bf16[576,512]{1,0:T(8,128)(2,1)} custom-call(bf16[304,512]{1,0:T(8,128)(2,1)S(1)} %get-tuple-element.11.refs_0_.pay1, bf16[304,512]{1,0:T(8,128)(2,1)S(1)} %get-tuple-element.12.refs_1_.refs_2_.pay2, bf16[304,512]{1,0:T(8,128)(2,1)S(1)} %collective-permute-done.refs_1_.far1, bf16[304,512]{1,0:T(8,128)(2,1)S(1)} %collective-permute-done.1.refs_2_.refs_3_.far2, ...), custom_call_target="tpu_custom_call" | custom-call | flops 1500000000 | bytes 4000000 | tf_op jit(solution)/shard_map/outer/pallas_call | solution.py:282
  (9 shorter events, 0.0 us)
Async XLA Ops:
  0.0 26.4 %copy-start.2 = (f32[1536]{0:T(1024)S(1)}, f32[1536]{0:T(1024)}, u32[]{:S(2)}) copy-start(f32[1536]{0:T(1024)} %b_qkv.5) | copy-start | bytes 18436
  0.0 26.4 %copy-start = (bf16[512,1536]{1,0:T(8,128)(2,1)S(1)}, bf16[512,1536]{1,0:T(8,128)(2,1)}, u32[]{:S(2)}) copy-start(bf16[512,1536]{1,0:T(8,128)(2,1)} %w_qkv.5) | copy-start | bytes 4718596
  0.0 26.4 %copy-start.4 = (f32[512]{0:T(512)S(1)}, f32[512]{0:T(512)}, u32[]{:S(2)}) copy-start(f32[512]{0:T(512)} %bias.5) | copy-start | bytes 6148
  0.0 26.5 %copy-start.3 = (f32[512]{0:T(512)S(1)}, f32[512]{0:T(512)}, u32[]{:S(2)}) copy-start(f32[512]{0:T(512)} %gain.5) | copy-start | bytes 6148
  0.0 1.2 %copy-start.6 = (bf16[2,24,12,512]{3,1,2,0:T(8,128)(2,1)S(1)}, bf16[2,24,12,512]{3,1,2,0:T(8,128)(2,1)}, u32[]{:S(2)}) copy-start(bf16[2,24,12,512]{3,1,2,0:T(8,128)(2,1)} %param.8) | copy-start | bytes 1769476
  1.2 0.7 %copy-start.7 = (s32[2,24,12]{1,0,2:T(2,128)S(1)}, s32[2,24,12]{1,0,2:T(2,128)}, u32[]{:S(2)}) copy-start(s32[2,24,12]{1,0,2:T(2,128)} %param.9) | copy-start | bytes 6916
  2.7 10.7 %collective-permute-start.1 = (bf16[304,512]{1,0:T(8,128)(2,1)S(1)}, bf16[304,512]{1,0:T(8,128)(2,1)S(1)}, u32[]{:S(2)}, u32[]{:S(2)}) collective-permute-start(bf16[304,512]{1,0:T(8,128)(2,1)S(1)} %get-tuple-element.12.refs_1_.refs_2_.pay2), channel_id=1, source_target_pairs={{0,8},{8,0},{16,24},{24,16},{32,40},{40,32},{48,56},{56,48},{64,72... | collective-permute-start | bytes 933896 | tf_op jit(solution)/shard_map/ppermute | solution.py:305
  11.5 16.3 %collective-permute-start = (bf16[304,512]{1,0:T(8,128)(2,1)S(1)}, bf16[304,512]{1,0:T(8,128)(2,1)S(1)}, u32[]{:S(2)}, u32[]{:S(2)}) collective-permute-start(bf16[304,512]{1,0:T(8,128)(2,1)S(1)} %get-tuple-element.11.refs_0_.pay1), channel_id=1, source_target_pairs={{8,16},{16,8},{24,32},{32,24},{40,48},{48,40},{56,64},{64,56},{72,... | collective-permute-start | bytes 933896 | tf_op jit(solution)/shard_map/ppermute | solution.py:305
  13.5 16.9 %collective-permute-start.2 = (bf16[128,512]{1,0:T(8,128)(2,1)S(1)}, bf16[128,512]{1,0:T(8,128)(2,1)S(1)}, u32[]{:S(2)}, u32[]{:S(2)}) collective-permute-start(bf16[128,512]{1,0:T(8,128)(2,1)S(1)} %edge1.1), channel_id=1, source_target_pairs={{1,2},{2,1},{3,4},{4,3},{5,6},{6,5},{7,0},{0,7},{9,10},{10,9},{11,... | collective-permute-start | bytes 393224 | tf_op jit(solution)/shard_map/ppermute | solution.py:305
  27.8 17.9 %copy-start.1 = (bf16[512,512]{1,0:T(8,128)(2,1)S(1)}, bf16[512,512]{1,0:T(8,128)(2,1)}, u32[]{:S(2)}) copy-start(bf16[512,512]{1,0:T(8,128)(2,1)} %w_out.3) | copy-start | bytes 1572868
  27.8 17.9 %copy-start.5 = (f32[512]{0:T(512)S(1)}, f32[512]{0:T(512)}, u32[]{:S(2)}) copy-start(f32[512]{0:T(512)} %b_out.3) | copy-start | bytes 6148
  27.9 21.6 %collective-permute-start.3 = (bf16[176,512]{1,0:T(8,128)(2,1)S(1)}, bf16[176,512]{1,0:T(8,128)(2,1)S(1)}, u32[]{:S(2)}, u32[]{:S(2)}) collective-permute-start(bf16[176,512]{1,0:T(8,128)(2,1)S(1)} %edge2.1), channel_id=1, source_target_pairs={{0,1},{1,0},{2,3},{3,2},{4,5},{5,4},{6,7},{7,6},{8,9},{9,8},{10,11... | collective-permute-start | bytes 540680 | tf_op jit(solution)/shard_map/ppermute | solution.py:305
  30.5 19.0 %collective-permute-start.4 = (bf16[48,512]{1,0:T(8,128)(2,1)S(1)}, bf16[48,512]{1,0:T(8,128)(2,1)S(1)}, u32[]{:S(2)}, u32[]{:S(2)}) collective-permute-start(bf16[48,512]{1,0:T(8,128)(2,1)S(1)} %corner.1), channel_id=1, source_target_pairs={{0,511},{1,2},{2,1},{3,508},{4,507},{5,6},{6,5},{7,504},{8,16},{9,... | collective-permute-start | bytes 147464 | tf_op jit(solution)/shard_map/ppermute | solution.py:323

commit v3 on v2

--- a/solution.py
+++ b/solution.py
@@ -64,7 +64,7 @@
     return pl.multiple_of(l * SIDE + half * (SIDE // 2), SIDE // 2)
 
 
-def prep_kernel(feat, ids, pay1, pay2, qlab, lab):
+def prep_kernel(feat, ids, pay1, pay2, qlab, edge1, bend, lab):
     odd_lon = lax.axis_index("lon") % 2
     odd_lat = lax.axis_index("lat") % 2
     first = lax.axis_index("lat") == 0
@@ -73,20 +73,34 @@
     spread = jnp.where(iota((128, SIDE), 0) == lat, 1.0, 0.0).astype(BF16)
     from_first = jnp.where((iota((LEV, ROWS), 1) < SLAT) & first, 4.0, 0.0)
     lab[...] = jnp.zeros_like(lab)
+    row = iota((HALF, SIDE), 0)
+    edge, edge_line = 0.0, 0.0
     for s, pay in enumerate((pay1, pay2)):
         tokens = jnp.concatenate([feat[pl.ds(side_rows(s, l), SIDE // 2), :] for l in range(LEV)], axis=0)
-        pay[:SIDE, :] = mm(order.astype(BF16), tokens).astype(BF16)
+        ordered = mm(order.astype(BF16), tokens)
+        pay[:SIDE, :] = ordered.astype(BF16)
         half = odd_lon if s == 0 else 1 - odd_lon
         for c in range(SLON):
             lab[s, LEV * c : LEV * (c + 1), :ROWS] = ids[SLON * half + c].astype(F32) + from_first
         line = mm(lab[s].astype(BF16), spread)
         line = jnp.sum(jnp.where(iota((16, SIDE), 0) == strip, line, 0.0), axis=0, keepdims=True)
         qlab[s] = jnp.broadcast_to(jnp.sum(order * line, axis=-1, keepdims=True), (SIDE, 128))
-        line = mm_nt(jnp.broadcast_to(line, (16, SIDE)).astype(BF16), order.astype(BF16))
-        pay[SIDE:, :] = jnp.concatenate([line, jnp.zeros((16, D - SIDE), F32)], axis=1).astype(BF16)
-
-
-def own_kernel(pay1, pay2, gain, bias, w_qkv, b_qkv, qkv):
+        line = jnp.broadcast_to(line, (16, SIDE)).astype(BF16)
+        ordered_line = jnp.concatenate([mm_nt(line, order.astype(BF16)), jnp.zeros((16, D - SIDE), F32)], axis=1)
+        pay[SIDE:, :] = ordered_line.astype(BF16)
+        wanted = jnp.where(row - HALF // 2 * s + 3 * HALF == place, 1.0, 0.0)
+        wanted = jnp.where((row < HALF // 2) if s == 0 else (row >= HALF // 2), wanted, 0.0).astype(BF16)
+        edge = edge + mm(wanted, tokens)
+        edge_line = edge_line + mm_nt(line, wanted)
+        if s == 0:
+            moved = shifted(ordered_line[:8], 3 * HALF, 0)
+            bend[...] = jnp.concatenate([ordered[3 * HALF : 3 * HALF + EDGE], moved], axis=0).astype(BF16)
+    edge_line = jnp.concatenate([edge_line[:8], jnp.zeros((8, D - HALF), F32)], axis=1)
+    edge1[...] = jnp.concatenate([edge, edge_line], axis=0).astype(BF16)
+
+
+def own_kernel(pay1, pay2, gain, bias, w_qkv, b_qkv, after, qkv):
+    del after
     g, b = gain[...].reshape(1, D), bias[...].reshape(1, D)
     for s, pay in enumerate((pay1, pay2)):
         normed = layer_norm(pay[:SIDE, :].astype(F32), g, b)
@@ -151,32 +165,28 @@
     return out
 
 
-def edge_kernel(e, *refs):
-    sides, out = refs[:-1], refs[-1]
-    rows = [edge_piece(ref, e) for ref in sides]
-    line = edge_labels([(label_line(ref, SIDE), 3 * HALF + 32 * e) for ref in sides])
-    rows += [line] * ((out.shape[0] - len(rows) * EDGE) // 8)
-    out[...] = jnp.concatenate(rows, axis=0).astype(BF16)
-
-
-def far_pairs(axis, size):
-    at = lax.axis_index(axis)
-    return (at % size == 0) | (at % size == size - 1)
-
-
-def corner_kernel(pay1, far1, over1, out):
-    lat_far = far_pairs("lat", LAT_RUN)
-    both_far = lat_far & far_pairs("lon", LON_RUN)
-    a, b, c = edge_piece(pay1, 0), edge_piece(far1, 0), over1[...].astype(F32)[:EDGE]
-    la, lb = (shifted(label_line(ref, SIDE), 3 * HALF, 0) for ref in (pay1, far1))
-    lc = label_line(over1, 3 * EDGE)
-    one = jnp.where(both_far, 1.0, 0.0)
-    two = jnp.where(lat_far, 1.0, 0.0)
-
-    def choose(a, b, c):
-        return jnp.where(jnp.full(a.shape, one) > 0.5, a, jnp.where(jnp.full(a.shape, two) > 0.5, c, b))
-
-    out[...] = jnp.concatenate([choose(a, b, c), choose(la, lb, lc)], axis=0).astype(BF16)
+def corner_piece(ref):
+    return jnp.concatenate([edge_piece(ref, 0), shifted(label_line(ref, SIDE), 3 * HALF, 0)], axis=0).astype(BF16)
+
+
+def second_kernel(pay1, far1, pay2, far2, out, bend):
+    refs = (pay1, far1, pay2, far2)
+    rows = [edge_piece(ref, 1) for ref in refs]
+    line = edge_labels([(label_line(ref, SIDE), 3 * HALF + 32) for ref in refs])
+    out[...] = jnp.concatenate([*rows, line, line], axis=0).astype(BF16)
+    bend[...] = corner_piece(far1)
+
+
+def gate_kernel(x, after, out):
+    del after
+    out[...] = x[...]
+
+
+def third_kernel(over1, after, first, second):
+    del after
+    x, line = over1[...].astype(F32), label_line(over1, HALF)
+    for out, at in ((first, 0), (second, 32)):
+        out[...] = jnp.concatenate([x[at : at + EDGE], shifted(line, at, 0)], axis=0).astype(BF16)
 
 
 def inner_kernel(pay1, pay2, far1, far2, qlab, qkv, gain, bias, w_qkv, b_qkv, w_out, b_out, kv_edge, mixed, back, kv):
@@ -213,7 +223,7 @@
     ]
 
 
-def edge_window(e, s, pay, far, over_kv, over_line, qlab, qkv, kv_edge):
+def edge_window(e, s, pay, far, over_kv, over_line, late, qlab, qkv, kv_edge):
     last = BLOCKS - 1
     keys = []
     for c in range(2):
@@ -228,10 +238,8 @@
     piece = lane - 2 * HALF
     piece = jnp.where(piece >= EDGE, piece - EDGE, piece)
     spot = jnp.where(lane < HALF, lane, jnp.where(lane < 2 * HALF, lane - HALF, piece))
-    if e == 0:
-        mine = spot < HALF // 2
-    else:
-        mine = spot >= jnp.where(lane < 2 * HALF, HALF // 2, EDGE - HALF // 2)
+    from_row = jnp.where(lane < 2 * HALF, HALF // 2 * e, EDGE - HALF // 2 if late else 0)
+    mine = (spot >= from_row) & (spot < from_row + HALF // 2)
     k_label = jnp.where(mine, k_label, -1.0)
     at = 32 * e
     q = qkv[s, last, :, :D].astype(F32)[at : at + EDGE]
@@ -239,27 +247,38 @@
     return attention(q, keys[0], keys[1], q_label, k_label)
 
 
+def near_kernel(pay1, pay2, far1, far2, over2, qlab, qkv, kv_edge, gain, bias, w_qkv, b_qkv, out):
+    g, b = gain[...].reshape(1, D), bias[...].reshape(1, D)
+    kv = project_kv(over2[...].astype(F32), g, b, w_qkv, b_qkv)
+    line = label_line(over2, 4 * EDGE)
+    for s, (pay, far) in enumerate(((pay1, far1), (pay2, far2))):
+        part = [k[2 * EDGE * s : 2 * EDGE * (s + 1)] for k in kv]
+        out[s] = edge_window(1, s, pay, far, part, shifted(line, 2 * EDGE * s, 2 * HALF), True, qlab, qkv, kv_edge)
+
+
 def outer_kernel(
-    pay1, pay2, far1, far2, over1, over2, corner, qlab, qkv, kv_edge, mixed, back, gain, bias, w_qkv, b_qkv, w_out, b_out, out
+    pay1, pay2, far1, far2, over1, bend1, bend2, bend3, bend4, near, qlab, qkv, kv_edge, mixed, back, gain, bias, w_qkv, b_qkv, w_out, b_out, out
 ):
     g, b = gain[...].reshape(1, D), bias[...].reshape(1, D)
-    kv1 = project_kv(over1[...].astype(F32), g, b, w_qkv, b_qkv)
-    kv2 = project_kv(over2[...].astype(F32), g, b, w_qkv, b_qkv)
-    kv3 = project_kv(corner[...].astype(F32), g, b, w_qkv, b_qkv)
-    line1, line2 = label_line(over1, 3 * EDGE), label_line(over2, 4 * EDGE)
-    line3 = label_line(corner, EDGE)
+    corner = bend1[...].astype(F32) + bend2[...].astype(F32) + bend3[...].astype(F32)
+    other = bend4[...].astype(F32)
+    kv = project_kv(jnp.concatenate([over1[...].astype(F32), corner, other], axis=0), g, b, w_qkv, b_qkv)
+    line = label_line(over1, HALF)
     lane = iota((8, D), 1)
-    first = jnp.where(lane < 2 * HALF + EDGE, shifted(line1, 0, 2 * HALF), shifted(line3, 0, 2 * HALF + EDGE))
     rest = (qlab, qkv, kv_edge)
-    z0 = edge_window(1, 0, pay1, far1, [k[: 2 * EDGE] for k in kv2], shifted(line2, 0, 2 * HALF), *rest)
-    z1 = edge_window(1, 1, pay2, far2, [k[2 * EDGE : 4 * EDGE] for k in kv2], shifted(line2, 2 * EDGE, 2 * HALF), *rest)
-    a1 = edge_window(0, 1, pay2, far2, [k[EDGE : 3 * EDGE] for k in kv1], shifted(line1, EDGE, 2 * HALF), *rest)
-    a0_kv = [jnp.concatenate([k1[:EDGE], k3[:EDGE]], axis=0) for k1, k3 in zip(kv1, kv3)]
-    a0 = edge_window(0, 0, pay1, far1, a0_kv, first, *rest)
+    at = over1.shape[0]
+    a = []
+    for s, (pay, far, bent) in enumerate(((pay1, far1, corner), (pay2, far2, other))):
+        kv_s = [jnp.concatenate([k[32 * s : 32 * s + EDGE], k[at : at + EDGE]], axis=0) for k in kv]
+        mine, theirs = shifted(line, 32 * s, 2 * HALF), shifted(bent[EDGE:], 0, 2 * HALF + EDGE)
+        line_s = jnp.where(lane < 2 * HALF + EDGE, mine, theirs)
+        a.append(edge_window(0, s, pay, far, kv_s, line_s, s == 1, *rest))
+        at += EDGE + 8
     heads, xs = [], []
-    for pay, a, z in ((pay1, a0, z0), (pay2, a1, z1)):
-        mid = jnp.where(iota((8, 1), 0) < 4, a[32:], z[:8])
-        heads.append(jnp.concatenate([a[:32], mid, z[8:]], axis=0))
+    for s, pay in enumerate((pay1, pay2)):
+        z = near[s]
+        mid = jnp.where(iota((8, 1), 0) < 4, a[s][32:], z[:8])
+        heads.append(jnp.concatenate([a[s][:32], mid, z[8:]], axis=0))
         xs.append(pay[:SIDE, :].astype(F32)[3 * HALF :])
     edges = finish(jnp.concatenate(heads, axis=0), jnp.concatenate(xs, axis=0), w_out[...], b_out[...].reshape(1, D))
     edges = edges.astype(F32)
@@ -295,6 +314,10 @@
     return pltpu.with_memory_space_constraint(x, pltpu.VMEM)
 
 
+def gate(x, after):
+    return held(call(gate_kernel, "gate", [(x.shape, x.dtype)], (held(x), after), 1_000)[0])
+
+
 def pairs(axis, first):
     n = lax.axis_size(axis)
     return [(i, (i + 1) % n) for i in range(first, n, 2)]
@@ -305,21 +328,18 @@
     return held(lax.ppermute(block, axis, route))
 
 
-def swap_corners(block):
+def swap_corners(block, way):
     n_lon, n_lat = lax.axis_size("lon"), lax.axis_size("lat")
     over_lon = {i: j for p in pairs("lon", 1) for i, j in (p, p[::-1])}
     over_lat = {i: j for p in pairs("lat", 1) for i, j in (p, p[::-1])}
     route = []
     for o in range(n_lon):
         for a in range(n_lat):
-            to_o, to_a = o, a
-            if a % LAT_RUN in (0, LAT_RUN - 1):
-                to_o = over_lon[o]
-                if o % LON_RUN in (0, LON_RUN - 1):
-                    to_a = over_lat[a]
-            else:
-                to_a = over_lat[a]
-            route.append((o * n_lat + a, to_o * n_lat + to_a))
+            far_lat = a % LAT_RUN in (0, LAT_RUN - 1)
+            far_lon = o % LON_RUN in (0, LON_RUN - 1)
+            if way == ("direct" if far_lat and far_lon else "lon" if far_lat else "lat"):
+                to = (o if way == "lat" else over_lon[o]) * n_lat + (a if way == "lon" else over_lat[a])
+                route.append((o * n_lat + a, to))
     return held(lax.ppermute(block, ("lon", "lat"), route))
 
 
@@ -329,10 +349,10 @@
     norm = (held(ln_gain), held(ln_bias))
     into = (held(w_qkv), held(b_qkv))
     outof = (held(w_out), held(b_out))
-    pay1, pay2, qlab = call(
+    pay1, pay2, qlab, edge1, bend = call(
         prep_kernel,
         "prep",
-        [((PAY, D), BF16), ((PAY, D), BF16), ((2, SIDE, 128), F32)],
+        [((PAY, D), BF16), ((PAY, D), BF16), ((2, SIDE, 128), F32), ((HALF + 8, D), BF16), ((EDGE + 8, D), BF16)],
         (feat, ids),
         200_000_000,
         [pltpu.VMEM((2, 16, 128), F32)],
@@ -340,15 +360,20 @@
     pay1, pay2, qlab = held(pay1), held(pay2), held(qlab)
     far2 = swap(pay2, "lon", 0)
     far1 = swap(pay1, "lon", 1)
-    (edge1,) = call(
-        functools.partial(edge_kernel, 0), "edge1", [((3 * EDGE + 8, D), BF16)], (pay1, pay2, far2), 1_000_000
-    )
+    edge1 = gate(edge1, far2)
     over1 = swap(edge1, "lat", 1)
-    (qkv,) = call(own_kernel, "own", [((2, BLOCKS, HALF, 3 * D), BF16)], (pay1, pay2, *norm, *into), 900_000_000)
+    bend = gate(bend, edge1)
+    bend1 = swap_corners(bend, "direct")
+    (qkv,) = call(own_kernel, "own", [((2, BLOCKS, HALF, 3 * D), BF16)], (pay1, pay2, *norm, *into, bend), 900_000_000)
     qkv = held(qkv)
-    (edge2,) = call(
-        functools.partial(edge_kernel, 1), "edge2", [((4 * EDGE + 16, D), BF16)], (pay1, far1, pay2, far2), 1_000_000
-    )
+    edge2, bend = call(
+        second_kernel,
+        "edge2",
+        [((4 * EDGE + 16, D), BF16), ((EDGE + 8, D), BF16)],
+        (pay1, far1, pay2, far2),
+        1_000_000,
+    )
+    bend2 = swap_corners(bend, "lat")
     over2 = swap(edge2, "lat", 0)
     kv_edge, mixed, back = call(
         inner_kernel,
@@ -359,13 +384,24 @@
         [pltpu.VMEM((2, SIDE, 2 * D), F32)],
     )
     kv_edge, mixed, back = held(kv_edge), held(mixed), held(back)
-    (bend,) = call(corner_kernel, "corner", [((EDGE + 8, D), BF16)], (pay1, far1, over1), 1_000_000)
-    corner = swap_corners(bend)
+    (near,) = call(
+        near_kernel,
+        "near",
+        [((2, EDGE, D), F32)],
+        (pay1, pay2, far1, far2, over2, qlab, qkv, kv_edge, *norm, *into),
+        1_000_000_000,
+    )
+    bend, other = call(third_kernel, "third", [((EDGE + 8, D), BF16)] * 2, (over1, kv_edge), 1_000_000)
+    bend3 = swap_corners(bend, "lon")
+    bend4 = swap(other, "lon", 0)
     (out,) = call(
         outer_kernel,
         "outer",
         [((2 * SIDE, D), BF16)],
-        (pay1, pay2, far1, far2, over1, over2, corner, qlab, qkv, kv_edge, mixed, back, *norm, *into, *outof),
+        (
+            *(pay1, pay2, far1, far2, over1, bend1, bend2, bend3, bend4, held(near)),
+            *(qlab, qkv, kv_edge, mixed, back, *norm, *into, *outof),
+        ),
         1_500_000_000,
         keep=False,
     )

time: 55.6 us -> 51 us (0.917); the launches traced: 54.6 us -> 50.7 us
  starting transfers between devices: 40.8 us -> 36.9 us
    ppermute x1 -> x3, starting transfers between devices: 15.2 us -> 7.93 us  [swap_corners(): return held(lax.ppermute(block, ('lon', 'lat'), route))]
    ppermute x4 -> x5, starting transfers between devices: 25.6 us -> 28.9 us  [swap(): return held(lax.ppermute(block, axis, route))]
    pallas_call x7 -> x9, Pallas kernels: 11.2 us -> 11.7 us  [call(): pl.pallas_call(kernel, out_shape=[make(shape, dtype) for shape, dtype in...]
  transfers between devices with their start and end apart: 5 -> 8, of which waited for: 1 -> 0; matrix products, arithmetic and copies ran while one was open for 0% -> 0% of each run, Pallas kernels for 10% -> 14%
where the time goes in v3:
time: 51 us; the launch traced here: 50.7 us
  starting transfers between devices  36.9 us (72%)
  Pallas kernels  11.7 us (23%)
  local copies, waits for them, and re-layouts  1.81 us (4%)
    ppermute x5, starting transfers between devices, swap(): return held(lax.ppermute(block, axis, route))  28.9 us
    pallas_call x9, Pallas kernels, call(): pl.pallas_call(kernel, out_shape=[make(shape, dtype) for shape, dtype in...  11.7 us
    ppermute x3, starting transfers between devices, swap_corners(): return held(lax.ppermute(block, ('lon', 'lat'), route))  7.93 us
    unnamed x16, local copies, waits for them, and re-layouts  1.81 us
  transfers between devices with their start and end apart: 8, of which 0 were waited for; matrix products, arithmetic and copies ran while one was open for 0% of the time, Pallas kernels for 14%

profile of v3, /device:TPU:1, one launch (start us, length us, event | category | flops | bytes accessed | tf_op | source)
XLA Modules:
  0.0 50.7 jit_solution(4321640252882113510)
XLA Ops:
  0.0 1.1 %copy-done.6 = bf16[2,24,12,512]{3,1,2,0:T(8,128)(2,1)S(1)} copy-done((bf16[2,24,12,512]{3,1,2,0:T(8,128)(2,1)S(1)}, bf16[2,24,12,512]{3,1,2,0:T(8,128)(2,1)}, u32[]{:S(2)}) %copy-start.6) | copy-done | bytes 589848
  1.1 0.7 %copy-done.7 = s32[2,24,12]{1,0,2:T(2,128)S(1)} copy-done((s32[2,24,12]{1,0,2:T(2,128)S(1)}, s32[2,24,12]{1,0,2:T(2,128)}, u32[]{:S(2)}) %copy-start.7) | copy-done | bytes 2328
  1.8 1.0 %prep.1 = (bf16[304,512]{1,0:T(8,128)(2,1)S(1)}, bf16[304,512]{1,0:T(8,128)(2,1)S(1)}, f32[2,288,128]{2,1,0:T(8,128)S(1)}, bf16[80,512]{1,0:T(8,128)(2,1)S(1)}, bf16[48,512]{1,0:T(8,128)(2,1)S(1)}) custom-call(bf16[576,512]{1,0:T(8,128)(2,1)S(1)} %bitcast.7, s32[12,2,24]{2,1,0:T(2,128)S(1)} %bitcast.8), custom_call_target="tpu_custom_call" | custom-call | flops 200000000 | bytes 4000000 | tf_op jit(solution)/shard_map/prep/pallas_call | solution.py:301
  2.8 0.0 copy-start
  2.8 0.0 copy-start.2
  2.8 0.0 copy-start.3
  2.9 0.0 copy-start.4
  2.9 8.9 %collective-permute-start.1 = (bf16[304,512]{1,0:T(8,128)(2,1)S(1)}, bf16[304,512]{1,0:T(8,128)(2,1)S(1)}, u32[]{:S(2)}, u32[]{:S(2)}) collective-permute-start(bf16[304,512]{1,0:T(8,128)(2,1)S(1)} %get-tuple-element.18.pay2), channel_id=1, source_target_pairs={{0,8},{8,0},{16,24},{24,16},{32,40},{40,32},{48,56},{56,48},{64,72... | collective-permute-start | bytes 933896 | tf_op jit(solution)/shard_map/ppermute | solution.py:328
  11.8 1.9 %collective-permute-start = (bf16[304,512]{1,0:T(8,128)(2,1)S(1)}, bf16[304,512]{1,0:T(8,128)(2,1)S(1)}, u32[]{:S(2)}, u32[]{:S(2)}) collective-permute-start(bf16[304,512]{1,0:T(8,128)(2,1)S(1)} %get-tuple-element.17.pay1), channel_id=1, source_target_pairs={{8,16},{16,8},{24,32},{32,24},{40,48},{48,40},{56,64},{64,56},{72,... | collective-permute-start | bytes 933896 | tf_op jit(solution)/shard_map/ppermute | solution.py:328
  13.7 12.9 %collective-permute-start.2 = (bf16[80,512]{1,0:T(8,128)(2,1)S(1)}, bf16[80,512]{1,0:T(8,128)(2,1)S(1)}, u32[]{:S(2)}, u32[]{:S(2)}) collective-permute-start(bf16[80,512]{1,0:T(8,128)(2,1)S(1)} %gate.2.after), channel_id=1, source_target_pairs={{1,2},{2,1},{3,4},{4,3},{5,6},{6,5},{7,0},{0,7},{9,10},{10,9},{11,... | collective-permute-start | bytes 245768 | tf_op jit(solution)/shard_map/ppermute | solution.py:328
  26.7 0.7 %collective-permute-start.3 = (bf16[48,512]{1,0:T(8,128)(2,1)S(1)}, bf16[48,512]{1,0:T(8,128)(2,1)S(1)}, u32[]{:S(2)}, u32[]{:S(2)}) collective-permute-start(bf16[48,512]{1,0:T(8,128)(2,1)S(1)} %gate.3.after), channel_id=1, source_target_pairs={{0,511},{3,508},{4,507},{7,504},{120,135},{123,132},{124,131},{127... | collective-permute-start | bytes 147464 | tf_op jit(solution)/shard_map/ppermute | solution.py:343
  27.3 0.0 collective-permute-done.far1
  27.3 0.1 edge2.1
  27.4 0.7 %collective-permute-start.4 = (bf16[48,512]{1,0:T(8,128)(2,1)S(1)}, bf16[48,512]{1,0:T(8,128)(2,1)S(1)}, u32[]{:S(2)}, u32[]{:S(2)}) collective-permute-start(bf16[48,512]{1,0:T(8,128)(2,1)S(1)} %get-tuple-element.21), channel_id=1, source_target_pairs={{1,2},{2,1},{5,6},{6,5},{9,10},{10,9},{13,14},{14,13},{17,18},{18,... | collective-permute-start | bytes 147464 | tf_op jit(solution)/shard_map/ppermute | solution.py:343
  28.1 0.0 copy-start.1
  28.1 0.0 copy-start.5
  28.1 2.1 %collective-permute-start.7 = (bf16[176,512]{1,0:T(8,128)(2,1)S(1)}, bf16[176,512]{1,0:T(8,128)(2,1)S(1)}, u32[]{:S(2)}, u32[]{:S(2)}) collective-permute-start(bf16[176,512]{1,0:T(8,128)(2,1)S(1)} %get-tuple-element.26), channel_id=1, source_target_pairs={{0,1},{1,0},{2,3},{3,2},{4,5},{5,4},{6,7},{7,6},{8,9},{9,8},{10,11... | collective-permute-start | bytes 540680 | tf_op jit(solution)/shard_map/ppermute | solution.py:328
  30.2 1.3 %own.1.qkv = bf16[2,4,72,1536]{3,2,1,0:T(8,128)(2,1)S(1)} custom-call(bf16[304,512]{1,0:T(8,128)(2,1)S(1)} %get-tuple-element.17.pay1, bf16[304,512]{1,0:T(8,128)(2,1)S(1)} %get-tuple-element.18.pay2, f32[512]{0:T(512)S(1)} %copy-done.3, f32[512]{0:T(512)S(1)} %copy-done.4, bf16[512,1536]{1,0:T(8,128)(2,1)S(1)} %copy-done, f32[1536]{0:T(1024)S(1)} %copy-done.2, ...), custom_call_target="tpu_custom_call" | custom-call | flops 900000000 | bytes 4000000 | tf_op jit(solution)/shard_map/own/pallas_call | solution.py:301
  31.6 3.8 %inner.1 = (bf16[2,72,1024]{2,1,0:T(8,128)(2,1)S(1)}, bf16[2,3,72,512]{3,2,1,0:T(8,128)(2,1)S(1)}, bf16[288,288]{1,0:T(8,128)(2,1)S(1)}) custom-call(bf16[304,512]{1,0:T(8,128)(2,1)S(1)} %get-tuple-element.17.pay1, bf16[304,512]{1,0:T(8,128)(2,1)S(1)} %get-tuple-element.18.pay2, bf16[304,512]{1,0:T(8,128)(2,1)S(1)} %collective-permute-done.far1, ...), custom_call_target="tpu_custom_call" | custom-call | flops 3000000000 | bytes 4000000 | tf_op jit(solution)/shard_map/inner/pallas_call | solution.py:301
  35.4 0.1 third.1
  35.5 6.6 %collective-permute-start.5 = (bf16[48,512]{1,0:T(8,128)(2,1)S(1)}, bf16[48,512]{1,0:T(8,128)(2,1)S(1)}, u32[]{:S(2)}, u32[]{:S(2)}) collective-permute-start(bf16[48,512]{1,0:T(8,128)(2,1)S(1)} %get-tuple-element.24), channel_id=1, source_target_pairs={{8,16},{11,19},{12,20},{15,23},{16,8},{19,11},{20,12},{23,15},{24,... | collective-permute-start | bytes 147464 | tf_op jit(solution)/shard_map/ppermute | solution.py:343
  42.1 3.2 %collective-permute-start.6 = (bf16[48,512]{1,0:T(8,128)(2,1)S(1)}, bf16[48,512]{1,0:T(8,128)(2,1)S(1)}, u32[]{:S(2)}, u32[]{:S(2)}) collective-permute-start(bf16[48,512]{1,0:T(8,128)(2,1)S(1)} %get-tuple-element.25), channel_id=1, source_target_pairs={{0,8},{8,0},{16,24},{24,16},{32,40},{40,32},{48,56},{56,48},{64,72... | collective-permute-start | bytes 147464 | tf_op jit(solution)/shard_map/ppermute | solution.py:328
  45.3 2.0 %near.1 = f32[2,40,512]{2,1,0:T(8,128)S(1)} custom-call(bf16[304,512]{1,0:T(8,128)(2,1)S(1)} %get-tuple-element.17.pay1, bf16[304,512]{1,0:T(8,128)(2,1)S(1)} %get-tuple-element.18.pay2, bf16[304,512]{1,0:T(8,128)(2,1)S(1)} %collective-permute-done.far1, bf16[304,512]{1,0:T(8,128)(2,1)S(1)} %collective-permute-done.1.after.far2, ...), custom_call_target="tpu_custom_call" | custom-call | flops 1000000000 | bytes 4000000 | tf_op jit(solution)/shard_map/near/pallas_call | solution.py:301
  47.3 3.3 %outer.1 = bf16[576,512]{1,0:T(8,128)(2,1)} custom-call(bf16[304,512]{1,0:T(8,128)(2,1)S(1)} %get-tuple-element.17.pay1, bf16[304,512]{1,0:T(8,128)(2,1)S(1)} %get-tuple-element.18.pay2, bf16[304,512]{1,0:T(8,128)(2,1)S(1)} %collective-permute-done.far1, bf16[304,512]{1,0:T(8,128)(2,1)S(1)} %collective-permute-done.1.after.far2, ...), custom_call_target="tpu_custom_call" | custom-call | flops 1500000000 | bytes 4000000 | tf_op jit(solution)/shard_map/outer/pallas_call | solution.py:301
  (17 shorter events, 0.0 us)
Async XLA Ops:
  0.0 1.1 %copy-start.6 = (bf16[2,24,12,512]{3,1,2,0:T(8,128)(2,1)S(1)}, bf16[2,24,12,512]{3,1,2,0:T(8,128)(2,1)}, u32[]{:S(2)}) copy-start(bf16[2,24,12,512]{3,1,2,0:T(8,128)(2,1)} %param.8) | copy-start | bytes 1769476
  1.1 0.7 %copy-start.7 = (s32[2,24,12]{1,0,2:T(2,128)S(1)}, s32[2,24,12]{1,0,2:T(2,128)}, u32[]{:S(2)}) copy-start(s32[2,24,12]{1,0,2:T(2,128)} %param.9) | copy-start | bytes 6916
  2.8 27.4 %copy-start = (bf16[512,1536]{1,0:T(8,128)(2,1)S(1)}, bf16[512,1536]{1,0:T(8,128)(2,1)}, u32[]{:S(2)}) copy-start(bf16[512,1536]{1,0:T(8,128)(2,1)} %w_qkv.7) | copy-start | bytes 4718596
  2.8 27.4 %copy-start.2 = (f32[1536]{0:T(1024)S(1)}, f32[1536]{0:T(1024)}, u32[]{:S(2)}) copy-start(f32[1536]{0:T(1024)} %b_qkv.7) | copy-start | bytes 18436
  2.8 27.3 %copy-start.3 = (f32[512]{0:T(512)S(1)}, f32[512]{0:T(512)}, u32[]{:S(2)}) copy-start(f32[512]{0:T(512)} %gain.7) | copy-start | bytes 6148
  2.9 27.3 %copy-start.4 = (f32[512]{0:T(512)S(1)}, f32[512]{0:T(512)}, u32[]{:S(2)}) copy-start(f32[512]{0:T(512)} %bias.7) | copy-start | bytes 6148
  2.9 10.9 %collective-permute-start.1 = (bf16[304,512]{1,0:T(8,128)(2,1)S(1)}, bf16[304,512]{1,0:T(8,128)(2,1)S(1)}, u32[]{:S(2)}, u32[]{:S(2)}) collective-permute-start(bf16[304,512]{1,0:T(8,128)(2,1)S(1)} %get-tuple-element.18.pay2), channel_id=1, source_target_pairs={{0,8},{8,0},{16,24},{24,16},{32,40},{40,32},{48,56},{56,48},{64,72... | collective-permute-start | bytes 933896 | tf_op jit(solution)/shard_map/ppermute | solution.py:328
  11.8 15.5 %collective-permute-start = (bf16[304,512]{1,0:T(8,128)(2,1)S(1)}, bf16[304,512]{1,0:T(8,128)(2,1)S(1)}, u32[]{:S(2)}, u32[]{:S(2)}) collective-permute-start(bf16[304,512]{1,0:T(8,128)(2,1)S(1)} %get-tuple-element.17.pay1), channel_id=1, source_target_pairs={{8,16},{16,8},{24,32},{32,24},{40,48},{48,40},{56,64},{64,56},{72,... | collective-permute-start | bytes 933896 | tf_op jit(solution)/shard_map/ppermute | solution.py:328
  13.7 21.6 %collective-permute-start.2 = (bf16[80,512]{1,0:T(8,128)(2,1)S(1)}, bf16[80,512]{1,0:T(8,128)(2,1)S(1)}, u32[]{:S(2)}, u32[]{:S(2)}) collective-permute-start(bf16[80,512]{1,0:T(8,128)(2,1)S(1)} %gate.2.after), channel_id=1, source_target_pairs={{1,2},{2,1},{3,4},{4,3},{5,6},{6,5},{7,0},{0,7},{9,10},{10,9},{11,... | collective-permute-start | bytes 245768 | tf_op jit(solution)/shard_map/ppermute | solution.py:328
  26.7 20.6 %collective-permute-start.3 = (bf16[48,512]{1,0:T(8,128)(2,1)S(1)}, bf16[48,512]{1,0:T(8,128)(2,1)S(1)}, u32[]{:S(2)}, u32[]{:S(2)}) collective-permute-start(bf16[48,512]{1,0:T(8,128)(2,1)S(1)} %gate.3.after), channel_id=1, source_target_pairs={{0,511},{3,508},{4,507},{7,504},{120,135},{123,132},{124,131},{127... | collective-permute-start | bytes 147464 | tf_op jit(solution)/shard_map/ppermute | solution.py:343
  27.4 19.9 %collective-permute-start.4 = (bf16[48,512]{1,0:T(8,128)(2,1)S(1)}, bf16[48,512]{1,0:T(8,128)(2,1)S(1)}, u32[]{:S(2)}, u32[]{:S(2)}) collective-permute-start(bf16[48,512]{1,0:T(8,128)(2,1)S(1)} %get-tuple-element.21), channel_id=1, source_target_pairs={{1,2},{2,1},{5,6},{6,5},{9,10},{10,9},{13,14},{14,13},{17,18},{18,... | collective-permute-start | bytes 147464 | tf_op jit(solution)/shard_map/ppermute | solution.py:343
  28.1 3.4 %copy-start.1 = (bf16[512,512]{1,0:T(8,128)(2,1)S(1)}, bf16[512,512]{1,0:T(8,128)(2,1)}, u32[]{:S(2)}) copy-start(bf16[512,512]{1,0:T(8,128)(2,1)} %w_out.3) | copy-start | bytes 1572868
  28.1 3.4 %copy-start.5 = (f32[512]{0:T(512)S(1)}, f32[512]{0:T(512)}, u32[]{:S(2)}) copy-start(f32[512]{0:T(512)} %b_out.3) | copy-start | bytes 6148
  28.1 17.2 %collective-permute-start.7 = (bf16[176,512]{1,0:T(8,128)(2,1)S(1)}, bf16[176,512]{1,0:T(8,128)(2,1)S(1)}, u32[]{:S(2)}, u32[]{:S(2)}) collective-permute-start(bf16[176,512]{1,0:T(8,128)(2,1)S(1)} %get-tuple-element.26), channel_id=1, source_target_pairs={{0,1},{1,0},{2,3},{3,2},{4,5},{5,4},{6,7},{7,6},{8,9},{9,8},{10,11... | collective-permute-start | bytes 540680 | tf_op jit(solution)/shard_map/ppermute | solution.py:328
  35.5 11.8 %collective-permute-start.5 = (bf16[48,512]{1,0:T(8,128)(2,1)S(1)}, bf16[48,512]{1,0:T(8,128)(2,1)S(1)}, u32[]{:S(2)}, u32[]{:S(2)}) collective-permute-start(bf16[48,512]{1,0:T(8,128)(2,1)S(1)} %get-tuple-element.24), channel_id=1, source_target_pairs={{8,16},{11,19},{12,20},{15,23},{16,8},{19,11},{20,12},{23,15},{24,... | collective-permute-start | bytes 147464 | tf_op jit(solution)/shard_map/ppermute | solution.py:343
  42.1 5.2 %collective-permute-start.6 = (bf16[48,512]{1,0:T(8,128)(2,1)S(1)}, bf16[48,512]{1,0:T(8,128)(2,1)S(1)}, u32[]{:S(2)}, u32[]{:S(2)}) collective-permute-start(bf16[48,512]{1,0:T(8,128)(2,1)S(1)} %get-tuple-element.25), channel_id=1, source_target_pairs={{0,8},{8,0},{16,24},{24,16},{32,40},{40,32},{48,56},{56,48},{64,72... | collective-permute-start | bytes 147464 | tf_op jit(solution)/shard_map/ppermute | solution.py:328

commit v4 on v3

--- a/solution.py
+++ b/solution.py
@@ -64,7 +64,11 @@
     return pl.multiple_of(l * SIDE + half * (SIDE // 2), SIDE // 2)
 
 
-def prep_kernel(feat, ids, pay1, pay2, qlab, edge1, bend, lab):
+def prep_kernel(*refs):
+    refs, (pay1, pay2, qlab, edge1, bend), weights, (lab, feat, ids, sem) = refs[:8], refs[8:13], refs[13:19], refs[19:]
+    copies = [pltpu.make_async_copy(a, b, sem.at[i]) for i, (a, b) in enumerate(zip(refs, (feat, ids, *weights)))]
+    for copy in copies:
+        copy.start()
     odd_lon = lax.axis_index("lon") % 2
     odd_lat = lax.axis_index("lat") % 2
     first = lax.axis_index("lat") == 0
@@ -75,6 +79,8 @@
     lab[...] = jnp.zeros_like(lab)
     row = iota((HALF, SIDE), 0)
     edge, edge_line = 0.0, 0.0
+    for copy in copies[:2]:
+        copy.wait()
     for s, pay in enumerate((pay1, pay2)):
         tokens = jnp.concatenate([feat[pl.ds(side_rows(s, l), SIDE // 2), :] for l in range(LEV)], axis=0)
         ordered = mm(order.astype(BF16), tokens)
@@ -97,10 +103,11 @@
             bend[...] = jnp.concatenate([ordered[3 * HALF : 3 * HALF + EDGE], moved], axis=0).astype(BF16)
     edge_line = jnp.concatenate([edge_line[:8], jnp.zeros((8, D - HALF), F32)], axis=1)
     edge1[...] = jnp.concatenate([edge, edge_line], axis=0).astype(BF16)
-
-
-def own_kernel(pay1, pay2, gain, bias, w_qkv, b_qkv, after, qkv):
-    del after
+    for copy in copies[2:]:
+        copy.wait()
+
+
+def own_part(pay1, pay2, gain, bias, w_qkv, b_qkv, qkv, back):
     g, b = gain[...].reshape(1, D), bias[...].reshape(1, D)
     for s, pay in enumerate((pay1, pay2)):
         normed = layer_norm(pay[:SIDE, :].astype(F32), g, b)
@@ -112,6 +119,28 @@
                 part = part * HS ** (-0.5)
             for m in range(BLOCKS):
                 qkv[s, m, :, cols] = part[m * HALF : (m + 1) * HALF].astype(BF16)
+    place, _, _ = place_of(iota((SIDE, 1), 0), lax.axis_index("lat") % 2)
+    back[...] = jnp.where(iota((SIDE, SIDE), 1) == place, 1.0, 0.0).astype(BF16)
+
+
+def soon():
+    return (lax.axis_index("lat") < LAT_RUN) & (lax.axis_index("lon") % LON_RUN < 6)
+
+
+def ahead_kernel(pay1, pay2, *refs):
+    qkv, back, _, _ = refs[-4:]
+
+    @pl.when(soon())
+    def _():
+        own_part(pay1, pay2, *refs[:-4], qkv, back)
+
+
+def own_kernel(pay1, pay2, gain, bias, w_qkv, b_qkv, after, qkv_in, back_in, qkv, back):
+    del after, qkv_in, back_in
+
+    @pl.when(jnp.logical_not(soon()))
+    def _():
+        own_part(pay1, pay2, gain, bias, w_qkv, b_qkv, qkv, back)
 
 
 def label_line(ref, at):
@@ -135,14 +164,14 @@
         qg = q[:, cols]
         stacked = jnp.concatenate([jnp.where(o, qg, 0.0) for o in own], axis=0).astype(BF16)
         scores = mm_nt(stacked, k[:, cols])
-        scores = jnp.where(allowed[None], scores.reshape(4, n, keys), -1e30)
-        top = jnp.max(scores, axis=-1, keepdims=True)
-        expd = jnp.exp(scores - top)
-        weights = (expd / jnp.sum(expd, axis=-1, keepdims=True)).astype(BF16)
-        full = mm(weights.reshape(4 * n, keys), v[:, cols])
-        picked = jnp.where(own[0], full[:n], 0.0)
+        scores = jnp.where(allowed[None], scores.reshape(4, n, keys), -1e30).reshape(4 * n, keys)
+        expd = jnp.exp(scores - jnp.max(scores, axis=-1, keepdims=True))
+        full = mm(expd.astype(BF16), v[:, cols])
+        share = 1.0 / jnp.sum(expd, axis=-1, keepdims=True)
+        picked = full[:n] * share[:n]
         for h in range(1, 4):
-            picked = jnp.where(own[h], full[h * n : (h + 1) * n], picked)
+            rows = slice(h * n, (h + 1) * n)
+            picked = jnp.where(own[h], full[rows] * share[rows], picked)
         out.append(picked)
     return jnp.concatenate(out, axis=1)
 
@@ -189,7 +218,7 @@
         out[...] = jnp.concatenate([x[at : at + EDGE], shifted(line, at, 0)], axis=0).astype(BF16)
 
 
-def inner_kernel(pay1, pay2, far1, far2, qlab, qkv, gain, bias, w_qkv, b_qkv, w_out, b_out, kv_edge, mixed, back, kv):
+def inner_kernel(pay1, pay2, far1, far2, qlab, qkv, gain, bias, w_qkv, b_qkv, w_out, b_out, kv_edge, mixed, kv):
     g, b = gain[...].reshape(1, D), bias[...].reshape(1, D)
     for s, far in enumerate((far1, far2)):
         normed = layer_norm(far[:SIDE, :].astype(F32), g, b)
@@ -198,8 +227,6 @@
             part = mm(normed, w_qkv[:, cols]) + b_qkv[cols].reshape(1, D)
             kv[s, :, c * D : (c + 1) * D] = part
             kv_edge[s, :, c * D : (c + 1) * D] = part[3 * HALF :].astype(BF16)
-    place, _, _ = place_of(iota((SIDE, 1), 0), lax.axis_index("lat") % 2)
-    back[...] = jnp.where(iota((SIDE, SIDE), 1) == place, 1.0, 0.0).astype(BF16)
     for m in range(BLOCKS - 1):
         rows = slice(m * HALF, (m + 1) * HALF)
         heads, xs = [], []
@@ -296,14 +323,15 @@
     return pl.CostEstimate(flops=flops, bytes_accessed=moved, transcendentals=exps)
 
 
-def call(kernel, name, outs, args, flops, scratch=(), keep=True):
+def call(kernel, name, outs, args, flops, scratch=(), keep=True, spec=VMEM, aliases=()):
     make = pltpu.VMEM if keep else jax.ShapeDtypeStruct
     return pl.pallas_call(
         kernel,
         out_shape=[make(shape, dtype) for shape, dtype in outs],
-        in_specs=[VMEM] * len(args),
+        in_specs=[spec] * len(args),
         out_specs=[VMEM] * len(outs),
         scratch_shapes=list(scratch),
+        input_output_aliases=dict(aliases),
         compiler_params=pltpu.CompilerParams(vmem_limit_bytes=LIMIT),
         cost_estimate=cost(flops, 4_000_000, 500_000),
         name=name,
@@ -346,16 +374,34 @@
 def local(features, region_ids, ln_gain, ln_bias, w_qkv, b_qkv, w_out, b_out):
     feat = features.transpose(0, 2, 1, 3).reshape(2 * SIDE, D)
     ids = region_ids.transpose(2, 0, 1)
-    norm = (held(ln_gain), held(ln_bias))
-    into = (held(w_qkv), held(b_qkv))
-    outof = (held(w_out), held(b_out))
-    pay1, pay2, qlab, edge1, bend = call(
+    weights = (ln_gain, ln_bias, w_qkv, b_qkv, w_out, b_out)
+    pay1, pay2, qlab, edge1, bend, *weights = call(
         prep_kernel,
         "prep",
-        [((PAY, D), BF16), ((PAY, D), BF16), ((2, SIDE, 128), F32), ((HALF + 8, D), BF16), ((EDGE + 8, D), BF16)],
-        (feat, ids),
+        [
+            *[((PAY, D), BF16), ((PAY, D), BF16), ((2, SIDE, 128), F32), ((HALF + 8, D), BF16), ((EDGE + 8, D), BF16)],
+            *[(w.shape, w.dtype) for w in weights],
+        ],
+        [pltpu.with_memory_space_constraint(x, pltpu.HBM) for x in (feat, ids, *weights)],
         200_000_000,
-        [pltpu.VMEM((2, 16, 128), F32)],
+        [
+            pltpu.VMEM((2, 16, 128), F32),
+            pltpu.VMEM(feat.shape, BF16),
+            pltpu.VMEM(ids.shape, jnp.int32),
+            pltpu.SemaphoreType.DMA((8,)),
+        ],
+        spec=pl.BlockSpec(memory_space=pl.ANY),
+    )
+    weights = [held(w) for w in weights]
+    norm, into, outof = weights[:2], weights[2:4], weights[4:]
+    qkv_back = [((2, BLOCKS, HALF, 3 * D), BF16), ((SIDE, SIDE), BF16)]
+    qkv, back, pay1, pay2 = call(
+        ahead_kernel,
+        "ahead",
+        [*qkv_back, ((PAY, D), BF16), ((PAY, D), BF16)],
+        (held(pay1), held(pay2), *norm, *into),
+        900_000_000,
+        aliases={0: 2, 1: 3},
     )
     pay1, pay2, qlab = held(pay1), held(pay2), held(qlab)
     far2 = swap(pay2, "lon", 0)
@@ -364,8 +410,9 @@
     over1 = swap(edge1, "lat", 1)
     bend = gate(bend, edge1)
     bend1 = swap_corners(bend, "direct")
-    (qkv,) = call(own_kernel, "own", [((2, BLOCKS, HALF, 3 * D), BF16)], (pay1, pay2, *norm, *into, bend), 900_000_000)
-    qkv = held(qkv)
+    args = (pay1, pay2, *norm, *into, far1, held(qkv), held(back))
+    qkv, back = call(own_kernel, "own", qkv_back, args, 900_000_000, aliases={7: 0, 8: 1})
+    qkv, back = held(qkv), held(back)
     edge2, bend = call(
         second_kernel,
         "edge2",
@@ -375,15 +422,15 @@
     )
     bend2 = swap_corners(bend, "lat")
     over2 = swap(edge2, "lat", 0)
-    kv_edge, mixed, back = call(
+    kv_edge, mixed = call(
         inner_kernel,
         "inner",
-        [((2, HALF, 2 * D), BF16), ((2, BLOCKS - 1, HALF, D), BF16), ((SIDE, SIDE), BF16)],
+        [((2, HALF, 2 * D), BF16), ((2, BLOCKS - 1, HALF, D), BF16)],
         (pay1, pay2, far1, far2, qlab, qkv, *norm, *into, *outof),
         3_000_000_000,
         [pltpu.VMEM((2, SIDE, 2 * D), F32)],
     )
-    kv_edge, mixed, back = held(kv_edge), held(mixed), held(back)
+    kv_edge, mixed = held(kv_edge), held(mixed)
     (near,) = call(
         near_kernel,
         "near",

time: 51 us -> 48.3 us (0.947)
  local copies, waits for them, and re-layouts: 1.81 us -> 0 us
  starting transfers between devices: 36.9 us -> 36.2 us
    ppermute x5, starting transfers between devices: 28.9 us -> 26.2 us  [swap(): return held(lax.ppermute(block, axis, route))]
    ppermute x3, starting transfers between devices: 7.93 us -> 10 us  [swap_corners(): return held(lax.ppermute(block, ('lon', 'lat'), route))]
    unnamed x16 -> x0, local copies, waits for them, and re-layouts: 1.81 us -> none
    pallas_call x9 -> x10, Pallas kernels: 11.7 us -> 11.6 us  [call(): pl.pallas_call(kernel, out_shape=[make(shape, dtype) for shape, dtype in...]
  transfers between devices with their start and end apart: 8 -> 8, of which waited for: 0 -> 0; matrix products, arithmetic and copies ran while one was open for 0% -> 0% of each run, Pallas kernels for 14% -> 11%
where the time goes in v4:
time: 48.3 us; the launch traced here: 48 us
  starting transfers between devices  36.2 us (75%)
  Pallas kernels  11.6 us (24%)
    ppermute x5, starting transfers between devices, swap(): return held(lax.ppermute(block, axis, route))  26.2 us
    pallas_call x10, Pallas kernels, call(): pl.pallas_call(kernel, out_shape=[make(shape, dtype) for shape, dtype in...  11.6 us
    ppermute x3, starting transfers between devices, swap_corners(): return held(lax.ppermute(block, ('lon', 'lat'), route))  10 us
  transfers between devices with their start and end apart: 8, of which 0 were waited for; matrix products, arithmetic and copies ran while one was open for 0% of the time, Pallas kernels for 11%

profile of v4, /device:TPU:1, one launch (start us, length us, event | category | flops | bytes accessed | tf_op | source)
XLA Modules:
  0.0 48.0 jit_solution(53183856741134402)
XLA Ops:
  0.0 2.2 %prep.1 = (bf16[304,512]{1,0:T(8,128)(2,1)S(1)}, bf16[304,512]{1,0:T(8,128)(2,1)S(1)}, f32[2,288,128]{2,1,0:T(8,128)S(1)}, bf16[80,512]{1,0:T(8,128)(2,1)S(1)}, ...) custom-call(bf16[576,512]{1,0:T(8,128)(2,1)} %bitcast.7, ...), custom_call_target="tpu_custom_call" | custom-call | flops 200000000 | bytes 4000000 | tf_op jit(solution)/shard_map/prep/pallas_call | solution.py:328
  2.2 1.5 %ahead.1 = (bf16[2,4,72,1536]{3,2,1,0:T(8,128)(2,1)S(1)}, bf16[288,288]{1,0:T(8,128)(2,1)S(1)}, bf16[304,512]{1,0:T(8,128)(2,1)S(1)}, bf16[304,512]{1,0:T(8,128)(2,1)S(1)}) custom-call(bf16[304,512]{1,0:T(8,128)(2,1)S(1)} %get-tuple-element.28.pay1, bf16[304,512]{1,0:T(8,128)(2,1)S(1)} %get-tuple-element.29.pay2, ...), custom_call_target="tpu_custom_call", output_to_operand_aliasing={{2}: (0, {}), {3}: (1, {})} | custom-call | flops 900000000 | bytes 4000000 | tf_op jit(solution)/shard_map/ahead/pallas_call | solution.py:328
  3.6 8.8 %collective-permute-start.1 = (bf16[304,512]{1,0:T(8,128)(2,1)S(1)}, bf16[304,512]{1,0:T(8,128)(2,1)S(1)}, u32[]{:S(2)}, u32[]{:S(2)}) collective-permute-start(bf16[304,512]{1,0:T(8,128)(2,1)S(1)} %get-tuple-element.35.pay2), channel_id=1, source_target_pairs={{0,8},{8,0},{16,24},{24,16},{32,40},{40,32},{48,56},{56,48},{64,72... | collective-permute-start | bytes 933896 | tf_op jit(solution)/shard_map/ppermute | solution.py:356
  12.4 1.9 %collective-permute-start = (bf16[304,512]{1,0:T(8,128)(2,1)S(1)}, bf16[304,512]{1,0:T(8,128)(2,1)S(1)}, u32[]{:S(2)}, u32[]{:S(2)}) collective-permute-start(bf16[304,512]{1,0:T(8,128)(2,1)S(1)} %get-tuple-element.34.pay1), channel_id=1, source_target_pairs={{8,16},{16,8},{24,32},{32,24},{40,48},{48,40},{56,64},{64,56},{72,... | collective-permute-start | bytes 933896 | tf_op jit(solution)/shard_map/ppermute | solution.py:356
  14.4 0.0 collective-permute-done.1.after.far2
  14.4 11.4 %collective-permute-start.2 = (bf16[80,512]{1,0:T(8,128)(2,1)S(1)}, bf16[80,512]{1,0:T(8,128)(2,1)S(1)}, u32[]{:S(2)}, u32[]{:S(2)}) collective-permute-start(bf16[80,512]{1,0:T(8,128)(2,1)S(1)} %gate.2.after), channel_id=1, source_target_pairs={{1,2},{2,1},{3,4},{4,3},{5,6},{6,5},{7,0},{0,7},{9,10},{10,9},{11,... | collective-permute-start | bytes 245768 | tf_op jit(solution)/shard_map/ppermute | solution.py:356
  25.9 0.7 %collective-permute-start.3 = (bf16[48,512]{1,0:T(8,128)(2,1)S(1)}, bf16[48,512]{1,0:T(8,128)(2,1)S(1)}, u32[]{:S(2)}, u32[]{:S(2)}) collective-permute-start(bf16[48,512]{1,0:T(8,128)(2,1)S(1)} %gate.3), channel_id=1, source_target_pairs={{0,511},{3,508},{4,507},{7,504},{120,135},{123,132},{124,131},{127... | collective-permute-start | bytes 147464 | tf_op jit(solution)/shard_map/ppermute | solution.py:371
  26.5 0.0 collective-permute-done.far1.after
  26.5 0.1 edge2.1
  26.6 0.7 %collective-permute-start.4 = (bf16[48,512]{1,0:T(8,128)(2,1)S(1)}, bf16[48,512]{1,0:T(8,128)(2,1)S(1)}, u32[]{:S(2)}, u32[]{:S(2)}) collective-permute-start(bf16[48,512]{1,0:T(8,128)(2,1)S(1)} %get-tuple-element.38), channel_id=1, source_target_pairs={{1,2},{2,1},{5,6},{6,5},{9,10},{10,9},{13,14},{14,13},{17,18},{18,... | collective-permute-start | bytes 147464 | tf_op jit(solution)/shard_map/ppermute | solution.py:371
  27.3 1.9 %collective-permute-start.7 = (bf16[176,512]{1,0:T(8,128)(2,1)S(1)}, bf16[176,512]{1,0:T(8,128)(2,1)S(1)}, u32[]{:S(2)}, u32[]{:S(2)}) collective-permute-start(bf16[176,512]{1,0:T(8,128)(2,1)S(1)} %get-tuple-element.48), channel_id=1, source_target_pairs={{0,1},{1,0},{2,3},{3,2},{4,5},{5,4},{6,7},{7,6},{8,9},{9,8},{10,11... | collective-permute-start | bytes 540680 | tf_op jit(solution)/shard_map/ppermute | solution.py:356
  29.2 3.3 %inner.1 = (bf16[2,72,1024]{2,1,0:T(8,128)(2,1)S(1)}, bf16[2,3,72,512]{3,2,1,0:T(8,128)(2,1)S(1)}) custom-call(bf16[304,512]{1,0:T(8,128)(2,1)S(1)} %get-tuple-element.34.pay1, bf16[304,512]{1,0:T(8,128)(2,1)S(1)} %get-tuple-element.35.pay2, bf16[304,512]{1,0:T(8,128)(2,1)S(1)} %collective-permute-done.far1.after, ...), custom_call_target="tpu_custom_call" | custom-call | flops 3000000000 | bytes 4000000 | tf_op jit(solution)/shard_map/inner/pallas_call | solution.py:328
  32.5 0.0 collective-permute-done.2.over1
  32.5 0.1 third.1
  32.6 8.7 %collective-permute-start.5 = (bf16[48,512]{1,0:T(8,128)(2,1)S(1)}, bf16[48,512]{1,0:T(8,128)(2,1)S(1)}, u32[]{:S(2)}, u32[]{:S(2)}) collective-permute-start(bf16[48,512]{1,0:T(8,128)(2,1)S(1)} %get-tuple-element.46), channel_id=1, source_target_pairs={{8,16},{11,19},{12,20},{15,23},{16,8},{19,11},{20,12},{23,15},{24,... | collective-permute-start | bytes 147464 | tf_op jit(solution)/shard_map/ppermute | solution.py:371
  41.3 2.2 %collective-permute-start.6 = (bf16[48,512]{1,0:T(8,128)(2,1)S(1)}, bf16[48,512]{1,0:T(8,128)(2,1)S(1)}, u32[]{:S(2)}, u32[]{:S(2)}) collective-permute-start(bf16[48,512]{1,0:T(8,128)(2,1)S(1)} %get-tuple-element.47), channel_id=1, source_target_pairs={{0,8},{8,0},{16,24},{24,16},{32,40},{40,32},{48,56},{56,48},{64,72... | collective-permute-start | bytes 147464 | tf_op jit(solution)/shard_map/ppermute | solution.py:356
  43.5 0.0 collective-permute-done.7.over2
  43.5 1.6 %near.1 = f32[2,40,512]{2,1,0:T(8,128)S(1)} custom-call(bf16[304,512]{1,0:T(8,128)(2,1)S(1)} %get-tuple-element.34.pay1, bf16[304,512]{1,0:T(8,128)(2,1)S(1)} %get-tuple-element.35.pay2, bf16[304,512]{1,0:T(8,128)(2,1)S(1)} %collective-permute-done.far1.after, bf16[304,512]{1,0:T(8,128)(2,1)S(1)} %collective-permute-done.1.after.far2, ...), custom_call_target="tpu_custom_call" | custom-call | flops 1000000000 | bytes 4000000 | tf_op jit(solution)/shard_map/near/pallas_call | solution.py:328
  45.1 0.0 collective-permute-done.3.bend1
  45.1 0.0 collective-permute-done.4.bend2
  45.1 0.0 collective-permute-done.5.bend3
  45.1 0.0 collective-permute-done.6.bend4
  45.1 2.9 %outer.1 = bf16[576,512]{1,0:T(8,128)(2,1)} custom-call(bf16[304,512]{1,0:T(8,128)(2,1)S(1)} %get-tuple-element.34.pay1, bf16[304,512]{1,0:T(8,128)(2,1)S(1)} %get-tuple-element.35.pay2, bf16[304,512]{1,0:T(8,128)(2,1)S(1)} %collective-permute-done.far1.after, bf16[304,512]{1,0:T(8,128)(2,1)S(1)} %collective-permute-done.1.after.far2, ...), custom_call_target="tpu_custom_call" | custom-call | flops 1500000000 | bytes 4000000 | tf_op jit(solution)/shard_map/outer/pallas_call | solution.py:328
  (3 shorter events, 0.0 us)
Async XLA Ops:
  3.6 10.7 %collective-permute-start.1 = (bf16[304,512]{1,0:T(8,128)(2,1)S(1)}, bf16[304,512]{1,0:T(8,128)(2,1)S(1)}, u32[]{:S(2)}, u32[]{:S(2)}) collective-permute-start(bf16[304,512]{1,0:T(8,128)(2,1)S(1)} %get-tuple-element.35.pay2), channel_id=1, source_target_pairs={{0,8},{8,0},{16,24},{24,16},{32,40},{40,32},{48,56},{56,48},{64,72... | collective-permute-start | bytes 933896 | tf_op jit(solution)/shard_map/ppermute | solution.py:356
  12.4 14.1 %collective-permute-start = (bf16[304,512]{1,0:T(8,128)(2,1)S(1)}, bf16[304,512]{1,0:T(8,128)(2,1)S(1)}, u32[]{:S(2)}, u32[]{:S(2)}) collective-permute-start(bf16[304,512]{1,0:T(8,128)(2,1)S(1)} %get-tuple-element.34.pay1), channel_id=1, source_target_pairs={{8,16},{16,8},{24,32},{32,24},{40,48},{48,40},{56,64},{64,56},{72,... | collective-permute-start | bytes 933896 | tf_op jit(solution)/shard_map/ppermute | solution.py:356
  14.4 18.1 %collective-permute-start.2 = (bf16[80,512]{1,0:T(8,128)(2,1)S(1)}, bf16[80,512]{1,0:T(8,128)(2,1)S(1)}, u32[]{:S(2)}, u32[]{:S(2)}) collective-permute-start(bf16[80,512]{1,0:T(8,128)(2,1)S(1)} %gate.2.after), channel_id=1, source_target_pairs={{1,2},{2,1},{3,4},{4,3},{5,6},{6,5},{7,0},{0,7},{9,10},{10,9},{11,... | collective-permute-start | bytes 245768 | tf_op jit(solution)/shard_map/ppermute | solution.py:356
  25.9 19.2 %collective-permute-start.3 = (bf16[48,512]{1,0:T(8,128)(2,1)S(1)}, bf16[48,512]{1,0:T(8,128)(2,1)S(1)}, u32[]{:S(2)}, u32[]{:S(2)}) collective-permute-start(bf16[48,512]{1,0:T(8,128)(2,1)S(1)} %gate.3), channel_id=1, source_target_pairs={{0,511},{3,508},{4,507},{7,504},{120,135},{123,132},{124,131},{127... | collective-permute-start | bytes 147464 | tf_op jit(solution)/shard_map/ppermute | solution.py:371
  26.6 18.5 %collective-permute-start.4 = (bf16[48,512]{1,0:T(8,128)(2,1)S(1)}, bf16[48,512]{1,0:T(8,128)(2,1)S(1)}, u32[]{:S(2)}, u32[]{:S(2)}) collective-permute-start(bf16[48,512]{1,0:T(8,128)(2,1)S(1)} %get-tuple-element.38), channel_id=1, source_target_pairs={{1,2},{2,1},{5,6},{6,5},{9,10},{10,9},{13,14},{14,13},{17,18},{18,... | collective-permute-start | bytes 147464 | tf_op jit(solution)/shard_map/ppermute | solution.py:371
  27.3 16.2 %collective-permute-start.7 = (bf16[176,512]{1,0:T(8,128)(2,1)S(1)}, bf16[176,512]{1,0:T(8,128)(2,1)S(1)}, u32[]{:S(2)}, u32[]{:S(2)}) collective-permute-start(bf16[176,512]{1,0:T(8,128)(2,1)S(1)} %get-tuple-element.48), channel_id=1, source_target_pairs={{0,1},{1,0},{2,3},{3,2},{4,5},{5,4},{6,7},{7,6},{8,9},{9,8},{10,11... | collective-permute-start | bytes 540680 | tf_op jit(solution)/shard_map/ppermute | solution.py:356
  32.6 12.5 %collective-permute-start.5 = (bf16[48,512]{1,0:T(8,128)(2,1)S(1)}, bf16[48,512]{1,0:T(8,128)(2,1)S(1)}, u32[]{:S(2)}, u32[]{:S(2)}) collective-permute-start(bf16[48,512]{1,0:T(8,128)(2,1)S(1)} %get-tuple-element.46), channel_id=1, source_target_pairs={{8,16},{11,19},{12,20},{15,23},{16,8},{19,11},{20,12},{23,15},{24,... | collective-permute-start | bytes 147464 | tf_op jit(solution)/shard_map/ppermute | solution.py:371
  41.3 3.8 %collective-permute-start.6 = (bf16[48,512]{1,0:T(8,128)(2,1)S(1)}, bf16[48,512]{1,0:T(8,128)(2,1)S(1)}, u32[]{:S(2)}, u32[]{:S(2)}) collective-permute-start(bf16[48,512]{1,0:T(8,128)(2,1)S(1)} %get-tuple-element.47), channel_id=1, source_target_pairs={{0,8},{8,0},{16,24},{24,16},{32,40},{40,32},{48,56},{56,48},{64,72... | collective-permute-start | bytes 147464 | tf_op jit(solution)/shard_map/ppermute | solution.py:356

commit v5 on v4

--- a/solution.py
+++ b/solution.py
@@ -107,7 +107,7 @@
         copy.wait()
 
 
-def own_part(pay1, pay2, gain, bias, w_qkv, b_qkv, qkv, back):
+def own_part(pay1, pay2, gain, bias, w_qkv, b_qkv, qkv, back, back_edge):
     g, b = gain[...].reshape(1, D), bias[...].reshape(1, D)
     for s, pay in enumerate((pay1, pay2)):
         normed = layer_norm(pay[:SIDE, :].astype(F32), g, b)
@@ -120,27 +120,22 @@
             for m in range(BLOCKS):
                 qkv[s, m, :, cols] = part[m * HALF : (m + 1) * HALF].astype(BF16)
     place, _, _ = place_of(iota((SIDE, 1), 0), lax.axis_index("lat") % 2)
-    back[...] = jnp.where(iota((SIDE, SIDE), 1) == place, 1.0, 0.0).astype(BF16)
-
-
-def soon():
-    return (lax.axis_index("lat") < LAT_RUN) & (lax.axis_index("lon") % LON_RUN < 6)
-
-
-def ahead_kernel(pay1, pay2, *refs):
-    qkv, back, _, _ = refs[-4:]
-
-    @pl.when(soon())
+    back[...] = jnp.where(iota((SIDE, 3 * HALF), 1) == place, 1.0, 0.0).astype(BF16)
+    back_edge[...] = jnp.where(iota((SIDE, HALF), 1) + 3 * HALF == place, 1.0, 0.0).astype(BF16)
+
+
+def turn():
+    lat, lon = lax.axis_index("lat"), lax.axis_index("lon")
+    early = (lat < LAT_RUN) & (lon % LON_RUN < 6)
+    return jnp.where(early, jnp.where((lat == 0) & (lon == 0), 1, 0), 2)
+
+
+def own_kernel(when, pay1, pay2, *refs):
+    outs = refs[-4:-1] if when < 2 else refs[-3:]
+
+    @pl.when(turn() == when)
     def _():
-        own_part(pay1, pay2, *refs[:-4], qkv, back)
-
-
-def own_kernel(pay1, pay2, gain, bias, w_qkv, b_qkv, after, qkv_in, back_in, qkv, back):
-    del after, qkv_in, back_in
-
-    @pl.when(jnp.logical_not(soon()))
-    def _():
-        own_part(pay1, pay2, gain, bias, w_qkv, b_qkv, qkv, back)
+        own_part(pay1, pay2, *refs[:4], *outs)
 
 
 def label_line(ref, at):
@@ -198,12 +193,36 @@
     return jnp.concatenate([edge_piece(ref, 0), shifted(label_line(ref, SIDE), 3 * HALF, 0)], axis=0).astype(BF16)
 
 
-def second_kernel(pay1, far1, pay2, far2, out, bend):
+def second_kernel(pay1, far1, pay2, far2, out):
     refs = (pay1, far1, pay2, far2)
     rows = [edge_piece(ref, 1) for ref in refs]
     line = edge_labels([(label_line(ref, SIDE), 3 * HALF + 32) for ref in refs])
     out[...] = jnp.concatenate([*rows, line, line], axis=0).astype(BF16)
-    bend[...] = corner_piece(far1)
+
+
+def bend_kernel(far1, after, out):
+    del after
+    out[...] = corner_piece(far1)
+
+
+def third_kernel(over, crossed, after, out):
+    del after
+    x = over_first(over, crossed)
+    out[...] = jnp.concatenate([x[32 : 32 + EDGE], shifted(x[HALF:], 32, 0)], axis=0).astype(BF16)
+
+
+def is_far(axis, run):
+    at = lax.axis_index(axis) % run
+    return (at == 0) | (at == run - 1)
+
+
+def choose(flag, a, b):
+    return jnp.where(jnp.full(a.shape, jnp.where(flag, 1.0, 0.0)) > 0.5, a, b)
+
+
+def over_first(over, crossed):
+    crosses = is_far("lat", LAT_RUN) & jnp.logical_not(is_far("lon", LON_RUN))
+    return choose(crosses, crossed[...].astype(F32), over[...].astype(F32))
 
 
 def gate_kernel(x, after, out):
@@ -211,14 +230,7 @@
     out[...] = x[...]
 
 
-def third_kernel(over1, after, first, second):
-    del after
-    x, line = over1[...].astype(F32), label_line(over1, HALF)
-    for out, at in ((first, 0), (second, 32)):
-        out[...] = jnp.concatenate([x[at : at + EDGE], shifted(line, at, 0)], axis=0).astype(BF16)
-
-
-def inner_kernel(pay1, pay2, far1, far2, qlab, qkv, gain, bias, w_qkv, b_qkv, w_out, b_out, kv_edge, mixed, kv):
+def inner_kernel(pay1, pay2, far1, far2, qlab, qkv, back, gain, bias, w_qkv, b_qkv, w_out, b_out, kv_edge, placed, kv):
     g, b = gain[...].reshape(1, D), bias[...].reshape(1, D)
     for s, far in enumerate((far1, far2)):
         normed = layer_norm(far[:SIDE, :].astype(F32), g, b)
@@ -227,6 +239,7 @@
             part = mm(normed, w_qkv[:, cols]) + b_qkv[cols].reshape(1, D)
             kv[s, :, c * D : (c + 1) * D] = part
             kv_edge[s, :, c * D : (c + 1) * D] = part[3 * HALF :].astype(BF16)
+    mixed = ([], [])
     for m in range(BLOCKS - 1):
         rows = slice(m * HALF, (m + 1) * HALF)
         heads, xs = [], []
@@ -239,8 +252,11 @@
             heads.append(attention(qkv[s, m, :, :D].astype(F32), both[:, :D], both[:, D:], q_label, k_label))
             xs.append(pay[:SIDE, :].astype(F32)[rows])
         done = finish(jnp.concatenate(heads, axis=0), jnp.concatenate(xs, axis=0), w_out[...], b_out[...].reshape(1, D))
-        mixed[0, m] = done[:HALF]
-        mixed[1, m] = done[HALF:]
+        done = done.astype(F32)
+        mixed[0].append(done[:HALF])
+        mixed[1].append(done[HALF:])
+    for s in range(2):
+        placed[s] = mm(back[...], jnp.concatenate(mixed[s], axis=0).astype(BF16)).astype(BF16)
 
 
 def project_kv(x, g, b, w_qkv, b_qkv):
@@ -274,33 +290,40 @@
     return attention(q, keys[0], keys[1], q_label, k_label)
 
 
-def near_kernel(pay1, pay2, far1, far2, over2, qlab, qkv, kv_edge, gain, bias, w_qkv, b_qkv, out):
-    g, b = gain[...].reshape(1, D), bias[...].reshape(1, D)
-    kv = project_kv(over2[...].astype(F32), g, b, w_qkv, b_qkv)
-    line = label_line(over2, 4 * EDGE)
-    for s, (pay, far) in enumerate(((pay1, far1), (pay2, far2))):
-        part = [k[2 * EDGE * s : 2 * EDGE * (s + 1)] for k in kv]
-        out[s] = edge_window(1, s, pay, far, part, shifted(line, 2 * EDGE * s, 2 * HALF), True, qlab, qkv, kv_edge)
+def near_kernel(when, pay1, pay2, far1, far2, over2, qlab, qkv, kv_edge, gain, bias, w_qkv, b_qkv, *refs):
+    out = refs[-1]
+    crosses = is_far("lat", LAT_RUN) & jnp.logical_not(is_far("lon", LON_RUN))
+
+    @pl.when(jnp.logical_not(crosses) if when else crosses)
+    def _():
+        g, b = gain[...].reshape(1, D), bias[...].reshape(1, D)
+        kv = project_kv(over2[...].astype(F32), g, b, w_qkv, b_qkv)
+        line = label_line(over2, 4 * EDGE)
+        for s, (pay, far) in enumerate(((pay1, far1), (pay2, far2))):
+            part = [k[2 * EDGE * s : 2 * EDGE * (s + 1)] for k in kv]
+            out[s] = edge_window(1, s, pay, far, part, shifted(line, 2 * EDGE * s, 2 * HALF), True, qlab, qkv, kv_edge)
 
 
 def outer_kernel(
-    pay1, pay2, far1, far2, over1, bend1, bend2, bend3, bend4, near, qlab, qkv, kv_edge, mixed, back, gain, bias, w_qkv, b_qkv, w_out, b_out, out
+    pay1, pay2, far1, far2, over, crossed, bend1, bend2, bend4, near, qlab, qkv, kv_edge, placed, back, gain, bias, w_qkv, b_qkv, w_out, b_out, out, done, sem
 ):
     g, b = gain[...].reshape(1, D), bias[...].reshape(1, D)
-    corner = bend1[...].astype(F32) + bend2[...].astype(F32) + bend3[...].astype(F32)
+    over1 = over_first(over, crossed)
+    corner, raw = bend1[...].astype(F32) + bend2[...].astype(F32), over[...].astype(F32)
+    crosses = is_far("lat", LAT_RUN) & jnp.logical_not(is_far("lon", LON_RUN))
+    corner = choose(crosses, jnp.concatenate([raw[:EDGE], raw[HALF:]], axis=0), corner)
     other = bend4[...].astype(F32)
-    kv = project_kv(jnp.concatenate([over1[...].astype(F32), corner, other], axis=0), g, b, w_qkv, b_qkv)
-    line = label_line(over1, HALF)
+    kv = project_kv(jnp.concatenate([over1, corner, other], axis=0), g, b, w_qkv, b_qkv)
+    line = over1[HALF:]
     lane = iota((8, D), 1)
     rest = (qlab, qkv, kv_edge)
-    at = over1.shape[0]
     a = []
     for s, (pay, far, bent) in enumerate(((pay1, far1, corner), (pay2, far2, other))):
+        at = over1.shape[0] + (EDGE + 8) * s
         kv_s = [jnp.concatenate([k[32 * s : 32 * s + EDGE], k[at : at + EDGE]], axis=0) for k in kv]
         mine, theirs = shifted(line, 32 * s, 2 * HALF), shifted(bent[EDGE:], 0, 2 * HALF + EDGE)
         line_s = jnp.where(lane < 2 * HALF + EDGE, mine, theirs)
         a.append(edge_window(0, s, pay, far, kv_s, line_s, s == 1, *rest))
-        at += EDGE + 8
     heads, xs = [], []
     for s, pay in enumerate((pay1, pay2)):
         z = near[s]
@@ -308,12 +331,18 @@
         heads.append(jnp.concatenate([a[s][:32], mid, z[8:]], axis=0))
         xs.append(pay[:SIDE, :].astype(F32)[3 * HALF :])
     edges = finish(jnp.concatenate(heads, axis=0), jnp.concatenate(xs, axis=0), w_out[...], b_out[...].reshape(1, D))
-    edges = edges.astype(F32)
+    copies = []
     for s in range(2):
-        parts = [mixed[s, m].astype(F32) for m in range(BLOCKS - 1)] + [edges[s * HALF : (s + 1) * HALF]]
-        done = mm(back[...], jnp.concatenate(parts, axis=0).astype(BF16)).astype(BF16)
         for l in range(LEV):
-            out[pl.ds(side_rows(s, l), SIDE // 2), :] = done[l * (SIDE // 2) : (l + 1) * (SIDE // 2)]
+            rows = pl.ds(l * (SIDE // 2), SIDE // 2)
+            product = mm(back[rows, :], edges[s * HALF : (s + 1) * HALF])
+            done[s, rows, :] = (product + placed[s, rows, :].astype(F32)).astype(BF16)
+            copies.append(
+                pltpu.make_async_copy(done.at[s, rows], out.at[pl.ds(side_rows(s, l), SIDE // 2)], sem.at[2 * s + l])
+            )
+            copies[-1].start()
+    for copy in copies:
+        copy.wait()
 
 
 VMEM = pl.BlockSpec(memory_space=pltpu.VMEM)
@@ -329,7 +358,7 @@
         kernel,
         out_shape=[make(shape, dtype) for shape, dtype in outs],
         in_specs=[spec] * len(args),
-        out_specs=[VMEM] * len(outs),
+        out_specs=[VMEM if keep else pl.BlockSpec(memory_space=pl.ANY)] * len(outs),
         scratch_shapes=list(scratch),
         input_output_aliases=dict(aliases),
         compiler_params=pltpu.CompilerParams(vmem_limit_bytes=LIMIT),
@@ -356,7 +385,7 @@
     return held(lax.ppermute(block, axis, route))
 
 
-def swap_corners(block, way):
+def swap_far(block, way):
     n_lon, n_lat = lax.axis_size("lon"), lax.axis_size("lat")
     over_lon = {i: j for p in pairs("lon", 1) for i, j in (p, p[::-1])}
     over_lat = {i: j for p in pairs("lat", 1) for i, j in (p, p[::-1])}
@@ -365,9 +394,11 @@
         for a in range(n_lat):
             far_lat = a % LAT_RUN in (0, LAT_RUN - 1)
             far_lon = o % LON_RUN in (0, LON_RUN - 1)
-            if way == ("direct" if far_lat and far_lon else "lon" if far_lat else "lat"):
-                to = (o if way == "lat" else over_lon[o]) * n_lat + (a if way == "lon" else over_lat[a])
-                route.append((o * n_lat + a, to))
+            own = "direct" if far_lat and far_lon else "lon" if far_lat else "lat"
+            if way in (own, "first"):
+                to_o = over_lon[o] if own == "lon" or way == "direct" else o
+                to_a = a if way == "lon" else over_lat[a]
+                route.append((o * n_lat + a, to_o * n_lat + to_a))
     return held(lax.ppermute(block, ("lon", "lat"), route))
 
 
@@ -394,62 +425,61 @@
     )
     weights = [held(w) for w in weights]
     norm, into, outof = weights[:2], weights[2:4], weights[4:]
-    qkv_back = [((2, BLOCKS, HALF, 3 * D), BF16), ((SIDE, SIDE), BF16)]
-    qkv, back, pay1, pay2 = call(
-        ahead_kernel,
-        "ahead",
-        [*qkv_back, ((PAY, D), BF16), ((PAY, D), BF16)],
-        (held(pay1), held(pay2), *norm, *into),
-        900_000_000,
-        aliases={0: 2, 1: 3},
-    )
-    pay1, pay2, qlab = held(pay1), held(pay2), held(qlab)
+    parts = [((2, BLOCKS, HALF, 3 * D), BF16), ((SIDE, 3 * HALF), BF16), ((SIDE, HALF), BF16)]
+
+    def own(when, more, aliases):
+        name = ("at_once", "after", "late")[when]
+        args = (held(pay1), held(pay2), *norm, *into, *more)
+        outs = parts + ([((PAY, D), BF16)] if when < 2 else [])
+        results = call(functools.partial(own_kernel, when), name, outs, args, 900_000_000, aliases=aliases)
+        return [held(x) for x in results[:3]], *results[3:]
+
+    ours, pay2 = own(0, (), {1: 3})
+    pay2 = held(pay2)
     far2 = swap(pay2, "lon", 0)
+    ours, pay1 = own(1, ours, {0: 3, 6: 0, 7: 1, 8: 2})
+    pay1, qlab = held(pay1), held(qlab)
     far1 = swap(pay1, "lon", 1)
     edge1 = gate(edge1, far2)
-    over1 = swap(edge1, "lat", 1)
+    over = swap_far(edge1, "first")
     bend = gate(bend, edge1)
-    bend1 = swap_corners(bend, "direct")
-    args = (pay1, pay2, *norm, *into, far1, held(qkv), held(back))
-    qkv, back = call(own_kernel, "own", qkv_back, args, 900_000_000, aliases={7: 0, 8: 1})
-    qkv, back = held(qkv), held(back)
-    edge2, bend = call(
-        second_kernel,
-        "edge2",
-        [((4 * EDGE + 16, D), BF16), ((EDGE + 8, D), BF16)],
-        (pay1, far1, pay2, far2),
-        1_000_000,
-    )
-    bend2 = swap_corners(bend, "lat")
+    bend1 = swap_far(bend, "direct")
+    ((qkv, back, back_edge),) = own(2, (*ours, far1), {6: 0, 7: 1, 8: 2})
+    (edge2,) = call(second_kernel, "edge2", [((4 * EDGE + 16, D), BF16)], (pay1, far1, pay2, far2), 1_000_000)
     over2 = swap(edge2, "lat", 0)
-    kv_edge, mixed = call(
+    (bend,) = call(bend_kernel, "bend", [((EDGE + 8, D), BF16)], (far1, held(bend)), 1_000_000)
+    bend2 = swap_far(bend, "lat")
+    kv_edge, placed = call(
         inner_kernel,
         "inner",
-        [((2, HALF, 2 * D), BF16), ((2, BLOCKS - 1, HALF, D), BF16)],
-        (pay1, pay2, far1, far2, qlab, qkv, *norm, *into, *outof),
+        [((2, HALF, 2 * D), BF16), ((2, SIDE, D), BF16)],
+        (pay1, pay2, far1, far2, qlab, qkv, back, *norm, *into, *outof),
         3_000_000_000,
         [pltpu.VMEM((2, SIDE, 2 * D), F32)],
     )
-    kv_edge, mixed = held(kv_edge), held(mixed)
-    (near,) = call(
-        near_kernel,
-        "near",
-        [((2, EDGE, D), F32)],
-        (pay1, pay2, far1, far2, over2, qlab, qkv, kv_edge, *norm, *into),
-        1_000_000_000,
-    )
-    bend, other = call(third_kernel, "third", [((EDGE + 8, D), BF16)] * 2, (over1, kv_edge), 1_000_000)
-    bend3 = swap_corners(bend, "lon")
-    bend4 = swap(other, "lon", 0)
+    kv_edge, placed = held(kv_edge), held(placed)
+    raw = gate(over, kv_edge)
+    crossed = swap_far(raw, "lon")
+
+    def near(when, *more):
+        args = (pay1, pay2, far1, far2, over2, qlab, qkv, kv_edge, *norm, *into, *more)
+        kernel, aliases = functools.partial(near_kernel, when), {13: 0} if when else {}
+        return held(call(kernel, "near", [((2, EDGE, D), F32)], args, 1_000_000_000, aliases=aliases)[0])
+
+    windows = near(0, raw)
+    (bend,) = call(third_kernel, "third", [((EDGE + 8, D), BF16)], (raw, crossed, windows), 1_000_000)
+    bend4 = swap(bend, "lon", 0)
+    windows = near(1, held(bend), windows)
     (out,) = call(
         outer_kernel,
         "outer",
         [((2 * SIDE, D), BF16)],
         (
-            *(pay1, pay2, far1, far2, over1, bend1, bend2, bend3, bend4, held(near)),
-            *(qlab, qkv, kv_edge, mixed, back, *norm, *into, *outof),
+            *(pay1, pay2, far1, far2, raw, crossed, bend1, bend2, bend4, windows),
+            *(qlab, qkv, kv_edge, placed, back_edge, *norm, *into, *outof),
         ),
         1_500_000_000,
+        [pltpu.VMEM((2, SIDE, D), BF16), pltpu.SemaphoreType.DMA((4,))],
         keep=False,
     )
     return out.reshape(LEV, COLS, ROWS, D).transpose(0, 2, 1, 3)

time: 48.3 us -> 48.1 us (level)
  starting transfers between devices: 36.2 us -> 33.6 us
  waiting for transfers between devices: 0.02 us -> 1.95 us
    ppermute x5 -> x4, starting transfers between devices: 26.2 us -> 16.2 us  [swap(): return held(lax.ppermute(block, axis, route))]
    ppermute x3 -> x4, starting transfers between devices: 10 us -> 17.4 us  [swap_far(): return held(lax.ppermute(block, ('lon', 'lat'), route))]
    ppermute x3 -> x4, waiting for transfers between devices: 0.01 us -> 1.14 us  [swap_far(): return held(lax.ppermute(block, ('lon', 'lat'), route))]
    ppermute x5 -> x4, waiting for transfers between devices: 0.01 us -> 0.81 us  [swap(): return held(lax.ppermute(block, axis, route))]
    pallas_call x10 -> x14, Pallas kernels: 11.6 us -> 11.8 us  [call(): pl.pallas_call(kernel, out_shape=[make(shape, dtype) for shape, dtype in...]
  transfers between devices with their start and end apart: 8 -> 8, of which waited for: 0 -> 2; matrix products, arithmetic and copies ran while one was open for 0% -> 0% of each run, Pallas kernels for 11% -> 12%
where the time goes in v5:
time: 48.1 us; the launch traced here: 47.6 us
  starting transfers between devices  33.6 us (70%)
  Pallas kernels  11.8 us (25%)
  waiting for transfers between devices  1.95 us (4%)
    ppermute x4, starting transfers between devices, swap_far(): return held(lax.ppermute(block, ('lon', 'lat'), route))  17.4 us
    ppermute x4, starting transfers between devices, swap(): return held(lax.ppermute(block, axis, route))  16.2 us
    pallas_call x14, Pallas kernels, call(): pl.pallas_call(kernel, out_shape=[make(shape, dtype) for shape, dtype in...  11.8 us
    ppermute x4, waiting for transfers between devices, swap_far(): return held(lax.ppermute(block, ('lon', 'lat'), route))  1.14 us
  transfers between devices with their start and end apart: 8, of which 2 were waited for; matrix products, arithmetic and copies ran while one was open for 0% of the time, Pallas kernels for 12%

profile of v5, /device:TPU:1, one launch (start us, length us, event | category | flops | bytes accessed | tf_op | source)
XLA Modules:
  0.0 47.6 jit_solution(8057100986750056185)
XLA Ops:
  0.0 2.2 %prep.1 = (bf16[304,512]{1,0:T(8,128)(2,1)S(1)}, bf16[304,512]{1,0:T(8,128)(2,1)S(1)}, f32[2,288,128]{2,1,0:T(8,128)S(1)}, bf16[80,512]{1,0:T(8,128)(2,1)S(1)}, ...) custom-call(bf16[576,512]{1,0:T(8,128)(2,1)} %bitcast.7, ...), custom_call_target="tpu_custom_call" | custom-call | flops 200000000 | bytes 4000000 | tf_op jit(solution)/shard_map/prep/pallas_call | solution.py:357
  2.2 1.5 %at_once.1 = (bf16[2,4,72,1536]{3,2,1,0:T(8,128)(2,1)S(1)}, bf16[288,216]{1,0:T(8,128)(2,1)S(1)}, bf16[288,72]{1,0:T(8,128)(2,1)S(1)}, bf16[304,512]{1,0:T(8,128)(2,1)S(1)}) custom-call(bf16[304,512]{1,0:T(8,128)(2,1)S(1)} %get-tuple-element.29.pay1, bf16[304,512]{1,0:T(8,128)(2,1)S(1)} %get-tuple-element.30.pay2, ...), custom_call_target="tpu_custom_call", output_to_operand_aliasing={{3}: (1, {})} | custom-call | flops 900000000 | bytes 4000000 | tf_op jit(solution)/shard_map/at_once/pallas_call | solution.py:357
  3.6 7.4 %collective-permute-start.1 = (bf16[304,512]{1,0:T(8,128)(2,1)S(1)}, bf16[304,512]{1,0:T(8,128)(2,1)S(1)}, u32[]{:S(2)}, u32[]{:S(2)}) collective-permute-start(bf16[304,512]{1,0:T(8,128)(2,1)S(1)} %get-tuple-element.35.pay2), channel_id=1, source_target_pairs={{0,8},{8,0},{16,24},{24,16},{32,40},{40,32},{48,56},{56,48},{64,72... | collective-permute-start | bytes 933896 | tf_op jit(solution)/shard_map/ppermute | solution.py:385
  11.0 1.9 %collective-permute-start = (bf16[304,512]{1,0:T(8,128)(2,1)S(1)}, bf16[304,512]{1,0:T(8,128)(2,1)S(1)}, u32[]{:S(2)}, u32[]{:S(2)}) collective-permute-start(bf16[304,512]{1,0:T(8,128)(2,1)S(1)} %get-tuple-element.39.pay1), channel_id=1, source_target_pairs={{8,16},{16,8},{24,32},{32,24},{40,48},{48,40},{56,64},{64,56},{72,... | collective-permute-start | bytes 933896 | tf_op jit(solution)/shard_map/ppermute | solution.py:385
  13.0 0.0 collective-permute-done.1.after.far2
  13.0 12.8 %collective-permute-start.2 = (bf16[80,512]{1,0:T(8,128)(2,1)S(1)}, bf16[80,512]{1,0:T(8,128)(2,1)S(1)}, u32[]{:S(2)}, u32[]{:S(2)}) collective-permute-start(bf16[80,512]{1,0:T(8,128)(2,1)S(1)} %gate.3.after), channel_id=1, source_target_pairs={{0,7},{1,2},{2,1},{3,4},{4,3},{5,6},{6,5},{7,0},{8,23},{9,10},{10,... | collective-permute-start | bytes 245768 | tf_op jit(solution)/shard_map/ppermute | solution.py:402
  25.8 0.7 %collective-permute-start.4 = (bf16[48,512]{1,0:T(8,128)(2,1)S(1)}, bf16[48,512]{1,0:T(8,128)(2,1)S(1)}, u32[]{:S(2)}, u32[]{:S(2)}) collective-permute-start(bf16[48,512]{1,0:T(8,128)(2,1)S(1)} %gate.5.after), channel_id=1, source_target_pairs={{0,511},{3,508},{4,507},{7,504},{120,135},{123,132},{124,131},{127... | collective-permute-start | bytes 147464 | tf_op jit(solution)/shard_map/ppermute | solution.py:402
  26.5 0.0 collective-permute-done.refs_7_.far1
  26.5 0.1 bend.1
  26.6 0.7 %collective-permute-start.5 = (bf16[48,512]{1,0:T(8,128)(2,1)S(1)}, bf16[48,512]{1,0:T(8,128)(2,1)S(1)}, u32[]{:S(2)}, u32[]{:S(2)}) collective-permute-start(bf16[48,512]{1,0:T(8,128)(2,1)S(1)} %bend.1), channel_id=1, source_target_pairs={{1,2},{2,1},{5,6},{6,5},{9,10},{10,9},{13,14},{14,13},{17,18},{18,... | collective-permute-start | bytes 147464 | tf_op jit(solution)/shard_map/ppermute | solution.py:402
  27.2 0.1 edge2.1
  27.3 1.9 %collective-permute-start.6 = (bf16[176,512]{1,0:T(8,128)(2,1)S(1)}, bf16[176,512]{1,0:T(8,128)(2,1)S(1)}, u32[]{:S(2)}, u32[]{:S(2)}) collective-permute-start(bf16[176,512]{1,0:T(8,128)(2,1)S(1)} %edge2.1), channel_id=1, source_target_pairs={{0,1},{1,0},{2,3},{3,2},{4,5},{5,4},{6,7},{7,6},{8,9},{9,8},{10,11... | collective-permute-start | bytes 540680 | tf_op jit(solution)/shard_map/ppermute | solution.py:385
  29.3 3.5 %inner.1 = (bf16[2,72,1024]{2,1,0:T(8,128)(2,1)S(1)}, bf16[2,288,512]{2,1,0:T(8,128)(2,1)S(1)}) custom-call(bf16[304,512]{1,0:T(8,128)(2,1)S(1)} %get-tuple-element.39.pay1, bf16[304,512]{1,0:T(8,128)(2,1)S(1)} %get-tuple-element.35.pay2, bf16[304,512]{1,0:T(8,128)(2,1)S(1)} %collective-permute-done.refs_7_.far1, ...), custom_call_target="tpu_custom_call" | custom-call | flops 3000000000 | bytes 4000000 | tf_op jit(solution)/shard_map/inner/pallas_call | solution.py:357
  32.8 0.0 collective-permute-done.2.x
  32.8 3.3 %collective-permute-start.3 = (bf16[80,512]{1,0:T(8,128)(2,1)S(1)}, bf16[80,512]{1,0:T(8,128)(2,1)S(1)}, u32[]{:S(2)}, u32[]{:S(2)}) collective-permute-start(bf16[80,512]{1,0:T(8,128)(2,1)S(1)} %gate.4.refs_0_.over), channel_id=1, source_target_pairs={{8,16},{11,19},{12,20},{15,23},{16,8},{19,11},{20,12},{23,15},{24,... | collective-permute-start | bytes 245768 | tf_op jit(solution)/shard_map/ppermute | solution.py:402
  36.2 0.0 collective-permute-done.6.over2
  36.2 1.6 %near.2.after.refs_1_ = f32[2,40,512]{2,1,0:T(8,128)S(1)} custom-call(bf16[304,512]{1,0:T(8,128)(2,1)S(1)} %get-tuple-element.39.pay1, bf16[304,512]{1,0:T(8,128)(2,1)S(1)} %get-tuple-element.35.pay2, bf16[304,512]{1,0:T(8,128)(2,1)S(1)} %collective-permute-done.refs_7_.far1, bf16[304,512]{1,0:T(8,128)(2,1)S(1)} %collective-permute-done.1.after.far2, ...), custom_call_target="tpu_custom_call" | custom-call | flops 1000000000 | bytes 4000000 | tf_op jit(solution)/shard_map/near/pallas_call | solution.py:357
  37.8 1.1 %collective-permute-done.3.crossed = bf16[80,512]{1,0:T(8,128)(2,1)S(1)} collective-permute-done((bf16[80,512]{1,0:T(8,128)(2,1)S(1)}, bf16[80,512]{1,0:T(8,128)(2,1)S(1)}, u32[]{:S(2)}, u32[]{:S(2)}) %collective-permute-start.3) | collective-permute-done | bytes 81952 | tf_op jit(solution)/shard_map/ppermute | solution.py:402
  38.9 0.1 third.1.refs_0_
  39.0 5.0 %collective-permute-start.7 = (bf16[48,512]{1,0:T(8,128)(2,1)S(1)}, bf16[48,512]{1,0:T(8,128)(2,1)S(1)}, u32[]{:S(2)}, u32[]{:S(2)}) collective-permute-start(bf16[48,512]{1,0:T(8,128)(2,1)S(1)} %third.1.refs_0_), channel_id=1, source_target_pairs={{0,8},{8,0},{16,24},{24,16},{32,40},{40,32},{48,56},{56,48},{64,72... | collective-permute-start | bytes 147464 | tf_op jit(solution)/shard_map/ppermute | solution.py:385
  44.0 0.0 collective-permute-done.5.bend2
  44.0 0.0 collective-permute-done.4.bend1
  44.0 0.8 %collective-permute-done.7.bend4 = bf16[48,512]{1,0:T(8,128)(2,1)S(1)} collective-permute-done((bf16[48,512]{1,0:T(8,128)(2,1)S(1)}, bf16[48,512]{1,0:T(8,128)(2,1)S(1)}, u32[]{:S(2)}, u32[]{:S(2)}) %collective-permute-start.7) | collective-permute-done | bytes 49184 | tf_op jit(solution)/shard_map/ppermute | solution.py:385
  44.8 2.7 %outer.1 = bf16[576,512]{1,0:T(8,128)(2,1)} custom-call(bf16[304,512]{1,0:T(8,128)(2,1)S(1)} %get-tuple-element.39.pay1, bf16[304,512]{1,0:T(8,128)(2,1)S(1)} %get-tuple-element.35.pay2, bf16[304,512]{1,0:T(8,128)(2,1)S(1)} %collective-permute-done.refs_7_.far1, bf16[304,512]{1,0:T(8,128)(2,1)S(1)} %collective-permute-done.1.after.far2, ...), custom_call_target="tpu_custom_call" | custom-call | flops 1500000000 | bytes 4000000 | tf_op jit(solution)/shard_map/outer/pallas_call | solution.py:357
  (6 shorter events, 0.1 us)
Async XLA Ops:
  3.6 9.3 %collective-permute-start.1 = (bf16[304,512]{1,0:T(8,128)(2,1)S(1)}, bf16[304,512]{1,0:T(8,128)(2,1)S(1)}, u32[]{:S(2)}, u32[]{:S(2)}) collective-permute-start(bf16[304,512]{1,0:T(8,128)(2,1)S(1)} %get-tuple-element.35.pay2), channel_id=1, source_target_pairs={{0,8},{8,0},{16,24},{24,16},{32,40},{40,32},{48,56},{56,48},{64,72... | collective-permute-start | bytes 933896 | tf_op jit(solution)/shard_map/ppermute | solution.py:385
  11.0 15.4 %collective-permute-start = (bf16[304,512]{1,0:T(8,128)(2,1)S(1)}, bf16[304,512]{1,0:T(8,128)(2,1)S(1)}, u32[]{:S(2)}, u32[]{:S(2)}) collective-permute-start(bf16[304,512]{1,0:T(8,128)(2,1)S(1)} %get-tuple-element.39.pay1), channel_id=1, source_target_pairs={{8,16},{16,8},{24,32},{32,24},{40,48},{48,40},{56,64},{64,56},{72,... | collective-permute-start | bytes 933896 | tf_op jit(solution)/shard_map/ppermute | solution.py:385
  13.0 19.8 %collective-permute-start.2 = (bf16[80,512]{1,0:T(8,128)(2,1)S(1)}, bf16[80,512]{1,0:T(8,128)(2,1)S(1)}, u32[]{:S(2)}, u32[]{:S(2)}) collective-permute-start(bf16[80,512]{1,0:T(8,128)(2,1)S(1)} %gate.3.after), channel_id=1, source_target_pairs={{0,7},{1,2},{2,1},{3,4},{4,3},{5,6},{6,5},{7,0},{8,23},{9,10},{10,... | collective-permute-start | bytes 245768 | tf_op jit(solution)/shard_map/ppermute | solution.py:402
  25.8 18.2 %collective-permute-start.4 = (bf16[48,512]{1,0:T(8,128)(2,1)S(1)}, bf16[48,512]{1,0:T(8,128)(2,1)S(1)}, u32[]{:S(2)}, u32[]{:S(2)}) collective-permute-start(bf16[48,512]{1,0:T(8,128)(2,1)S(1)} %gate.5.after), channel_id=1, source_target_pairs={{0,511},{3,508},{4,507},{7,504},{120,135},{123,132},{124,131},{127... | collective-permute-start | bytes 147464 | tf_op jit(solution)/shard_map/ppermute | solution.py:402
  26.6 17.4 %collective-permute-start.5 = (bf16[48,512]{1,0:T(8,128)(2,1)S(1)}, bf16[48,512]{1,0:T(8,128)(2,1)S(1)}, u32[]{:S(2)}, u32[]{:S(2)}) collective-permute-start(bf16[48,512]{1,0:T(8,128)(2,1)S(1)} %bend.1), channel_id=1, source_target_pairs={{1,2},{2,1},{5,6},{6,5},{9,10},{10,9},{13,14},{14,13},{17,18},{18,... | collective-permute-start | bytes 147464 | tf_op jit(solution)/shard_map/ppermute | solution.py:402
  27.3 8.8 %collective-permute-start.6 = (bf16[176,512]{1,0:T(8,128)(2,1)S(1)}, bf16[176,512]{1,0:T(8,128)(2,1)S(1)}, u32[]{:S(2)}, u32[]{:S(2)}) collective-permute-start(bf16[176,512]{1,0:T(8,128)(2,1)S(1)} %edge2.1), channel_id=1, source_target_pairs={{0,1},{1,0},{2,3},{3,2},{4,5},{5,4},{6,7},{7,6},{8,9},{9,8},{10,11... | collective-permute-start | bytes 540680 | tf_op jit(solution)/shard_map/ppermute | solution.py:385
  32.8 6.1 %collective-permute-start.3 = (bf16[80,512]{1,0:T(8,128)(2,1)S(1)}, bf16[80,512]{1,0:T(8,128)(2,1)S(1)}, u32[]{:S(2)}, u32[]{:S(2)}) collective-permute-start(bf16[80,512]{1,0:T(8,128)(2,1)S(1)} %gate.4.refs_0_.over), channel_id=1, source_target_pairs={{8,16},{11,19},{12,20},{15,23},{16,8},{19,11},{20,12},{23,15},{24,... | collective-permute-start | bytes 245768 | tf_op jit(solution)/shard_map/ppermute | solution.py:402
  39.0 5.9 %collective-permute-start.7 = (bf16[48,512]{1,0:T(8,128)(2,1)S(1)}, bf16[48,512]{1,0:T(8,128)(2,1)S(1)}, u32[]{:S(2)}, u32[]{:S(2)}) collective-permute-start(bf16[48,512]{1,0:T(8,128)(2,1)S(1)} %third.1.refs_0_), channel_id=1, source_target_pairs={{0,8},{8,0},{16,24},{24,16},{32,40},{40,32},{48,56},{56,48},{64,72... | collective-permute-start | bytes 147464 | tf_op jit(solution)/shard_map/ppermute | solution.py:385

commit v6 on v4

--- a/solution.py
+++ b/solution.py
@@ -107,7 +107,7 @@
         copy.wait()
 
 
-def own_part(pay1, pay2, gain, bias, w_qkv, b_qkv, qkv, back):
+def own_part(pay1, pay2, gain, bias, w_qkv, b_qkv, qkv, back, back_edge):
     g, b = gain[...].reshape(1, D), bias[...].reshape(1, D)
     for s, pay in enumerate((pay1, pay2)):
         normed = layer_norm(pay[:SIDE, :].astype(F32), g, b)
@@ -120,27 +120,22 @@
             for m in range(BLOCKS):
                 qkv[s, m, :, cols] = part[m * HALF : (m + 1) * HALF].astype(BF16)
     place, _, _ = place_of(iota((SIDE, 1), 0), lax.axis_index("lat") % 2)
-    back[...] = jnp.where(iota((SIDE, SIDE), 1) == place, 1.0, 0.0).astype(BF16)
-
-
-def soon():
-    return (lax.axis_index("lat") < LAT_RUN) & (lax.axis_index("lon") % LON_RUN < 6)
-
-
-def ahead_kernel(pay1, pay2, *refs):
-    qkv, back, _, _ = refs[-4:]
-
-    @pl.when(soon())
+    back[...] = jnp.where(iota((SIDE, 3 * HALF), 1) == place, 1.0, 0.0).astype(BF16)
+    back_edge[...] = jnp.where(iota((SIDE, HALF), 1) + 3 * HALF == place, 1.0, 0.0).astype(BF16)
+
+
+def turn():
+    lat, lon = lax.axis_index("lat"), lax.axis_index("lon")
+    early = (lat < LAT_RUN) & (lon % LON_RUN < 6)
+    return jnp.where(early, jnp.where((lat == 0) & (lon == 0), 1, 0), 2)
+
+
+def own_kernel(when, pay1, pay2, *refs):
+    outs = refs[-4:-1] if when < 2 else refs[-3:]
+
+    @pl.when(turn() == when)
     def _():
-        own_part(pay1, pay2, *refs[:-4], qkv, back)
-
-
-def own_kernel(pay1, pay2, gain, bias, w_qkv, b_qkv, after, qkv_in, back_in, qkv, back):
-    del after, qkv_in, back_in
-
-    @pl.when(jnp.logical_not(soon()))
-    def _():
-        own_part(pay1, pay2, gain, bias, w_qkv, b_qkv, qkv, back)
+        own_part(pay1, pay2, *refs[:4], *outs)
 
 
 def label_line(ref, at):
@@ -218,7 +213,7 @@
         out[...] = jnp.concatenate([x[at : at + EDGE], shifted(line, at, 0)], axis=0).astype(BF16)
 
 
-def inner_kernel(pay1, pay2, far1, far2, qlab, qkv, gain, bias, w_qkv, b_qkv, w_out, b_out, kv_edge, mixed, kv):
+def inner_kernel(pay1, pay2, far1, far2, qlab, qkv, back, gain, bias, w_qkv, b_qkv, w_out, b_out, kv_edge, placed, kv):
     g, b = gain[...].reshape(1, D), bias[...].reshape(1, D)
     for s, far in enumerate((far1, far2)):
         normed = layer_norm(far[:SIDE, :].astype(F32), g, b)
@@ -227,6 +222,7 @@
             part = mm(normed, w_qkv[:, cols]) + b_qkv[cols].reshape(1, D)
             kv[s, :, c * D : (c + 1) * D] = part
             kv_edge[s, :, c * D : (c + 1) * D] = part[3 * HALF :].astype(BF16)
+    mixed = ([], [])
     for m in range(BLOCKS - 1):
         rows = slice(m * HALF, (m + 1) * HALF)
         heads, xs = [], []
@@ -239,8 +235,11 @@
             heads.append(attention(qkv[s, m, :, :D].astype(F32), both[:, :D], both[:, D:], q_label, k_label))
             xs.append(pay[:SIDE, :].astype(F32)[rows])
         done = finish(jnp.concatenate(heads, axis=0), jnp.concatenate(xs, axis=0), w_out[...], b_out[...].reshape(1, D))
-        mixed[0, m] = done[:HALF]
-        mixed[1, m] = done[HALF:]
+        done = done.astype(F32)
+        mixed[0].append(done[:HALF])
+        mixed[1].append(done[HALF:])
+    for s in range(2):
+        placed[s] = mm(back[...], jnp.concatenate(mixed[s], axis=0).astype(BF16)).astype(BF16)
 
 
 def project_kv(x, g, b, w_qkv, b_qkv):
@@ -284,7 +283,7 @@
 
 
 def outer_kernel(
-    pay1, pay2, far1, far2, over1, bend1, bend2, bend3, bend4, near, qlab, qkv, kv_edge, mixed, back, gain, bias, w_qkv, b_qkv, w_out, b_out, out
+    pay1, pay2, far1, far2, over1, bend1, bend2, bend3, bend4, near, qlab, qkv, kv_edge, placed, back, gain, bias, w_qkv, b_qkv, w_out, b_out, out, done, sem
 ):
     g, b = gain[...].reshape(1, D), bias[...].reshape(1, D)
     corner = bend1[...].astype(F32) + bend2[...].astype(F32) + bend3[...].astype(F32)
@@ -293,14 +292,13 @@
     line = label_line(over1, HALF)
     lane = iota((8, D), 1)
     rest = (qlab, qkv, kv_edge)
-    at = over1.shape[0]
     a = []
     for s, (pay, far, bent) in enumerate(((pay1, far1, corner), (pay2, far2, other))):
+        at = over1.shape[0] + (EDGE + 8) * s
         kv_s = [jnp.concatenate([k[32 * s : 32 * s + EDGE], k[at : at + EDGE]], axis=0) for k in kv]
         mine, theirs = shifted(line, 32 * s, 2 * HALF), shifted(bent[EDGE:], 0, 2 * HALF + EDGE)
         line_s = jnp.where(lane < 2 * HALF + EDGE, mine, theirs)
         a.append(edge_window(0, s, pay, far, kv_s, line_s, s == 1, *rest))
-        at += EDGE + 8
     heads, xs = [], []
     for s, pay in enumerate((pay1, pay2)):
         z = near[s]
@@ -308,12 +306,18 @@
         heads.append(jnp.concatenate([a[s][:32], mid, z[8:]], axis=0))
         xs.append(pay[:SIDE, :].astype(F32)[3 * HALF :])
     edges = finish(jnp.concatenate(heads, axis=0), jnp.concatenate(xs, axis=0), w_out[...], b_out[...].reshape(1, D))
-    edges = edges.astype(F32)
+    copies = []
     for s in range(2):
-        parts = [mixed[s, m].astype(F32) for m in range(BLOCKS - 1)] + [edges[s * HALF : (s + 1) * HALF]]
-        done = mm(back[...], jnp.concatenate(parts, axis=0).astype(BF16)).astype(BF16)
         for l in range(LEV):
-            out[pl.ds(side_rows(s, l), SIDE // 2), :] = done[l * (SIDE // 2) : (l + 1) * (SIDE // 2)]
+            rows = pl.ds(l * (SIDE // 2), SIDE // 2)
+            product = mm(back[rows, :], edges[s * HALF : (s + 1) * HALF])
+            done[s, rows, :] = (product + placed[s, rows, :].astype(F32)).astype(BF16)
+            copies.append(
+                pltpu.make_async_copy(done.at[s, rows], out.at[pl.ds(side_rows(s, l), SIDE // 2)], sem.at[2 * s + l])
+            )
+            copies[-1].start()
+    for copy in copies:
+        copy.wait()
 
 
 VMEM = pl.BlockSpec(memory_space=pltpu.VMEM)
@@ -329,7 +333,7 @@
         kernel,
         out_shape=[make(shape, dtype) for shape, dtype in outs],
         in_specs=[spec] * len(args),
-        out_specs=[VMEM] * len(outs),
+        out_specs=[VMEM if keep else pl.BlockSpec(memory_space=pl.ANY)] * len(outs),
         scratch_shapes=list(scratch),
         input_output_aliases=dict(aliases),
         compiler_params=pltpu.CompilerParams(vmem_limit_bytes=LIMIT),
@@ -394,25 +398,26 @@
     )
     weights = [held(w) for w in weights]
     norm, into, outof = weights[:2], weights[2:4], weights[4:]
-    qkv_back = [((2, BLOCKS, HALF, 3 * D), BF16), ((SIDE, SIDE), BF16)]
-    qkv, back, pay1, pay2 = call(
-        ahead_kernel,
-        "ahead",
-        [*qkv_back, ((PAY, D), BF16), ((PAY, D), BF16)],
-        (held(pay1), held(pay2), *norm, *into),
-        900_000_000,
-        aliases={0: 2, 1: 3},
-    )
-    pay1, pay2, qlab = held(pay1), held(pay2), held(qlab)
+    parts = [((2, BLOCKS, HALF, 3 * D), BF16), ((SIDE, 3 * HALF), BF16), ((SIDE, HALF), BF16)]
+
+    def own(when, more, aliases):
+        name = ("at_once", "after", "late")[when]
+        args = (held(pay1), held(pay2), *norm, *into, *more)
+        outs = parts + ([((PAY, D), BF16)] if when < 2 else [])
+        results = call(functools.partial(own_kernel, when), name, outs, args, 900_000_000, aliases=aliases)
+        return [held(x) for x in results[:3]], *results[3:]
+
+    ours, pay2 = own(0, (), {1: 3})
+    pay2 = held(pay2)
     far2 = swap(pay2, "lon", 0)
+    ours, pay1 = own(1, ours, {0: 3, 6: 0, 7: 1, 8: 2})
+    pay1, qlab = held(pay1), held(qlab)
     far1 = swap(pay1, "lon", 1)
     edge1 = gate(edge1, far2)
     over1 = swap(edge1, "lat", 1)
     bend = gate(bend, edge1)
     bend1 = swap_corners(bend, "direct")
-    args = (pay1, pay2, *norm, *into, far1, held(qkv), held(back))
-    qkv, back = call(own_kernel, "own", qkv_back, args, 900_000_000, aliases={7: 0, 8: 1})
-    qkv, back = held(qkv), held(back)
+    ((qkv, back, back_edge),) = own(2, (*ours, far1), {6: 0, 7: 1, 8: 2})
     edge2, bend = call(
         second_kernel,
         "edge2",
@@ -422,15 +427,15 @@
     )
     bend2 = swap_corners(bend, "lat")
     over2 = swap(edge2, "lat", 0)
-    kv_edge, mixed = call(
+    kv_edge, placed = call(
         inner_kernel,
         "inner",
-        [((2, HALF, 2 * D), BF16), ((2, BLOCKS - 1, HALF, D), BF16)],
-        (pay1, pay2, far1, far2, qlab, qkv, *norm, *into, *outof),
+        [((2, HALF, 2 * D), BF16), ((2, SIDE, D), BF16)],
+        (pay1, pay2, far1, far2, qlab, qkv, back, *norm, *into, *outof),
         3_000_000_000,
         [pltpu.VMEM((2, SIDE, 2 * D), F32)],
     )
-    kv_edge, mixed = held(kv_edge), held(mixed)
+    kv_edge, placed = held(kv_edge), held(placed)
     (near,) = call(
         near_kernel,
         "near",
@@ -438,6 +443,7 @@
         (pay1, pay2, far1, far2, over2, qlab, qkv, kv_edge, *norm, *into),
         1_000_000_000,
     )
+    near = held(near)
     bend, other = call(third_kernel, "third", [((EDGE + 8, D), BF16)] * 2, (over1, kv_edge), 1_000_000)
     bend3 = swap_corners(bend, "lon")
     bend4 = swap(other, "lon", 0)
@@ -446,10 +452,11 @@
         "outer",
         [((2 * SIDE, D), BF16)],
         (
-            *(pay1, pay2, far1, far2, over1, bend1, bend2, bend3, bend4, held(near)),
-            *(qlab, qkv, kv_edge, mixed, back, *norm, *into, *outof),
+            *(pay1, pay2, far1, far2, over1, bend1, bend2, bend3, bend4, near),
+            *(qlab, qkv, kv_edge, placed, back_edge, *norm, *into, *outof),
         ),
         1_500_000_000,
+        [pltpu.VMEM((2, SIDE, D), BF16), pltpu.SemaphoreType.DMA((4,))],
         keep=False,
     )
     return out.reshape(LEV, COLS, ROWS, D).transpose(0, 2, 1, 3)

time: 48.3 us -> 48.2 us (level)
    pallas_call x10 -> x11, Pallas kernels: 11.6 us -> 11.7 us  [call(): pl.pallas_call(kernel, out_shape=[make(shape, dtype) for shape, dtype in...]
where the time goes in v6:
time: 48.2 us; the launch traced here: 47.9 us
  starting transfers between devices  36 us (75%)
  Pallas kernels  11.7 us (24%)
    ppermute x5, starting transfers between devices, swap(): return held(lax.ppermute(block, axis, route))  26.3 us
    pallas_call x11, Pallas kernels, call(): pl.pallas_call(kernel, out_shape=[make(shape, dtype) for shape, dtype in...  11.7 us
    ppermute x3, starting transfers between devices, swap_corners(): return held(lax.ppermute(block, ('lon', 'lat'), route))  9.68 us
  transfers between devices with their start and end apart: 8, of which 0 were waited for; matrix products, arithmetic and copies ran while one was open for 0% of the time, Pallas kernels for 11%

profile of v6, /device:TPU:1, one launch (start us, length us, event | category | flops | bytes accessed | tf_op | source)
XLA Modules:
  0.0 47.9 jit_solution(17572883828768168453)
XLA Ops:
  0.0 2.2 %prep.1 = (bf16[304,512]{1,0:T(8,128)(2,1)S(1)}, bf16[304,512]{1,0:T(8,128)(2,1)S(1)}, f32[2,288,128]{2,1,0:T(8,128)S(1)}, bf16[80,512]{1,0:T(8,128)(2,1)S(1)}, ...) custom-call(bf16[576,512]{1,0:T(8,128)(2,1)} %bitcast.7, ...), custom_call_target="tpu_custom_call" | custom-call | flops 200000000 | bytes 4000000 | tf_op jit(solution)/shard_map/prep/pallas_call | solution.py:332
  2.2 1.5 %at_once.1 = (bf16[2,4,72,1536]{3,2,1,0:T(8,128)(2,1)S(1)}, bf16[288,216]{1,0:T(8,128)(2,1)S(1)}, bf16[288,72]{1,0:T(8,128)(2,1)S(1)}, bf16[304,512]{1,0:T(8,128)(2,1)S(1)}) custom-call(bf16[304,512]{1,0:T(8,128)(2,1)S(1)} %get-tuple-element.33.pay1, bf16[304,512]{1,0:T(8,128)(2,1)S(1)} %get-tuple-element.34.pay2, ...), custom_call_target="tpu_custom_call", output_to_operand_aliasing={{3}: (1, {})} | custom-call | flops 900000000 | bytes 4000000 | tf_op jit(solution)/shard_map/at_once/pallas_call | solution.py:332
  3.6 7.4 %collective-permute-start.1 = (bf16[304,512]{1,0:T(8,128)(2,1)S(1)}, bf16[304,512]{1,0:T(8,128)(2,1)S(1)}, u32[]{:S(2)}, u32[]{:S(2)}) collective-permute-start(bf16[304,512]{1,0:T(8,128)(2,1)S(1)} %get-tuple-element.39.pay2), channel_id=1, source_target_pairs={{0,8},{8,0},{16,24},{24,16},{32,40},{40,32},{48,56},{56,48},{64,72... | collective-permute-start | bytes 933896 | tf_op jit(solution)/shard_map/ppermute | solution.py:360
  11.0 1.9 %collective-permute-start = (bf16[304,512]{1,0:T(8,128)(2,1)S(1)}, bf16[304,512]{1,0:T(8,128)(2,1)S(1)}, u32[]{:S(2)}, u32[]{:S(2)}) collective-permute-start(bf16[304,512]{1,0:T(8,128)(2,1)S(1)} %get-tuple-element.43.pay1), channel_id=1, source_target_pairs={{8,16},{16,8},{24,32},{32,24},{40,48},{48,40},{56,64},{64,56},{72,... | collective-permute-start | bytes 933896 | tf_op jit(solution)/shard_map/ppermute | solution.py:360
  13.0 0.0 collective-permute-done.1.after.far2
  13.0 12.9 %collective-permute-start.2 = (bf16[80,512]{1,0:T(8,128)(2,1)S(1)}, bf16[80,512]{1,0:T(8,128)(2,1)S(1)}, u32[]{:S(2)}, u32[]{:S(2)}) collective-permute-start(bf16[80,512]{1,0:T(8,128)(2,1)S(1)} %gate.2.after), channel_id=1, source_target_pairs={{1,2},{2,1},{3,4},{4,3},{5,6},{6,5},{7,0},{0,7},{9,10},{10,9},{11,... | collective-permute-start | bytes 245768 | tf_op jit(solution)/shard_map/ppermute | solution.py:360
  25.9 0.7 %collective-permute-start.3 = (bf16[48,512]{1,0:T(8,128)(2,1)S(1)}, bf16[48,512]{1,0:T(8,128)(2,1)S(1)}, u32[]{:S(2)}, u32[]{:S(2)}) collective-permute-start(bf16[48,512]{1,0:T(8,128)(2,1)S(1)} %gate.3), channel_id=1, source_target_pairs={{0,511},{3,508},{4,507},{7,504},{120,135},{123,132},{124,131},{127... | collective-permute-start | bytes 147464 | tf_op jit(solution)/shard_map/ppermute | solution.py:375
  26.6 0.0 collective-permute-done.far1.refs_7_
  26.6 0.1 edge2.1
  26.7 0.7 %collective-permute-start.4 = (bf16[48,512]{1,0:T(8,128)(2,1)S(1)}, bf16[48,512]{1,0:T(8,128)(2,1)S(1)}, u32[]{:S(2)}, u32[]{:S(2)}) collective-permute-start(bf16[48,512]{1,0:T(8,128)(2,1)S(1)} %get-tuple-element.46), channel_id=1, source_target_pairs={{1,2},{2,1},{5,6},{6,5},{9,10},{10,9},{13,14},{14,13},{17,18},{18,... | collective-permute-start | bytes 147464 | tf_op jit(solution)/shard_map/ppermute | solution.py:375
  27.3 1.9 %collective-permute-start.7 = (bf16[176,512]{1,0:T(8,128)(2,1)S(1)}, bf16[176,512]{1,0:T(8,128)(2,1)S(1)}, u32[]{:S(2)}, u32[]{:S(2)}) collective-permute-start(bf16[176,512]{1,0:T(8,128)(2,1)S(1)} %get-tuple-element.58), channel_id=1, source_target_pairs={{0,1},{1,0},{2,3},{3,2},{4,5},{5,4},{6,7},{7,6},{8,9},{9,8},{10,11... | collective-permute-start | bytes 540680 | tf_op jit(solution)/shard_map/ppermute | solution.py:360
  29.3 3.6 %inner.1 = (bf16[2,72,1024]{2,1,0:T(8,128)(2,1)S(1)}, bf16[2,288,512]{2,1,0:T(8,128)(2,1)S(1)}) custom-call(bf16[304,512]{1,0:T(8,128)(2,1)S(1)} %get-tuple-element.43.pay1, bf16[304,512]{1,0:T(8,128)(2,1)S(1)} %get-tuple-element.39.pay2, bf16[304,512]{1,0:T(8,128)(2,1)S(1)} %collective-permute-done.far1.refs_7_, ...), custom_call_target="tpu_custom_call" | custom-call | flops 3000000000 | bytes 4000000 | tf_op jit(solution)/shard_map/inner/pallas_call | solution.py:332
  32.8 0.0 collective-permute-done.2.over1
  32.9 0.1 third.1
  32.9 8.4 %collective-permute-start.5 = (bf16[48,512]{1,0:T(8,128)(2,1)S(1)}, bf16[48,512]{1,0:T(8,128)(2,1)S(1)}, u32[]{:S(2)}, u32[]{:S(2)}) collective-permute-start(bf16[48,512]{1,0:T(8,128)(2,1)S(1)} %get-tuple-element.56), channel_id=1, source_target_pairs={{8,16},{11,19},{12,20},{15,23},{16,8},{19,11},{20,12},{23,15},{24,... | collective-permute-start | bytes 147464 | tf_op jit(solution)/shard_map/ppermute | solution.py:375
  41.3 2.2 %collective-permute-start.6 = (bf16[48,512]{1,0:T(8,128)(2,1)S(1)}, bf16[48,512]{1,0:T(8,128)(2,1)S(1)}, u32[]{:S(2)}, u32[]{:S(2)}) collective-permute-start(bf16[48,512]{1,0:T(8,128)(2,1)S(1)} %get-tuple-element.57), channel_id=1, source_target_pairs={{0,8},{8,0},{16,24},{24,16},{32,40},{40,32},{48,56},{56,48},{64,72... | collective-permute-start | bytes 147464 | tf_op jit(solution)/shard_map/ppermute | solution.py:360
  43.5 0.0 collective-permute-done.7.over2
  43.5 1.6 %near.1 = f32[2,40,512]{2,1,0:T(8,128)S(1)} custom-call(bf16[304,512]{1,0:T(8,128)(2,1)S(1)} %get-tuple-element.43.pay1, bf16[304,512]{1,0:T(8,128)(2,1)S(1)} %get-tuple-element.39.pay2, bf16[304,512]{1,0:T(8,128)(2,1)S(1)} %collective-permute-done.far1.refs_7_, bf16[304,512]{1,0:T(8,128)(2,1)S(1)} %collective-permute-done.1.after.far2, ...), custom_call_target="tpu_custom_call" | custom-call | flops 1000000000 | bytes 4000000 | tf_op jit(solution)/shard_map/near/pallas_call | solution.py:332
  45.1 0.0 collective-permute-done.3.bend1
  45.1 0.0 collective-permute-done.4.bend2
  45.2 0.0 collective-permute-done.5.bend3
  45.2 0.0 collective-permute-done.6.bend4
  45.2 2.7 %outer.1 = bf16[576,512]{1,0:T(8,128)(2,1)} custom-call(bf16[304,512]{1,0:T(8,128)(2,1)S(1)} %get-tuple-element.43.pay1, bf16[304,512]{1,0:T(8,128)(2,1)S(1)} %get-tuple-element.39.pay2, bf16[304,512]{1,0:T(8,128)(2,1)S(1)} %collective-permute-done.far1.refs_7_, bf16[304,512]{1,0:T(8,128)(2,1)S(1)} %collective-permute-done.1.after.far2, ...), custom_call_target="tpu_custom_call" | custom-call | flops 1500000000 | bytes 4000000 | tf_op jit(solution)/shard_map/outer/pallas_call | solution.py:332
  (4 shorter events, 0.1 us)
Async XLA Ops:
  3.6 9.3 %collective-permute-start.1 = (bf16[304,512]{1,0:T(8,128)(2,1)S(1)}, bf16[304,512]{1,0:T(8,128)(2,1)S(1)}, u32[]{:S(2)}, u32[]{:S(2)}) collective-permute-start(bf16[304,512]{1,0:T(8,128)(2,1)S(1)} %get-tuple-element.39.pay2), channel_id=1, source_target_pairs={{0,8},{8,0},{16,24},{24,16},{32,40},{40,32},{48,56},{56,48},{64,72... | collective-permute-start | bytes 933896 | tf_op jit(solution)/shard_map/ppermute | solution.py:360
  11.0 15.5 %collective-permute-start = (bf16[304,512]{1,0:T(8,128)(2,1)S(1)}, bf16[304,512]{1,0:T(8,128)(2,1)S(1)}, u32[]{:S(2)}, u32[]{:S(2)}) collective-permute-start(bf16[304,512]{1,0:T(8,128)(2,1)S(1)} %get-tuple-element.43.pay1), channel_id=1, source_target_pairs={{8,16},{16,8},{24,32},{32,24},{40,48},{48,40},{56,64},{64,56},{72,... | collective-permute-start | bytes 933896 | tf_op jit(solution)/shard_map/ppermute | solution.py:360
  13.0 19.9 %collective-permute-start.2 = (bf16[80,512]{1,0:T(8,128)(2,1)S(1)}, bf16[80,512]{1,0:T(8,128)(2,1)S(1)}, u32[]{:S(2)}, u32[]{:S(2)}) collective-permute-start(bf16[80,512]{1,0:T(8,128)(2,1)S(1)} %gate.2.after), channel_id=1, source_target_pairs={{1,2},{2,1},{3,4},{4,3},{5,6},{6,5},{7,0},{0,7},{9,10},{10,9},{11,... | collective-permute-start | bytes 245768 | tf_op jit(solution)/shard_map/ppermute | solution.py:360
  25.9 19.2 %collective-permute-start.3 = (bf16[48,512]{1,0:T(8,128)(2,1)S(1)}, bf16[48,512]{1,0:T(8,128)(2,1)S(1)}, u32[]{:S(2)}, u32[]{:S(2)}) collective-permute-start(bf16[48,512]{1,0:T(8,128)(2,1)S(1)} %gate.3), channel_id=1, source_target_pairs={{0,511},{3,508},{4,507},{7,504},{120,135},{123,132},{124,131},{127... | collective-permute-start | bytes 147464 | tf_op jit(solution)/shard_map/ppermute | solution.py:375
  26.7 18.5 %collective-permute-start.4 = (bf16[48,512]{1,0:T(8,128)(2,1)S(1)}, bf16[48,512]{1,0:T(8,128)(2,1)S(1)}, u32[]{:S(2)}, u32[]{:S(2)}) collective-permute-start(bf16[48,512]{1,0:T(8,128)(2,1)S(1)} %get-tuple-element.46), channel_id=1, source_target_pairs={{1,2},{2,1},{5,6},{6,5},{9,10},{10,9},{13,14},{14,13},{17,18},{18,... | collective-permute-start | bytes 147464 | tf_op jit(solution)/shard_map/ppermute | solution.py:375
  27.3 16.2 %collective-permute-start.7 = (bf16[176,512]{1,0:T(8,128)(2,1)S(1)}, bf16[176,512]{1,0:T(8,128)(2,1)S(1)}, u32[]{:S(2)}, u32[]{:S(2)}) collective-permute-start(bf16[176,512]{1,0:T(8,128)(2,1)S(1)} %get-tuple-element.58), channel_id=1, source_target_pairs={{0,1},{1,0},{2,3},{3,2},{4,5},{5,4},{6,7},{7,6},{8,9},{9,8},{10,11... | collective-permute-start | bytes 540680 | tf_op jit(solution)/shard_map/ppermute | solution.py:360
  32.9 12.2 %collective-permute-start.5 = (bf16[48,512]{1,0:T(8,128)(2,1)S(1)}, bf16[48,512]{1,0:T(8,128)(2,1)S(1)}, u32[]{:S(2)}, u32[]{:S(2)}) collective-permute-start(bf16[48,512]{1,0:T(8,128)(2,1)S(1)} %get-tuple-element.56), channel_id=1, source_target_pairs={{8,16},{11,19},{12,20},{15,23},{16,8},{19,11},{20,12},{23,15},{24,... | collective-permute-start | bytes 147464 | tf_op jit(solution)/shard_map/ppermute | solution.py:375
  41.3 3.9 %collective-permute-start.6 = (bf16[48,512]{1,0:T(8,128)(2,1)S(1)}, bf16[48,512]{1,0:T(8,128)(2,1)S(1)}, u32[]{:S(2)}, u32[]{:S(2)}) collective-permute-start(bf16[48,512]{1,0:T(8,128)(2,1)S(1)} %get-tuple-element.57), channel_id=1, source_target_pairs={{0,8},{8,0},{16,24},{24,16},{32,40},{40,32},{48,56},{56,48},{64,72... | collective-permute-start | bytes 147464 | tf_op jit(solution)/shard_map/ppermute | solution.py:360
